TPU v7x, 256 devices: a whole 4x4x8 slice. The times are simulated.
256 devices in a mesh: sub: 32 (over x, z), load: 8 (over y, core).
Axes of the slice: x: 4, y: 4, z: 8, core: 2. Of those that a mesh axis runs over, the one named last changes fastest.
Arguments:
- dual_ops: bfloat16 [256, 1024, 1024], P(('sub', 'load')), may hold values from -0.1875 to 0.1875
- dual_rhs: float32 [256, 1024, 128], P(('sub', 'load')), may hold values from -6 to 6
- partner: int32 [256, 1024], P(('sub', 'load')), may hold values from 0 to 3071, as said below
- coarse_basis: bfloat16 [256, 12, 1024], P(('sub', 'load')), may hold values from -0.1875 to 0.1875
- coarse_inverse: float32 [3072, 3072], P(('sub', 'load')), as said below
- damping: float32 [128], replicated, may hold values from 0.05 to 0.5
- recovery: bfloat16 [256, 1536, 1024], P(('sub', 'load')), may hold values from -0.1875 to 0.1875
- base_disp: bfloat16 [256, 1536, 128], P(('sub', 'load')), may hold values from -6 to 6
- adjoint: bfloat16 [256, 1536, 128], P(('sub', 'load')), may hold values from -6 to 6
- elem_voxel: int32 [256, 128], P(('sub', 'load')), may hold values from 0 to 32767
- fibre_class: int32 [256, 1024], P('sub', 'load'), may hold values from 0 to 3
Outputs:
- multipliers: float32 [256, 1024, 128], P(('sub', 'load'))
- gradient_field: float32 [256, 1024], P('sub', 'load')
Inputs may be any that keep to these rules, and one draw needn't show every extreme that they name: `partner`: entry (s, j) names the other copy of the same multiplier among the subdomains s - 1 (values 0 to 1023), s (1024 to 2047) and s + 1 (2048 to 3071), wrapping around over all 256 subdomains, as v mod 1024 = the copy's row. The pairing is one to one and symmetric; in every subdomain a quarter of the entries point to s - 1, a quarter to s + 1 and half inside. `elem_voxel`: value v places the element at grid row v // 128 and at column v mod 128 of the 128 columns of its subdomain's block of columns. coarse_inverse equals its transpose.
All inputs are finite; a program needn't handle non-finite values.
Results may differ from a plain program's by a relative error of at most 0.0021.
Values may be sent and summed in bfloat16 or wider, within the bound.
No kernel may reach another device: no remote copies, remote signals or barrier semaphores. Data moves between devices by JAX's collectives and lax.ppermute only.
A program may use at most 64 MiB of HBM per device.

v0:
```python
import math

import jax
import jax.numpy as jnp
from jax import lax
from jax.sharding import PartitionSpec as P

EDOF = 12
ITERS = 3
SMOOTH = 2


FIBRE_RATE = 0.3
ISO_RATE = 0.05
EPSILON = 1e-06


def extended(value, sides, width, wrap):
    for axis, dim in sides:
        size, length = (lax.axis_size(axis), value.shape[dim])
        up = [(i, (i + 1) % size) for i in range(size if wrap else size - 1)]
        down = [(j, i) for i, j in up]
        last = lax.slice_in_dim(value, length - width, length, axis=dim)
        first = lax.slice_in_dim(value, 0, width, axis=dim)
        before = lax.ppermute(last, axis, up)
        after = lax.ppermute(first, axis, down)
        value = jnp.concatenate([before, value, after], axis=dim)
    return value


def fibre_step(smoothed, classes):
    padded = extended(smoothed, (("sub", 0), ("load", 1)), 1, False)
    along_rows = padded[2:, 1:-1] + padded[:-2, 1:-1] - 2.0 * smoothed
    along_cols = padded[1:-1, 2:] + padded[1:-1, :-2] - 2.0 * smoothed
    diag_main = padded[2:, 2:] + padded[:-2, :-2] - 2.0 * smoothed
    diag_anti = padded[2:, :-2] + padded[:-2, 2:] - 2.0 * smoothed
    chosen = jnp.where(
        classes == 0,
        along_rows,
        jnp.where(classes == 1, along_cols, jnp.where(classes == 2, diag_main, diag_anti)),
    )
    return smoothed + FIBRE_RATE * chosen + ISO_RATE * (along_rows + along_cols)


def on_device(
    dual_ops,
    dual_rhs,
    partner,
    coarse_basis,
    coarse_inverse,
    damping,
    recovery,
    base_disp,
    adjoint,
    elem_voxel,
    fibre_class,
):
    operator = dual_ops[0]
    right_side = dual_rhs[0]
    partner_rows = partner[0]
    mode_basis = coarse_basis[0].astype(jnp.float32)
    spots, columns = right_side.shape
    entries = lax.axis_size("sub") * lax.axis_size("load") * spots
    dual_iterate = jnp.zeros_like(right_side)
    for iteration in range(ITERS):
        rounded = dual_iterate.astype(jnp.bfloat16)
        images = jnp.dot(operator, rounded, preferred_element_type=jnp.float32).astype(jnp.bfloat16)
        window = extended(images[None], ((("sub", "load"), 0),), 1, True).reshape(
            3 * spots, columns
        )
        partners = jnp.take(window, partner_rows, axis=0)
        residual = right_side - (images.astype(jnp.float32) + partners.astype(jnp.float32))
        coarse_terms = jnp.dot(mode_basis, residual, precision=lax.Precision.HIGHEST)
        squares = jnp.sum(residual * residual, axis=0, keepdims=True)
        gathered = lax.all_gather(coarse_terms, ("sub", "load"), axis=0, tiled=True)
        total_squares = lax.psum(squares, ("sub", "load"))
        correction = jnp.dot(coarse_inverse, gathered, precision=lax.Precision.HIGHEST)
        step_size = damping.reshape(1, columns) / jnp.sqrt(total_squares / entries + EPSILON)
        projected = residual - jnp.dot(mode_basis.T, correction, precision=lax.Precision.HIGHEST)
        dual_iterate = dual_iterate + step_size * projected
    final_rounded = dual_iterate.astype(jnp.bfloat16)
    displaced = base_disp[0].astype(jnp.float32) - jnp.dot(
        recovery[0], final_rounded, preferred_element_type=jnp.float32
    )
    products = (displaced * adjoint[0].astype(jnp.float32)).reshape(-1, EDOF, columns)
    element_grad = jnp.sum(products, axis=(1, 2)) / math.sqrt(EDOF * columns)
    grid_rows = fibre_class.shape[0] * lax.axis_size("sub")
    grid_cols = fibre_class.shape[1]
    spread = jax.ops.segment_sum(
        element_grad, elem_voxel[0], num_segments=grid_rows * grid_cols
    ).reshape(grid_rows, grid_cols)
    smoothed = lax.psum_scatter(spread, "sub", scatter_dimension=0, tiled=True)
    for repeat in range(SMOOTH):
        smoothed = fibre_step(smoothed, fibre_class)
    return (dual_iterate[None], smoothed)


def solution(mesh):
    placed = (
        P(("sub", "load"), None, None),
        P(("sub", "load"), None, None),
        P(("sub", "load"), None),
        P(("sub", "load"), None, None),
        P(("sub", "load"), None),
        P(),
        P(("sub", "load"), None, None),
        P(("sub", "load"), None, None),
        P(("sub", "load"), None, None),
        P(("sub", "load"), None),
        P("sub", "load"),
    )
    return jax.shard_map(
        on_device,
        mesh=mesh,
        in_specs=placed,
        out_specs=(P(("sub", "load"), None, None), P("sub", "load")),
        check_vma=False,
    )
```

profile of v0, /device:TPU:1, one launch (start us, length us, event | category | flops | bytes accessed | tf_op | source)
XLA Modules:
  0.0 596.2 jit_solution(7070193673359352173)
XLA Ops:
  7.2 2.6 fusion.28
  9.8 2.8 collective-permute-start
  15.9 2.6 collective-permute-done.1
  22.8 5.3 gather_fusion
  33.0 84.3 %psum.21 = f32[1,128]{1,0:T(1,128)S(1)} all-reduce(f32[1,128]{1,0:T(1,128)S(1)} %bitcast.163), channel_id=1, replica_groups=mesh['sub'=32,'load'=8] {'sub','load'}, use_global_device_ids=true, to_apply=%region_1.3 | all-reduce | flops 128 | bytes 1024 | tf_op jit(solution)/shard_map/psum | solution.py:76
  117.3 24.5 %all-gather.7.cloned.1.call-done = f32[256,12,128]{2,1,0:T(8,128)} async-done(((f32[1,12,128]{2,1,0:T(8,128)}), f32[256,12,128]{2,1,0:T(8,128)}) %all-gather.7.cloned.1.call-update) | async-done | bytes 1572880 | tf_op jit(solution)/shard_map/all_gather | solution.py:75
  141.8 2.5 reshape.76
  144.3 2.5 fusion.78
  150.6 3.3 collective-permute-done.2
  159.7 5.3 gather_fusion.1
  169.9 81.8 %psum.22 = f32[1,128]{1,0:T(1,128)S(1)} all-reduce(f32[1,128]{1,0:T(1,128)S(1)} %bitcast.164), channel_id=1, replica_groups=mesh['sub'=32,'load'=8] {'sub','load'}, use_global_device_ids=true, to_apply=%region_3.5 | all-reduce | flops 128 | bytes 1024 | tf_op jit(solution)/shard_map/psum | solution.py:76
  251.7 24.3 %all-gather.9.cloned.1.call-done = f32[256,12,128]{2,1,0:T(8,128)} async-done(((f32[1,12,128]{2,1,0:T(8,128)}), f32[256,12,128]{2,1,0:T(8,128)}) %all-gather.9.cloned.1.call-update) | async-done | bytes 1572880 | tf_op jit(solution)/shard_map/all_gather | solution.py:75
  275.9 2.5 reshape.78
  284.9 3.3 collective-permute-done.4
  294.0 5.3 gather_fusion.2
  308.1 81.7 %psum.23 = f32[1,128]{1,0:T(1,128)S(1)} all-reduce(f32[1,128]{1,0:T(1,128)S(1)} %bitcast.162), channel_id=1, replica_groups=mesh['sub'=32,'load'=8] {'sub','load'}, use_global_device_ids=true, to_apply=%region_5.7 | all-reduce | flops 128 | bytes 1024 | tf_op jit(solution)/shard_map/psum | solution.py:76
  389.8 20.5 %all-gather.11.cloned.1.call-done = f32[256,12,128]{2,1,0:T(8,128)} async-done(((f32[1,12,128]{2,1,0:T(8,128)}), f32[256,12,128]{2,1,0:T(8,128)}) %all-gather.11.cloned.1.call-update) | async-done | bytes 1572880 | tf_op jit(solution)/shard_map/all_gather | solution.py:75
  410.3 2.5 reshape.80
  421.3 134.5 %all-reduce.3.cloned.1.call-done = f32[256,128]{1,0:T(8,128)} async-done(((f32[256,128]{1,0:T(8,128)}), f32[256,128]{1,0:T(8,128)}) %all-reduce.3.cloned.1.call-update) | async-done | bytes 131088
  557.8 4.0 collective-permute-start.7
  562.5 7.4 %collective-permute-start.8 = (f32[10,1]{1,0:T(8,128)S(1)}, f32[10,1]{1,0:T(8,128)S(1)}, u32[]{:S(2)}, u32[]{:S(2)}) collective-permute-start(f32[10,1]{1,0:T(8,128)S(1)} %get-tuple-element.22), channel_id=1, source_target_pairs={{1,0},{2,1},{3,2},{4,3},{5,4},{6,5},{7,6},{9,8},{10,9},{11,10},{12... | collective-permute-start | bytes 128 | tf_op jit(solution)/shard_map/ppermute | solution.py:26
  570.0 3.0 collective-permute-start.9
  575.2 4.5 collective-permute-start.11
  583.8 4.5 collective-permute-start.13
  (115 shorter events, 66.1 us)
Async XLA Ops:
  7.2 409.4 %copy-start = (bf16[1,1536,1024]{2,1,0:T(8,128)(2,1)S(1)}, bf16[1,1536,1024]{2,1,0:T(8,128)(2,1)}, u32[]{:S(2)}) copy-start(bf16[1,1536,1024]{2,1,0:T(8,128)(2,1)} %param.19) | copy-start | bytes 9437188
  7.2 134.6 %all-gather.7.cloned.1.call-start = ((), (), s32[]{:S(2)}) async-start(), calls=%async_computation | async-start | bytes 2105344 | tf_op jit(solution)/shard_map/all_gather | solution.py:75
  9.8 6.1 %collective-permute-start = (bf16[1,1024,128]{1,2,0:T(8,128)(2,1)S(1)}, bf16[1,1024,128]{1,2,0:T(8,128)(2,1)}, u32[]{:S(2)}, u32[]{:S(2)}) collective-permute-start(bf16[1,1024,128]{1,2,0:T(8,128)(2,1)S(1)} %bitcast.150), channel_id=1, source_target_pairs={{0,1},{1,2},{2,3},{3,4},{4,5},{5,6},{6,7},{7,8},{8,9},{9,10},{10,1... | collective-permute-start | bytes 786440 | tf_op jit(solution)/shard_map/ppermute | solution.py:25
  12.6 5.9 collective-permute-start.1
  22.8 94.5 %copy-start.19 = (f32[128]{0:T(128)S(1)}, f32[128]{0:T(128)}, u32[]{:S(2)}) copy-start(f32[128]{0:T(128)} %param.18) | copy-start | bytes 1540
  32.0 112.3 %copy-start.11 = (f32[12,3072]{1,0:T(8,128)S(1)}, f32[12,3072]{1,0:T(8,128)}, u32[]{:S(2)}) copy-start(f32[12,3072]{1,0:T(8,128)} %param.17) | copy-start | bytes 442372
  33.0 243.0 %all-gather.9.cloned.1.call-start = ((), (), s32[]{:S(2)}) async-start(), calls=%async_computation.1 | async-start | bytes 2105344 | tf_op jit(solution)/shard_map/all_gather | solution.py:75
  149.2 4.7 collective-permute-start.2
  150.6 5.8 collective-permute-start.3
  168.9 109.6 %copy-start.12 = (f32[12,3072]{1,0:T(8,128)S(1)}, f32[12,3072]{1,0:T(8,128)}, u32[]{:S(2)}) copy-start(f32[12,3072]{1,0:T(8,128)} %param.17) | copy-start | bytes 442372
  169.8 240.4 %all-gather.11.cloned.1.call-start = ((), (), s32[]{:S(2)}) async-start(), calls=%async_computation.2 | async-start | bytes 2105344 | tf_op jit(solution)/shard_map/all_gather | solution.py:75
  283.5 4.7 collective-permute-start.4
  284.9 5.8 collective-permute-start.5
  304.2 251.6 %all-reduce.3.cloned.1.call-start = ((), (), s32[]{:S(2)}) async-start(), calls=%async_computation.3 | async-start | bytes 262144
  306.1 106.7 %copy-start.13 = (f32[12,3072]{1,0:T(8,128)S(1)}, f32[12,3072]{1,0:T(8,128)}, u32[]{:S(2)}) copy-start(f32[12,3072]{1,0:T(8,128)} %param.17) | copy-start | bytes 442372
  416.6 157.2 %copy-start.18 = (s32[8,128]{1,0:T(8,128)S(1)}, s32[8,128]{1,0:T(8,128)}, u32[]{:S(2)}) copy-start(s32[8,128]{1,0:T(8,128)} %param.23) | copy-start | bytes 12292
  556.5 5.3 collective-permute-start.6
  557.8 4.7 collective-permute-start.7
  562.5 10.5 %collective-permute-start.8 = (f32[10,1]{1,0:T(8,128)S(1)}, f32[10,1]{1,0:T(8,128)S(1)}, u32[]{:S(2)}, u32[]{:S(2)}) collective-permute-start(f32[10,1]{1,0:T(8,128)S(1)} %get-tuple-element.22), channel_id=1, source_target_pairs={{1,0},{2,1},{3,2},{4,3},{5,4},{6,5},{7,6},{9,8},{10,9},{11,10},{12... | collective-permute-start | bytes 128 | tf_op jit(solution)/shard_map/ppermute | solution.py:26
  570.0 3.8 collective-permute-start.9
  573.9 7.8 %collective-permute-start.10 = (f32[1,128]{1,0:T(1,128)S(1)}, f32[1,128]{1,0:T(1,128)S(1)}, u32[]{:S(2)}, u32[]{:S(2)}) collective-permute-start(f32[1,128]{1,0:T(1,128)S(1)} %get-tuple-element.24), channel_id=1, source_target_pairs={{8,0},{16,8},{24,16},{32,24},{40,32},{48,40},{56,48},{64,56},{72,6... | collective-permute-start | bytes 1544 | tf_op jit(solution)/shard_map/ppermute | solution.py:26
  575.2 6.5 %collective-permute-start.11 = (f32[1,128]{1,0:T(1,128)S(1)}, f32[1,128]{1,0:T(1,128)S(1)}, u32[]{:S(2)}, u32[]{:S(2)}) collective-permute-start(f32[1,128]{1,0:T(1,128)S(1)} %get-tuple-element.23), channel_id=1, source_target_pairs={{0,8},{8,16},{16,24},{24,32},{32,40},{40,48},{48,56},{56,64},{64,7... | collective-permute-start | bytes 1544 | tf_op jit(solution)/shard_map/ppermute | solution.py:25
  581.8 6.4 %collective-permute-start.12 = (f32[10,1]{1,0:T(8,128)S(1)}, f32[10,1]{1,0:T(8,128)S(1)}, u32[]{:S(2)}, u32[]{:S(2)}) collective-permute-start(f32[10,1]{1,0:T(8,128)S(1)} %get-tuple-element.20), channel_id=1, source_target_pairs={{1,0},{2,1},{3,2},{4,3},{5,4},{6,5},{7,6},{9,8},{10,9},{11,10},{12... | collective-permute-start | bytes 128 | tf_op jit(solution)/shard_map/ppermute | solution.py:26
  583.8 5.3 collective-permute-start.13
  (15 other events, 44.4 us)
Sparse Core Ops, SparseCore 0:
  33.1 108.6 all-gather.6
  170.0 105.9 all-gather.8
  304.3 105.9 all-gather.10
  420.2 135.5 all-reduce.2
where the time goes:
time: 602 us; the launch traced here: 596 us
  blocking collectives  248 us (41%)
  waiting for transfers between devices  221 us (37%)
  local copies, waits for them, and re-layouts  48.3 us (8%)
  starting transfers between devices  34.3 us (6%)
  matrix products  19.3 us (3%)
  between operations  14.8 us (2%)
  other arithmetic  10.9 us (2%)
    psum x3, blocking collectives, on_device(): total_squares = lax.psum(squares, ('sub', 'load'))  248 us
    unnamed x5, waiting for transfers between devices  135 us
    all_gather x3, waiting for transfers between devices, on_device(): gathered = lax.all_gather(coarse_terms, ('sub', 'load'), axis=0, tiled=True)  69.3 us
    ppermute x7, starting transfers between devices, extended(): before = lax.ppermute(last, axis, up)  21.5 us
    gather x6, local copies, waits for them, and re-layouts, on_device(): partners = jnp.take(window, partner_rows, axis=0)  21.2 us
    unnamed x51, local copies, waits for them, and re-layouts  20 us
    ppermute x7, starting transfers between devices, extended(): after = lax.ppermute(first, axis, down)  12.6 us
  transfers between devices with their start and end apart: 18, of which 13 were waited for; matrix products, arithmetic and copies ran while one was open for 1% of the time, Pallas kernels for 0%

commit v1 on v0

v1 whole, which is shorter than its diff:
```python
import functools
import math

import jax
import jax.numpy as jnp
from jax import lax
from jax.experimental import pallas as pl
from jax.experimental.pallas import tpu as pltpu
from jax.sharding import PartitionSpec as P

EDOF = 12
MODES = 12
SUB = 32
LOAD = 8
SPOTS = 1024
COLS = 128
UNKNOWNS = 1536
EDGE = 256
MARK = 120
ENTRIES = SUB * LOAD * SPOTS
GRID_ROWS = 256
FIBRE_RATE = 0.3
ISO_RATE = 0.05
EPSILON = 1e-06

F32 = jnp.float32
BF16 = jnp.bfloat16


def call(kernel, outs, operands, name, flops=0, moved=0, limit=24, scratch=()):
    return pl.pallas_call(
        kernel,
        out_shape=[jax.ShapeDtypeStruct(shape, dtype) for shape, dtype in outs],
        scratch_shapes=list(scratch),
        compiler_params=pltpu.CompilerParams(vmem_limit_bytes=limit * 2**20),
        cost_estimate=pl.CostEstimate(flops=flops, bytes_accessed=moved, transcendentals=0),
        name=name,
    )(*operands)


def split2(value):
    high = value.astype(BF16)
    return high, (value - high.astype(F32)).astype(BF16)


def split3(value):
    high = value.astype(BF16)
    rest = value - high.astype(F32)
    middle = rest.astype(BF16)
    return high, middle, (rest - middle.astype(F32)).astype(BF16)


def dot(left, right):
    return jnp.dot(left, right, preferred_element_type=F32)


def lanes_of(shape):
    return lax.broadcasted_iota(jnp.int32, shape, 1)


def rows_of(shape):
    return lax.broadcasted_iota(jnp.int32, shape, 0)


def padded_basis(basis_ref, rows):
    basis = basis_ref[0].astype(F32)
    return jnp.concatenate([basis, jnp.zeros((rows - MODES, SPOTS), F32)], axis=0)


def coarse_rows(basis_ref, residual):
    basis = padded_basis(basis_ref, 16).astype(BF16)
    parts = dot(basis, jnp.concatenate(split3(residual), axis=1))
    terms = parts[:, :COLS] + parts[:, COLS : 2 * COLS] + parts[:, 2 * COLS :]
    squares = jnp.sum(residual * residual, axis=0, keepdims=True)
    return jnp.where(rows_of(terms.shape) == MODES, squares, terms)


def first_terms(rhs_ref, basis_ref, inverse_ref, out_ref):
    rows = coarse_rows(basis_ref, rhs_ref[0])
    inverse = jnp.concatenate([inverse_ref[...], jnp.zeros((4, SUB * LOAD * MODES), F32)], axis=0)
    inverse = jnp.concatenate([inverse, inverse[:, :128]], axis=1)
    lanes = lanes_of((16, COLS))
    mark = jnp.where((rows_of((16, COLS)) == MODES) & (lanes == MARK), 1.0, 0.0)
    for peer in range(SUB):
        start = peer * LOAD * MODES
        tile, offset = start // 128, start % 128
        piece = inverse[:, 128 * tile : 128 * tile + 256]
        if offset:
            piece = pltpu.roll(piece, 256 - offset, axis=1)
        out_ref[peer, :16, :] = rows
        out_ref[peer, 16:, :] = jnp.where(lanes < LOAD * MODES, piece[:, :128], mark)


def partial_rows(high, low, terms, out_ref):
    terms_high, terms_low = split2(terms)
    partial = dot(high, terms_high) + dot(high, terms_low) + dot(low, terms_high)
    last = jnp.concatenate([partial[MARK : MARK + 1], jnp.zeros((3, COLS), F32)], axis=0)
    for peer in range(LOAD):
        out_ref[peer] = jnp.concatenate([partial[MODES * peer : MODES * peer + MODES], last], axis=0)


def first_partial(received_ref, out_ref, block_ref):
    terms = received_ref[:, :16, :].reshape(SUB * 16, COLS)
    block = received_ref[:, 16:, :].reshape(SUB * 16, COLS).T
    high, low = split2(block)
    block_ref[:, : SUB * 16] = high
    block_ref[:, SUB * 16 :] = low
    partial_rows(high, low, terms, out_ref)


def later_partial(received_ref, block_ref, out_ref):
    terms = received_ref[...].reshape(SUB * 16, COLS)
    partial_rows(block_ref[:, : SUB * 16], block_ref[:, SUB * 16 :], terms, out_ref)


def setup(partner_ref, basis_ref, send_ref, pick_ref, lifted_ref):
    basis = padded_basis(basis_ref, COLS).T
    basis = basis + pltpu.roll(basis, 16, axis=1) + pltpu.roll(basis, 32, axis=1)
    lifted_ref[...] = basis.astype(BF16)
    partners = partner_ref[...].astype(F32)
    to_before = jnp.where(partners < SPOTS, 1.0, 0.0)
    to_after = jnp.where(partners >= 2 * SPOTS, 1.0, 0.0)
    sides = jnp.concatenate([to_before, to_after, jnp.zeros((14, SPOTS), F32)], axis=0)
    earlier = jnp.where(rows_of((SPOTS, SPOTS)) < lanes_of((SPOTS, SPOTS)), 1.0, 0.0).astype(BF16)
    place = dot(sides.astype(BF16), earlier)
    place = jnp.where(sides > 0.0, place, -1.0)
    slots = rows_of((EDGE, SPOTS)).astype(F32)
    send_ref[:EDGE, :] = jnp.where(slots == place[0:1], 1.0, 0.0).astype(BF16)
    send_ref[EDGE:, :] = jnp.where(slots == place[1:2], 1.0, 0.0).astype(BF16)
    lanes = lanes_of((128, 128)).astype(F32)
    for block in range(SPOTS // 128):
        here = slice(128 * block, 128 * block + 128)
        wanted = jnp.broadcast_to(partners[:, here], (128, 128)).T
        smaller = jnp.zeros((128, 128), F32)
        for tile in range(SPOTS // 128):
            smaller = smaller + jnp.where(partners[:, 128 * tile : 128 * tile + 128] < wanted, 1.0, 0.0)
        rank = jnp.broadcast_to(jnp.sum(smaller, axis=1, keepdims=True), (128, 128))
        for tile in range((2 * EDGE + SPOTS) // 128):
            start = 128 * tile
            if start < EDGE:
                hit = rank == lanes + start
            elif start < EDGE + SPOTS:
                hit = wanted == lanes + (start - EDGE + SPOTS)
            else:
                hit = rank == lanes + (start - EDGE - SPOTS + 3 * EDGE)
            pick_ref[here, start : start + 128] = jnp.where(hit, 1.0, 0.0).astype(BF16)


def step_parts(received_ref, damping_ref, lifted_ref):
    total = received_ref[0]
    for peer in range(1, LOAD):
        total = total + received_ref[peer]
    step = damping_ref[...] / jnp.sqrt(total[MODES : MODES + 1] / ENTRIES + EPSILON)
    correction = jnp.where(rows_of(total.shape) < MODES, total, 0.0)
    stacked = jnp.concatenate(split3(correction) + (jnp.zeros((COLS - 48, COLS), BF16),), axis=0)
    return step, dot(lifted_ref[...], stacked)


def advance(first, received_ref, damping_ref, lifted_ref, operator_ref, send_ref, residual_ref, *rest):
    step, lifted = step_parts(received_ref, damping_ref, lifted_ref)
    if first:
        iterate_ref, images_ref, down_ref, up_ref = rest
        iterate = step * (residual_ref[0] - lifted)
    else:
        before_ref, iterate_ref, images_ref, down_ref, up_ref = rest
        iterate = before_ref[...] + step * (residual_ref[...] - lifted)
    iterate_ref[...] = iterate
    images = dot(operator_ref[0], iterate.astype(BF16)).astype(BF16)
    images_ref[...] = images
    edges = dot(send_ref[...], images).astype(BF16)
    down_ref[...] = edges[:EDGE]
    up_ref[...] = edges[EDGE:]


def inner_pairs(images_ref, pick_ref, out_ref):
    out_ref[...] = dot(pick_ref[:, EDGE : EDGE + SPOTS], images_ref[...])


def residual_terms(rhs_ref, images_ref, inner_ref, pick_ref, before_ref, after_ref, basis_ref, residual_ref, out_ref):
    partners = inner_ref[...] + dot(pick_ref[:, :EDGE], before_ref[...])
    partners = partners + dot(pick_ref[:, EDGE + SPOTS :], after_ref[...])
    residual = rhs_ref[0] - (images_ref[...].astype(F32) + partners)
    residual_ref[...] = residual
    rows = coarse_rows(basis_ref, residual)
    for peer in range(SUB):
        out_ref[peer] = rows


def gradients(
    received_ref,
    damping_ref,
    lifted_ref,
    residual_ref,
    iterate_ref,
    recovery_ref,
    base_ref,
    adjoint_ref,
    voxel_ref,
    multipliers_ref,
    out_ref,
):
    step, lifted = step_parts(received_ref, damping_ref, lifted_ref)
    multipliers = iterate_ref[...] + step * (residual_ref[...] - lifted)
    multipliers_ref[0] = multipliers
    displaced = base_ref[0].astype(F32) - dot(recovery_ref[0], multipliers.astype(BF16))
    products = displaced * adjoint_ref[0].astype(F32)
    first = EDOF * rows_of((128, UNKNOWNS))
    lanes = lanes_of((128, UNKNOWNS))
    groups = jnp.where((lanes >= first) & (lanes < first + EDOF), 1.0, 0.0).astype(BF16)
    sums = dot(groups, jnp.concatenate(split2(products), axis=1))
    element = jnp.sum(sums, axis=1, keepdims=True) / math.sqrt(EDOF * COLS)
    voxel = voxel_ref[...]
    column = jnp.broadcast_to(voxel & 127, (128, 128)).astype(F32).T.astype(jnp.int32)
    placed = jnp.where(column == lanes_of((128, 128)), element, 0.0)
    rows = GRID_ROWS + 16
    at_row = jnp.where(rows_of((rows, 128)) - 2 == (voxel >> 7), 1.0, 0.0).astype(BF16)
    parts = dot(at_row, jnp.concatenate(split3(placed), axis=1))
    spread = parts[:, :COLS] + parts[:, COLS : 2 * COLS] + parts[:, 2 * COLS :]
    for peer in range(SUB):
        out_ref[peer] = spread[8 * peer : 8 * peer + 16]


def smooth(middle_ref, left_ref, right_ref, classes_ref, out_ref):
    beside = jnp.where(lanes_of((16, 128)) < 64, right_ref[...], left_ref[...])
    field = jnp.concatenate([middle_ref[...], beside], axis=1)
    classes = classes_ref[...]

    def moved(value, row, lane):
        if row:
            value = pltpu.roll(value, row % 16, axis=0)
        if lane:
            value = pltpu.roll(value, lane % 256, axis=1)
        return value

    for _ in range(2):
        twice = 2.0 * field
        up, down = moved(field, 1, 0), moved(field, -1, 0)
        along_rows = down + up - twice
        along_cols = moved(field, 0, -1) + moved(field, 0, 1) - twice
        diag_main = moved(down, 0, -1) + moved(up, 0, 1) - twice
        diag_anti = moved(down, 0, 1) + moved(up, 0, -1) - twice
        chosen = jnp.where(
            classes == 1.0,
            along_rows,
            jnp.where(classes == 2.0, along_cols, jnp.where(classes == 3.0, diag_main, diag_anti)),
        )
        field = field + FIBRE_RATE * chosen + ISO_RATE * (along_rows + along_cols)
        field = jnp.where(classes > 0.0, field, 0.0)
    out_ref[...] = field[2:10, :128]


def both_ways(value, axes, size, wrap):
    up = [(i, (i + 1) % size) for i in range(size if wrap else size - 1)]
    down = [(j, i) for i, j in up]
    return lax.ppermute(value, axes, up), lax.ppermute(value, axes, down)


def class_window(fibre_class):
    shifted = (fibre_class + 1).astype(F32)
    above, _ = both_ways(shifted[7:8], "sub", SUB, False)
    _, below = both_ways(shifted[0:1], "sub", SUB, False)
    gap = jnp.zeros((1, COLS), F32)
    middle = jnp.concatenate([gap, above, shifted, below, gap, gap, gap, gap, gap], axis=0)
    left, right = both_ways(middle, "load", LOAD, False)
    beside = jnp.where(lanes_of((16, 128)) < 64, right, left)
    return jnp.concatenate([middle, beside], axis=1)


def on_device(
    dual_ops,
    dual_rhs,
    partner,
    coarse_basis,
    coarse_inverse,
    damping,
    recovery,
    base_disp,
    adjoint,
    elem_voxel,
    fibre_class,
):
    damping = damping.reshape(1, COLS)
    tall = ((SPOTS, COLS), F32)
    to_sub = ((SUB, 16, COLS), F32)
    to_load = ((LOAD, 16, COLS), F32)
    edge = ((EDGE, COLS), BF16)
    whole = ("sub", "load")
    up = [(i, (i + 1) % (SUB * LOAD)) for i in range(SUB * LOAD)]
    down = [(j, i) for i, j in up]

    def over(value, axis):
        return lax.all_to_all(value, axis, 0, 0, tiled=True)

    (sent,) = call(
        first_terms,
        [((SUB, 32, COLS), F32)],
        (dual_rhs, coarse_basis, coarse_inverse),
        "first_terms",
    )
    received = over(sent, "sub")
    send, pick, lifted = call(
        setup,
        [((2 * EDGE, SPOTS), BF16), ((SPOTS, SPOTS + 2 * EDGE), BF16), ((SPOTS, COLS), BF16)],
        (partner, coarse_basis),
        "setup",
        flops=2 * SPOTS * SPOTS * 1024,
        moved=16 * 2**20,
    )
    partial, block = call(
        first_partial,
        [to_load, ((COLS, 2 * SUB * 16), BF16)],
        (received,),
        "first_partial",
    )
    residual = dual_rhs
    before = ()
    for iteration in range(2):
        received = over(partial, "load")
        iterate, images, lower, upper = call(
            functools.partial(advance, iteration == 0),
            [tall, ((SPOTS, COLS), BF16), edge, edge],
            (received, damping, lifted, dual_ops, send, residual) + before,
            "advance",
        )
        before = (iterate,)
        from_before = lax.ppermute(upper, whole, up)
        from_after = lax.ppermute(lower, whole, down)
        (inner,) = call(
            inner_pairs,
            [tall],
            (images, pick),
            "inner_pairs",
            flops=2 * SPOTS * SPOTS * 256,
            moved=4 * 2**20,
        )
        residual, sent = call(
            residual_terms,
            [tall, to_sub],
            (dual_rhs, images, inner, pick, from_before, from_after, coarse_basis),
            "residual_terms",
        )
        received = over(sent, "sub")
        (partial,) = call(later_partial, [to_load], (received, block), "later_partial")
    received = over(partial, "load")
    multipliers, sent = call(
        gradients,
        [((1, SPOTS, COLS), F32), to_sub],
        (received, damping, lifted, residual, iterate, recovery, base_disp, adjoint, elem_voxel),
        "gradients",
        limit=32,
    )
    middle = jnp.sum(over(sent, "sub"), axis=0)
    left, right = both_ways(middle, "load", LOAD, False)
    (field,) = call(
        smooth,
        [(fibre_class.shape, F32)],
        (middle, left, right, class_window(fibre_class)),
        "smooth",
    )
    return multipliers, field


def solution(mesh):
    placed = (
        P(("sub", "load"), None, None),
        P(("sub", "load"), None, None),
        P(("sub", "load"), None),
        P(("sub", "load"), None, None),
        P(("sub", "load"), None),
        P(),
        P(("sub", "load"), None, None),
        P(("sub", "load"), None, None),
        P(("sub", "load"), None, None),
        P(("sub", "load"), None),
        P("sub", "load"),
    )
    return jax.shard_map(
        on_device,
        mesh=mesh,
        in_specs=placed,
        out_specs=(P(("sub", "load"), None, None), P("sub", "load")),
        check_vma=False,
    )
```

time: 602 us -> 164 us (0.27)
  waiting for transfers between devices: 221 us -> 18.7 us
  blocking collectives: 248 us -> 69.5 us
  local copies, waits for them, and re-layouts: 48.3 us -> 17.4 us
  matrix products: 19.3 us -> 0 us
  between operations: 14.8 us -> 0.91 us
  Pallas kernels: 0 us -> 13.4 us
  other arithmetic: 10.9 us -> 0.05 us
  starting transfers between devices: 34.3 us -> 42.3 us
    psum x3 -> x0, blocking collectives: 248 us -> none  [on_device(): total_squares = lax.psum(squares, ('sub', 'load'))]
    unnamed x5 -> x0, waiting for transfers between devices: 135 us -> none
    all_to_all x0 -> x4, blocking collectives: none -> 69.5 us  [over(): return lax.all_to_all(value, axis, 0, 0, tiled=True)]
    all_gather x3 -> x0, waiting for transfers between devices: 69.3 us -> none  [on_device(): gathered = lax.all_gather(coarse_terms, ('sub', 'load'), axis=0, tiled=True)]
    all_to_all x0 -> x3, starting transfers between devices: none -> 23.6 us  [over(): return lax.all_to_all(value, axis, 0, 0, tiled=True)]
    gather x6 -> x0, local copies, waits for them, and re-layouts: 21.2 us -> none  [on_device(): partners = jnp.take(window, partner_rows, axis=0)]
    dot_general x13 -> x0, matrix products: 19.3 us -> none  [the longest x3 7.47 us: on_device(): jnp.dot(coarse_inverse, gathered, precision=lax.Precision.HIGHEST)]
    ppermute x14 -> x10, starting transfers between devices: 34.1 us -> 18.7 us  [the longest x6 16.7 us: both_ways(): return (lax.ppermute(value, axes, up), lax.ppermute(value, axes, down))]
  transfers between devices with their start and end apart: 18 -> 13, of which waited for: 13 -> 9; matrix products, arithmetic and copies ran while one was open for 1% -> 0% of each run, Pallas kernels for 0% -> 2%
where the time goes in v1:
time: 164 us; the launch traced here: 162 us
  blocking collectives  69.5 us (42%)
  starting transfers between devices  42.3 us (26%)
  waiting for transfers between devices  18.7 us (11%)
  local copies, waits for them, and re-layouts  17.4 us (11%)
  Pallas kernels  13.4 us (8%)
    all_to_all x4, blocking collectives, over(): return lax.all_to_all(value, axis, 0, 0, tiled=True)  69.5 us
    all_to_all x3, starting transfers between devices, over(): return lax.all_to_all(value, axis, 0, 0, tiled=True)  23.6 us
    unnamed x50, local copies, waits for them, and re-layouts  17.3 us
    ppermute x6, starting transfers between devices, both_ways(): return (lax.ppermute(value, axes, up), lax.ppermute(value, axes, down))  16.7 us
    pallas_call x13, Pallas kernels, call(): pl.pallas_call(kernel, out_shape=[jax.ShapeDtypeStruct(shape, dtype) for...  13.4 us
    ppermute x6, waiting for transfers between devices, both_ways(): return (lax.ppermute(value, axes, up), lax.ppermute(value, axes, down))  7.37 us
    all_to_all x3, waiting for transfers between devices, over(): return lax.all_to_all(value, axis, 0, 0, tiled=True)  5.48 us
    ppermute x2, waiting for transfers between devices, on_device(): from_after = lax.ppermute(lower, whole, down)  4.72 us
  transfers between devices with their start and end apart: 13, of which 9 were waited for; matrix products, arithmetic and copies ran while one was open for 0% of the time, Pallas kernels for 2%

profile of v1, /device:TPU:1, one launch (start us, length us, event | category | flops | bytes accessed | tf_op | source)
XLA Modules:
  0.0 162.4 jit_solution(4673613516426411741)
XLA Ops:
  3.6 26.0 %all_to_all.35.received_ref = f32[32,32,128]{2,1,0:T(8,128)S(1)} all-to-all(f32[32,32,128]{2,1,0:T(8,128)S(1)} %first_terms.1), channel_id=1, replica_groups=mesh['sub'=32,'load'=8] {'sub'}, dimensions={0} | all-to-all | bytes 1048576 | tf_op jit(solution)/shard_map/all_to_all | solution.py:292
  31.3 8.0 %all-to-all-start.1 = ((f32[8,16,128]{2,1,0:T(8,128)}), f32[8,16,128]{2,1,0:T(8,128)S(1)}, u32[]{:S(2)}, u32[]{:S(2)}) async-start(f32[8,16,128]{2,1,0:T(8,128)} %get-tuple-element.21), calls=%async_computation.1 | async-start | bytes 131072 | tf_op jit(solution)/shard_map/all_to_all | solution.py:292
  40.7 1.7 %setup.1 = (bf16[512,1024]{1,0:T(8,128)(2,1)S(1)}, bf16[1024,1536]{1,0:T(8,128)(2,1)S(1)}, bf16[1024,128]{1,0:T(8,128)(2,1)S(1)}) custom-call(s32[1,1024]{1,0:T(1,128)S(1)} %copy-done.23, bf16[1,12,1024]{2,1,0:T(8,128)(2,1)S(1)} %copy-done.18), custom_call_target="tpu_custom_call" | custom-call | flops 2147483648 | bytes 16777216 | tf_op jit(solution)/shard_map/setup/pallas_call | solution.py:31
  45.2 1.6 copy-done.3
  48.0 1.6 advance.2
  52.0 2.4 %collective-permute-done.1.after_ref = bf16[256,128]{1,0:T(8,128)(2,1)S(1)} collective-permute-done((bf16[256,128]{1,0:T(8,128)(2,1)S(1)}, bf16[256,128]{1,0:T(8,128)(2,1)S(1)}, u32[]{:S(2)}, u32[]{:S(2)}) %collective-permute-start.1) | collective-permute-done | bytes 65568 | tf_op jit(solution)/shard_map/ppermute | solution.py:327
  55.0 14.9 %all_to_all.36.received_ref = f32[32,16,128]{2,1,0:T(8,128)S(1)} all-to-all(f32[32,16,128]{2,1,0:T(8,128)S(1)} %get-tuple-element.28), channel_id=1, replica_groups=mesh['sub'=32,'load'=8] {'sub'}, dimensions={0} | all-to-all | bytes 524288 | tf_op jit(solution)/shard_map/all_to_all | solution.py:292
  70.1 14.8 %all_to_all.37.received_ref = f32[8,16,128]{2,1,0:T(8,128)S(1)} all-to-all(f32[8,16,128]{2,1,0:T(8,128)S(1)} %later_partial.2), channel_id=1, replica_groups=mesh['sub'=32,'load'=8] {'load'}, dimensions={0} | all-to-all | bytes 131072 | tf_op jit(solution)/shard_map/all_to_all | solution.py:292
  85.0 1.6 advance.3
  89.7 2.4 %collective-permute-done.3.after_ref = bf16[256,128]{1,0:T(8,128)(2,1)S(1)} collective-permute-done((bf16[256,128]{1,0:T(8,128)(2,1)S(1)}, bf16[256,128]{1,0:T(8,128)(2,1)S(1)}, u32[]{:S(2)}, u32[]{:S(2)}) %collective-permute-start.3) | collective-permute-done | bytes 65568 | tf_op jit(solution)/shard_map/ppermute | solution.py:327
  93.4 13.9 %all_to_all.38.received_ref = f32[32,16,128]{2,1,0:T(8,128)S(1)} all-to-all(f32[32,16,128]{2,1,0:T(8,128)S(1)} %get-tuple-element.35), channel_id=1, replica_groups=mesh['sub'=32,'load'=8] {'sub'}, dimensions={0} | all-to-all | bytes 524288 | tf_op jit(solution)/shard_map/all_to_all | solution.py:292
  108.2 11.2 %all-to-all-start.5 = ((f32[8,16,128]{2,1,0:T(8,128)}), f32[8,16,128]{2,1,0:T(8,128)S(1)}, u32[]{:S(2)}, u32[]{:S(2)}) async-start(f32[8,16,128]{2,1,0:T(8,128)} %later_partial.3), calls=%async_computation.5 | async-start | bytes 131072 | tf_op jit(solution)/shard_map/all_to_all | solution.py:292
  119.4 4.8 %all-to-all-done.5.received_ref = f32[8,16,128]{2,1,0:T(8,128)S(1)} async-done(((f32[8,16,128]{2,1,0:T(8,128)}), f32[8,16,128]{2,1,0:T(8,128)S(1)}, u32[]{:S(2)}, u32[]{:S(2)}) %all-to-all-start.5) | async-done | bytes 65568 | tf_op jit(solution)/shard_map/all_to_all | solution.py:292
  124.3 1.9 %copy-done.8 = bf16[1,1536,1024]{2,1,0:T(8,128)(2,1)S(1)} copy-done((bf16[1,1536,1024]{2,1,0:T(8,128)(2,1)S(1)}, bf16[1,1536,1024]{2,1,0:T(8,128)(2,1)}, u32[]{:S(2)}) %copy-start.8) | copy-done | bytes 3145752
  130.2 2.7 %gradients.1 = (f32[1,1024,128]{2,1,0:T(8,128)}, f32[32,16,128]{2,1,0:T(8,128)}) custom-call(f32[8,16,128]{2,1,0:T(8,128)S(1)} %all-to-all-done.5.received_ref, f32[1,128]{1,0:T(1,128)S(1)} %bitcast.3, bf16[1024,128]{1,0:T(8,128)(2,1)S(1)} %get-tuple-element.22.lifted_ref, f32[1024,128]{1,0:T(8,128)S(1)} %copy-done.14, f32[1024,128]{1,0:T(8,128)S(1)} %copy-done.12, ...), custom_call_target="tpu_custom_call" | custom-call | tf_op jit(solution)/shard_map/gradients/pallas_call | solution.py:31
  132.9 4.4 %all-to-all-start.6 = ((f32[32,16,128]{2,1,0:T(8,128)}), f32[32,16,128]{2,1,0:T(8,128)S(1)}, u32[]{:S(2)}, u32[]{:S(2)}) async-start(f32[32,16,128]{2,1,0:T(8,128)} %get-tuple-element.39), calls=%async_computation.6 | async-start | bytes 524288 | tf_op jit(solution)/shard_map/all_to_all | solution.py:292
  137.3 3.1 %collective-permute-start.6 = (f32[1,128]{1,0:T(1,128)S(1)}, f32[1,128]{1,0:T(1,128)S(1)}, u32[]{:S(2)}, u32[]{:S(2)}) collective-permute-start(f32[1,128]{1,0:T(1,128)S(1)} %get-tuple-element.41), channel_id=1, source_target_pairs={{0,8},{8,16},{16,24},{24,32},{32,40},{40,48},{48,56},{56,64},{64,7... | collective-permute-start | bytes 1544 | tf_op jit(solution)/shard_map/ppermute | solution.py:255
  140.4 1.3 collective-permute-start.7
  141.7 3.4 %collective-permute-done.7 = f32[1,128]{1,0:T(1,128)S(1)} collective-permute-done((f32[1,128]{1,0:T(1,128)S(1)}, f32[1,128]{1,0:T(1,128)S(1)}, u32[]{:S(2)}, u32[]{:S(2)}) %collective-permute-start.7) | collective-permute-done | bytes 544 | tf_op jit(solution)/shard_map/ppermute | solution.py:255
  145.3 4.2 %collective-permute-start.8 = (f32[16,128]{1,0:T(8,128)S(1)}, f32[16,128]{1,0:T(8,128)S(1)}, u32[]{:S(2)}, u32[]{:S(2)}) collective-permute-start(f32[16,128]{1,0:T(8,128)S(1)} %concatenate.10), channel_id=1, source_target_pairs={{1,0},{2,1},{3,2},{4,3},{5,4},{6,5},{7,6},{9,8},{10,9},{11,10},{12... | collective-permute-start | bytes 24584 | tf_op jit(solution)/shard_map/ppermute | solution.py:255
  149.5 2.1 %collective-permute-start.9 = (f32[16,128]{1,0:T(8,128)S(1)}, f32[16,128]{1,0:T(8,128)S(1)}, u32[]{:S(2)}, u32[]{:S(2)}) collective-permute-start(f32[16,128]{1,0:T(8,128)S(1)} %concatenate.10), channel_id=1, source_target_pairs={{0,1},{1,2},{2,3},{3,4},{4,5},{5,6},{6,7},{8,9},{9,10},{10,11},{11... | collective-permute-start | bytes 24584 | tf_op jit(solution)/shard_map/ppermute | solution.py:255
  152.6 4.0 %collective-permute-start.4 = (f32[16,128]{1,0:T(8,128)S(1)}, f32[16,128]{1,0:T(8,128)S(1)}, u32[]{:S(2)}, u32[]{:S(2)}) collective-permute-start(f32[16,128]{1,0:T(8,128)S(1)} %reduce_sum.9.middle_ref), channel_id=1, source_target_pairs={{0,1},{1,2},{2,3},{3,4},{4,5},{5,6},{6,7},{8,9},{9,10},{10,11},{11... | collective-permute-start | bytes 24584 | tf_op jit(solution)/shard_map/ppermute | solution.py:255
  156.6 1.9 %collective-permute-start.5 = (f32[16,128]{1,0:T(8,128)S(1)}, f32[16,128]{1,0:T(8,128)S(1)}, u32[]{:S(2)}, u32[]{:S(2)}) collective-permute-start(f32[16,128]{1,0:T(8,128)S(1)} %reduce_sum.9.middle_ref), channel_id=1, source_target_pairs={{1,0},{2,1},{3,2},{4,3},{5,4},{6,5},{7,6},{9,8},{10,9},{11,10},{12... | collective-permute-start | bytes 24584 | tf_op jit(solution)/shard_map/ppermute | solution.py:255
  158.6 3.0 %collective-permute-done.5.right_ref = f32[16,128]{1,0:T(8,128)S(1)} collective-permute-done((f32[16,128]{1,0:T(8,128)S(1)}, f32[16,128]{1,0:T(8,128)S(1)}, u32[]{:S(2)}, u32[]{:S(2)}) %collective-permute-start.5) | collective-permute-done | bytes 8224 | tf_op jit(solution)/shard_map/ppermute | solution.py:255
  (78 shorter events, 24.6 us)
Async XLA Ops:
  31.3 12.8 %all-to-all-start.1 = ((f32[8,16,128]{2,1,0:T(8,128)}), f32[8,16,128]{2,1,0:T(8,128)S(1)}, u32[]{:S(2)}, u32[]{:S(2)}) async-start(f32[8,16,128]{2,1,0:T(8,128)} %get-tuple-element.21), calls=%async_computation.1 | async-start | bytes 131072 | tf_op jit(solution)/shard_map/all_to_all | solution.py:292
  40.7 3.4 %copy-start.21 = (f32[128]{0:T(128)S(1)}, f32[128]{0:T(128)}, u32[]{:S(2)}) copy-start(f32[128]{0:T(128)} %param.16) | copy-start | bytes 1540
  45.2 1.6 copy-start.3
  46.8 1.2 copy-start.6
  48.0 6.4 %copy-start.19 = (bf16[1,12,1024]{2,1,0:T(8,128)(2,1)S(1)}, bf16[1,12,1024]{2,1,0:T(8,128)(2,1)}, u32[]{:S(2)}) copy-start(bf16[1,12,1024]{2,1,0:T(8,128)(2,1)} %basis_ref.7) | copy-start | bytes 73732
  49.6 2.4 %collective-permute-start = (bf16[256,128]{1,0:T(8,128)(2,1)S(1)}, bf16[256,128]{1,0:T(8,128)(2,1)S(1)}, u32[]{:S(2)}, u32[]{:S(2)}) collective-permute-start(bf16[256,128]{1,0:T(8,128)(2,1)S(1)} %get-tuple-element.26), channel_id=1, source_target_pairs={{0,1},{1,2},{2,3},{3,4},{4,5},{5,6},{6,7},{7,8},{8,9},{9,10},{10,1... | collective-permute-start | bytes 196616 | tf_op jit(solution)/shard_map/ppermute | solution.py:326
  50.7 3.7 %collective-permute-start.1 = (bf16[256,128]{1,0:T(8,128)(2,1)S(1)}, bf16[256,128]{1,0:T(8,128)(2,1)S(1)}, u32[]{:S(2)}, u32[]{:S(2)}) collective-permute-start(bf16[256,128]{1,0:T(8,128)(2,1)S(1)} %get-tuple-element.27), channel_id=1, source_target_pairs={{1,0},{2,1},{3,2},{4,3},{5,4},{6,5},{7,6},{8,7},{9,8},{10,9},{11,1... | collective-permute-start | bytes 196616 | tf_op jit(solution)/shard_map/ppermute | solution.py:327
  51.4 18.4 %copy-start.10 = (bf16[128,1024]{1,0:T(8,128)(2,1)S(1)}, bf16[128,1024]{1,0:T(8,128)(2,1)}, u32[]{:S(2)}) copy-start(bf16[128,1024]{1,0:T(8,128)(2,1)} %copy-done.9) | copy-start | bytes 786436
  51.4 33.5 %copy-start.4 = (bf16[1,1024,1024]{2,1,0:T(8,128)(2,1)S(1)}, bf16[1,1024,1024]{2,1,0:T(8,128)(2,1)}, u32[]{:S(2)}) copy-start(bf16[1,1024,1024]{2,1,0:T(8,128)(2,1)} %operator_ref.3) | copy-start | bytes 6291460
  51.4 33.5 %copy-start.7 = (bf16[512,1024]{1,0:T(8,128)(2,1)S(1)}, bf16[512,1024]{1,0:T(8,128)(2,1)}, u32[]{:S(2)}) copy-start(bf16[512,1024]{1,0:T(8,128)(2,1)} %copy-done.5) | copy-start | bytes 3145732
  85.0 7.1 %copy-start.2 = (f32[1,1024,128]{2,1,0:T(8,128)S(1)}, f32[1,1024,128]{2,1,0:T(8,128)}, u32[]{:S(2)}) copy-start(f32[1,1024,128]{2,1,0:T(8,128)} %rhs_ref.5) | copy-start | bytes 1572868
  87.4 2.3 %collective-permute-start.2 = (bf16[256,128]{1,0:T(8,128)(2,1)S(1)}, bf16[256,128]{1,0:T(8,128)(2,1)S(1)}, u32[]{:S(2)}, u32[]{:S(2)}) collective-permute-start(bf16[256,128]{1,0:T(8,128)(2,1)S(1)} %get-tuple-element.33), channel_id=1, source_target_pairs={{0,1},{1,2},{2,3},{3,4},{4,5},{5,6},{6,7},{7,8},{8,9},{9,10},{10,1... | collective-permute-start | bytes 196616 | tf_op jit(solution)/shard_map/ppermute | solution.py:326
  88.3 3.7 %collective-permute-start.3 = (bf16[256,128]{1,0:T(8,128)(2,1)S(1)}, bf16[256,128]{1,0:T(8,128)(2,1)S(1)}, u32[]{:S(2)}, u32[]{:S(2)}) collective-permute-start(bf16[256,128]{1,0:T(8,128)(2,1)S(1)} %get-tuple-element.34), channel_id=1, source_target_pairs={{1,0},{2,1},{3,2},{4,3},{5,4},{6,5},{7,6},{8,7},{9,8},{10,9},{11,1... | collective-permute-start | bytes 196616 | tf_op jit(solution)/shard_map/ppermute | solution.py:327
  89.1 30.4 %copy-start.24 = (s32[8,128]{1,0:T(8,128)S(1)}, s32[8,128]{1,0:T(8,128)}, u32[]{:S(2)}) copy-start(s32[8,128]{1,0:T(8,128)} %param.21) | copy-start | bytes 12292
  89.1 35.2 %copy-start.22 = (s32[1,128]{1,0:T(1,128)S(1)}, s32[1,128]{1,0:T(1,128)}, u32[]{:S(2)}) copy-start(s32[1,128]{1,0:T(1,128)} %voxel_ref.1) | copy-start | bytes 1540
  108.2 16.1 %all-to-all-start.5 = ((f32[8,16,128]{2,1,0:T(8,128)}), f32[8,16,128]{2,1,0:T(8,128)S(1)}, u32[]{:S(2)}, u32[]{:S(2)}) async-start(f32[8,16,128]{2,1,0:T(8,128)} %later_partial.3), calls=%async_computation.5 | async-start | bytes 131072 | tf_op jit(solution)/shard_map/all_to_all | solution.py:292
  124.3 1.9 %copy-start.8 = (bf16[1,1536,1024]{2,1,0:T(8,128)(2,1)S(1)}, bf16[1,1536,1024]{2,1,0:T(8,128)(2,1)}, u32[]{:S(2)}) copy-start(bf16[1,1536,1024]{2,1,0:T(8,128)(2,1)} %recovery_ref.1) | copy-start | bytes 9437188
  132.9 19.7 %all-to-all-start.6 = ((f32[32,16,128]{2,1,0:T(8,128)}), f32[32,16,128]{2,1,0:T(8,128)S(1)}, u32[]{:S(2)}, u32[]{:S(2)}) async-start(f32[32,16,128]{2,1,0:T(8,128)} %get-tuple-element.39), calls=%async_computation.6 | async-start | bytes 524288 | tf_op jit(solution)/shard_map/all_to_all | solution.py:292
  137.3 4.4 %collective-permute-start.6 = (f32[1,128]{1,0:T(1,128)S(1)}, f32[1,128]{1,0:T(1,128)S(1)}, u32[]{:S(2)}, u32[]{:S(2)}) collective-permute-start(f32[1,128]{1,0:T(1,128)S(1)} %get-tuple-element.41), channel_id=1, source_target_pairs={{0,8},{8,16},{16,24},{24,32},{32,40},{40,48},{48,56},{56,64},{64,7... | collective-permute-start | bytes 1544 | tf_op jit(solution)/shard_map/ppermute | solution.py:255
  140.4 4.7 %collective-permute-start.7 = (f32[1,128]{1,0:T(1,128)S(1)}, f32[1,128]{1,0:T(1,128)S(1)}, u32[]{:S(2)}, u32[]{:S(2)}) collective-permute-start(f32[1,128]{1,0:T(1,128)S(1)} %get-tuple-element.40), channel_id=1, source_target_pairs={{8,0},{16,8},{24,16},{32,24},{40,32},{48,40},{56,48},{64,56},{72,6... | collective-permute-start | bytes 1544 | tf_op jit(solution)/shard_map/ppermute | solution.py:255
  145.3 6.4 %collective-permute-start.8 = (f32[16,128]{1,0:T(8,128)S(1)}, f32[16,128]{1,0:T(8,128)S(1)}, u32[]{:S(2)}, u32[]{:S(2)}) collective-permute-start(f32[16,128]{1,0:T(8,128)S(1)} %concatenate.10), channel_id=1, source_target_pairs={{1,0},{2,1},{3,2},{4,3},{5,4},{6,5},{7,6},{9,8},{10,9},{11,10},{12... | collective-permute-start | bytes 24584 | tf_op jit(solution)/shard_map/ppermute | solution.py:255
  149.5 3.1 %collective-permute-start.9 = (f32[16,128]{1,0:T(8,128)S(1)}, f32[16,128]{1,0:T(8,128)S(1)}, u32[]{:S(2)}, u32[]{:S(2)}) collective-permute-start(f32[16,128]{1,0:T(8,128)S(1)} %concatenate.10), channel_id=1, source_target_pairs={{0,1},{1,2},{2,3},{3,4},{4,5},{5,6},{6,7},{8,9},{9,10},{10,11},{11... | collective-permute-start | bytes 24584 | tf_op jit(solution)/shard_map/ppermute | solution.py:255
  152.6 5.9 %collective-permute-start.4 = (f32[16,128]{1,0:T(8,128)S(1)}, f32[16,128]{1,0:T(8,128)S(1)}, u32[]{:S(2)}, u32[]{:S(2)}) collective-permute-start(f32[16,128]{1,0:T(8,128)S(1)} %reduce_sum.9.middle_ref), channel_id=1, source_target_pairs={{0,1},{1,2},{2,3},{3,4},{4,5},{5,6},{6,7},{8,9},{9,10},{10,11},{11... | collective-permute-start | bytes 24584 | tf_op jit(solution)/shard_map/ppermute | solution.py:255
  156.6 5.0 %collective-permute-start.5 = (f32[16,128]{1,0:T(8,128)S(1)}, f32[16,128]{1,0:T(8,128)S(1)}, u32[]{:S(2)}, u32[]{:S(2)}) collective-permute-start(f32[16,128]{1,0:T(8,128)S(1)} %reduce_sum.9.middle_ref), channel_id=1, source_target_pairs={{1,0},{2,1},{3,2},{4,3},{5,4},{6,5},{7,6},{9,8},{10,9},{11,10},{12... | collective-permute-start | bytes 24584 | tf_op jit(solution)/shard_map/ppermute | solution.py:255
  (14 other events, 12.6 us)

commit v2 on v1

--- a/solution.py
+++ b/solution.py
@@ -27,7 +27,7 @@
 BF16 = jnp.bfloat16
 
 
-def call(kernel, outs, operands, name, flops=0, moved=0, limit=24, scratch=()):
+def call(kernel, outs, operands, name, flops=0, moved=0, limit=16, scratch=()):
     return pl.pallas_call(
         kernel,
         out_shape=[jax.ShapeDtypeStruct(shape, dtype) for shape, dtype in outs],
@@ -75,20 +75,30 @@
     return jnp.where(rows_of(terms.shape) == MODES, squares, terms)
 
 
-def first_terms(rhs_ref, basis_ref, inverse_ref, out_ref):
+def first_terms(rhs_ref, basis_ref, inverse_ref, class_ref, out_ref):
     rows = coarse_rows(basis_ref, rhs_ref[0])
-    inverse = jnp.concatenate([inverse_ref[...], jnp.zeros((4, SUB * LOAD * MODES), F32)], axis=0)
+    classes = (class_ref[...] + 1).astype(F32)
+    row = rows_of(rows.shape)
+    rows = jnp.where(row == 13, classes[0:1], jnp.where(row == 14, classes[7:8], rows))
+    inverse = inverse_ref[...]
     inverse = jnp.concatenate([inverse, inverse[:, :128]], axis=1)
-    lanes = lanes_of((16, COLS))
-    mark = jnp.where((rows_of((16, COLS)) == MODES) & (lanes == MARK), 1.0, 0.0)
+    lanes = lanes_of((8, COLS))
+    lane = lanes_of((1, COLS))
     for peer in range(SUB):
         start = peer * LOAD * MODES
         tile, offset = start // 128, start % 128
         piece = inverse[:, 128 * tile : 128 * tile + 256]
         if offset:
             piece = pltpu.roll(piece, 256 - offset, axis=1)
-        out_ref[peer, :16, :] = rows
-        out_ref[peer, 16:, :] = jnp.where(lanes < LOAD * MODES, piece[:, :128], mark)
+        piece = piece[:, :128]
+        last = piece[8:12]
+        beside = jnp.concatenate([pltpu.roll(last, 96, axis=1), pltpu.roll(last, 64, axis=1)], axis=0)
+        spare = pltpu.roll(last[0:1], 64, axis=1)
+        for place, turn in ((1, 96), (2, 0), (3, 32)):
+            part = last[place : place + 1]
+            spare = jnp.where(lane < 32 * place, spare, pltpu.roll(part, turn, axis=1) if turn else part)
+        out_ref[peer, :16, :] = jnp.where(row == 15, spare, rows)
+        out_ref[peer, 16:, :] = jnp.where(lanes < 96, piece[:8], beside)
 
 
 def partial_rows(high, low, terms, out_ref):
@@ -99,13 +109,38 @@
         out_ref[peer] = jnp.concatenate([partial[MODES * peer : MODES * peer + MODES], last], axis=0)
 
 
-def first_partial(received_ref, out_ref, block_ref):
+def first_partial(received_ref, class_ref, out_ref, block_ref, middle_ref):
     terms = received_ref[:, :16, :].reshape(SUB * 16, COLS)
-    block = received_ref[:, 16:, :].reshape(SUB * 16, COLS).T
-    high, low = split2(block)
+    packed = received_ref[:, 16:, :].reshape(SUB * 8, COLS)
+    lanes = lanes_of((SUB * 8, COLS))
+    upper = jnp.where(lanes < 96, packed, 0.0).reshape(SUB, 8, COLS)
+    first = pltpu.roll(packed, 32, axis=1).reshape(SUB, 8, COLS)[:, :4]
+    second = pltpu.roll(packed, 64, axis=1).reshape(SUB, 8, COLS)[:, 4:]
+    spare = received_ref[:, 15, :]
+    third = [pltpu.roll(spare, 64, axis=1), pltpu.roll(spare, 32, axis=1), spare, pltpu.roll(spare, 96, axis=1)]
+    third = jnp.concatenate([part.reshape(SUB, 1, COLS) for part in third], axis=1)
+    lanes = lax.broadcasted_iota(jnp.int32, (SUB, 4, COLS), 2)
+    lower = jnp.where(lanes < 32, first, jnp.where(lanes < 64, second, jnp.where(lanes < 96, third, 0.0)))
+    places = lax.broadcasted_iota(jnp.int32, (SUB, 4, COLS), 1)
+    mark = jnp.where((places == 0) & (lanes == MARK), 1.0, 0.0)
+    block = jnp.concatenate([upper, jnp.concatenate([lower, mark], axis=1)], axis=1)
+    high, low = split2(block.reshape(SUB * 16, COLS).T)
     block_ref[:, : SUB * 16] = high
     block_ref[:, SUB * 16 :] = low
     partial_rows(high, low, terms, out_ref)
+    here = lax.axis_index("sub")
+    above = received_ref[jnp.maximum(here - 1, 0)][14:15]
+    below = received_ref[jnp.minimum(here + 1, SUB - 1)][13:14]
+    above = jnp.where(here > 0, above, 0.0)
+    below = jnp.where(here < SUB - 1, below, 0.0)
+    classes = (class_ref[...] + 1).astype(F32)
+    gap = jnp.zeros((1, COLS), F32)
+    middle = jnp.concatenate([gap, above, classes, below, gap, gap, gap, gap, gap], axis=0)
+    middle_ref[...] = middle
+    sides = jnp.concatenate([middle, jnp.zeros((COLS - 16, COLS), F32)], axis=0).T
+    for peer in range(LOAD):
+        out_ref[peer, 13:14, :] = sides[0:1]
+        out_ref[peer, 14:15, :] = sides[127:128]
 
 
 def later_partial(received_ref, block_ref, out_ref):
@@ -174,6 +209,20 @@
 
 def inner_pairs(images_ref, pick_ref, out_ref):
     out_ref[...] = dot(pick_ref[:, EDGE : EDGE + SPOTS], images_ref[...])
+
+
+def inner_classes(images_ref, pick_ref, received_ref, middle_ref, out_ref, classes_ref):
+    here = lax.axis_index("load")
+    right = received_ref[jnp.minimum(here + 1, LOAD - 1)][13:14]
+    left = received_ref[jnp.maximum(here - 1, 0)][14:15]
+    right = jnp.where(here < LOAD - 1, right, 0.0)
+    left = jnp.where(here > 0, left, 0.0)
+    right = jnp.broadcast_to(right, (128, 128)).T[:16]
+    left = jnp.broadcast_to(left, (128, 128)).T[:16]
+    lanes = lanes_of((16, 128))
+    classes_ref[:, :128] = middle_ref[...]
+    classes_ref[:, 128:] = jnp.where(lanes == 0, right, jnp.where(lanes == 127, left, 0.0))
+    inner_pairs(images_ref, pick_ref, out_ref)
 
 
 def residual_terms(rhs_ref, images_ref, inner_ref, pick_ref, before_ref, after_ref, basis_ref, residual_ref, out_ref):
@@ -255,17 +304,6 @@
     return lax.ppermute(value, axes, up), lax.ppermute(value, axes, down)
 
 
-def class_window(fibre_class):
-    shifted = (fibre_class + 1).astype(F32)
-    above, _ = both_ways(shifted[7:8], "sub", SUB, False)
-    _, below = both_ways(shifted[0:1], "sub", SUB, False)
-    gap = jnp.zeros((1, COLS), F32)
-    middle = jnp.concatenate([gap, above, shifted, below, gap, gap, gap, gap, gap], axis=0)
-    left, right = both_ways(middle, "load", LOAD, False)
-    beside = jnp.where(lanes_of((16, 128)) < 64, right, left)
-    return jnp.concatenate([middle, beside], axis=1)
-
-
 def on_device(
     dual_ops,
     dual_rhs,
@@ -293,8 +331,8 @@
 
     (sent,) = call(
         first_terms,
-        [((SUB, 32, COLS), F32)],
-        (dual_rhs, coarse_basis, coarse_inverse),
+        [((SUB, 24, COLS), F32)],
+        (dual_rhs, coarse_basis, coarse_inverse, fibre_class),
         "first_terms",
     )
     received = over(sent, "sub")
@@ -306,10 +344,10 @@
         flops=2 * SPOTS * SPOTS * 1024,
         moved=16 * 2**20,
     )
-    partial, block = call(
+    partial, block, middle = call(
         first_partial,
-        [to_load, ((COLS, 2 * SUB * 16), BF16)],
-        (received,),
+        [to_load, ((COLS, 2 * SUB * 16), BF16), ((16, COLS), F32)],
+        (received, fibre_class),
         "first_partial",
     )
     residual = dual_rhs
@@ -325,14 +363,18 @@
         before = (iterate,)
         from_before = lax.ppermute(upper, whole, up)
         from_after = lax.ppermute(lower, whole, down)
-        (inner,) = call(
-            inner_pairs,
-            [tall],
-            (images, pick),
+        more = (received, middle) if iteration == 0 else ()
+        inner = call(
+            inner_pairs if iteration else inner_classes,
+            [tall] if iteration else [tall, ((16, 2 * COLS), F32)],
+            (images, pick) + more,
             "inner_pairs",
             flops=2 * SPOTS * SPOTS * 256,
             moved=4 * 2**20,
         )
+        if iteration == 0:
+            classes = inner[1]
+        inner = inner[0]
         residual, sent = call(
             residual_terms,
             [tall, to_sub],
@@ -347,14 +389,13 @@
         [((1, SPOTS, COLS), F32), to_sub],
         (received, damping, lifted, residual, iterate, recovery, base_disp, adjoint, elem_voxel),
         "gradients",
-        limit=32,
     )
     middle = jnp.sum(over(sent, "sub"), axis=0)
     left, right = both_ways(middle, "load", LOAD, False)
     (field,) = call(
         smooth,
         [(fibre_class.shape, F32)],
-        (middle, left, right, class_window(fibre_class)),
+        (middle, left, right, classes),
         "smooth",
     )
     return multipliers, field

time: 164 us -> 148 us (0.902)
  blocking collectives: 69.5 us -> 96.6 us
  starting transfers between devices: 42.3 us -> 18 us
  waiting for transfers between devices: 18.7 us -> 7.48 us
  local copies, waits for them, and re-layouts: 17.4 us -> 10.4 us
    all_to_all x4 -> x6, blocking collectives: 69.5 us -> 96.6 us  [over(): return lax.all_to_all(value, axis, 0, 0, tiled=True)]
    all_to_all x3 -> x1, starting transfers between devices: 23.6 us -> 8.3 us  [over(): return lax.all_to_all(value, axis, 0, 0, tiled=True)]
    ppermute x6 -> x2, starting transfers between devices: 16.7 us -> 7.66 us  [both_ways(): return (lax.ppermute(value, axes, up), lax.ppermute(value, axes, down))]
    unnamed x50 -> x42, local copies, waits for them, and re-layouts: 17.3 us -> 10.4 us
    ppermute x6 -> x2, waiting for transfers between devices: 7.37 us -> 0.96 us  [both_ways(): return (lax.ppermute(value, axes, up), lax.ppermute(value, axes, down))]
    all_to_all x3 -> x1, waiting for transfers between devices: 5.48 us -> 0.66 us  [over(): return lax.all_to_all(value, axis, 0, 0, tiled=True)]
  transfers between devices with their start and end apart: 13 -> 7, of which waited for: 9 -> 6; matrix products, arithmetic and copies ran while one was open for 0% -> 0% of each run, Pallas kernels for 2% -> 2%
where the time goes in v2:
time: 148 us; the launch traced here: 147 us
  blocking collectives  96.6 us (65%)
  starting transfers between devices  18 us (12%)
  Pallas kernels  13.3 us (9%)
  local copies, waits for them, and re-layouts  10.4 us (7%)
  waiting for transfers between devices  7.48 us (5%)
    all_to_all x6, blocking collectives, over(): return lax.all_to_all(value, axis, 0, 0, tiled=True)  96.6 us
    pallas_call x13, Pallas kernels, call(): pl.pallas_call(kernel, out_shape=[jax.ShapeDtypeStruct(shape, dtype) for...  13.3 us
    unnamed x42, local copies, waits for them, and re-layouts  10.4 us
    all_to_all x1, starting transfers between devices, over(): return lax.all_to_all(value, axis, 0, 0, tiled=True)  8.3 us
    ppermute x2, starting transfers between devices, both_ways(): return (lax.ppermute(value, axes, up), lax.ppermute(value, axes, down))  7.66 us
    ppermute x2, waiting for transfers between devices, on_device(): from_after = lax.ppermute(lower, whole, down)  4.72 us
  transfers between devices with their start and end apart: 7, of which 6 were waited for; matrix products, arithmetic and copies ran while one was open for 0% of the time, Pallas kernels for 2%

profile of v2, /device:TPU:1, one launch (start us, length us, event | category | flops | bytes accessed | tf_op | source)
XLA Modules:
  0.0 146.7 jit_solution(15320961703740590473)
XLA Ops:
  0.6 1.0 copy-done
  4.0 1.0 first_terms.1
  5.1 23.3 %all_to_all.35.received_ref = f32[32,24,128]{2,1,0:T(8,128)S(1)} all-to-all(f32[32,24,128]{2,1,0:T(8,128)S(1)} %first_terms.1), channel_id=1, replica_groups=mesh['sub'=32,'load'=8] {'sub'}, dimensions={0} | all-to-all | bytes 786432 | tf_op jit(solution)/shard_map/all_to_all | solution.py:330
  28.4 1.1 first_partial.1
  30.2 8.3 %all-to-all-start.1 = ((f32[8,16,128]{2,1,0:T(8,128)}), f32[8,16,128]{2,1,0:T(8,128)S(1)}, u32[]{:S(2)}, u32[]{:S(2)}) async-start(f32[8,16,128]{2,1,0:T(8,128)} %get-tuple-element.24), calls=%async_computation.1 | async-start | bytes 131072 | tf_op jit(solution)/shard_map/all_to_all | solution.py:330
  40.0 1.7 %setup.1 = (bf16[512,1024]{1,0:T(8,128)(2,1)S(1)}, bf16[1024,1536]{1,0:T(8,128)(2,1)S(1)}, bf16[1024,128]{1,0:T(8,128)(2,1)S(1)}) custom-call(s32[1,1024]{1,0:T(1,128)S(1)} %copy-done.20, bf16[1,12,1024]{2,1,0:T(8,128)(2,1)S(1)} %copy-done.14), custom_call_target="tpu_custom_call" | custom-call | flops 2147483648 | bytes 16777216 | tf_op jit(solution)/shard_map/setup/pallas_call | solution.py:31
  41.7 1.0 copy-done.5
  43.4 1.0 copy-done.1
  44.4 1.6 %copy-done.3 = bf16[1,1024,1024]{2,1,0:T(8,128)(2,1)S(1)} copy-done((bf16[1,1024,1024]{2,1,0:T(8,128)(2,1)S(1)}, bf16[1,1024,1024]{2,1,0:T(8,128)(2,1)}, u32[]{:S(2)}) %copy-start.3) | copy-done | bytes 2097176
  46.0 1.2 copy-done.6
  47.2 1.6 %advance.2 = (f32[1024,128]{1,0:T(8,128)S(1)}, bf16[1024,128]{1,0:T(8,128)(2,1)S(1)}, bf16[256,128]{1,0:T(8,128)(2,1)S(1)}, bf16[256,128]{1,0:T(8,128)(2,1)S(1)}) custom-call(f32[8,16,128]{2,1,0:T(8,128)S(1)} %all-to-all-done.1.received_ref, f32[1,128]{1,0:T(1,128)S(1)} %bitcast.1, bf16[1024,128]{1,0:T(8,128)(2,1)S(1)} %get-tuple-element.25.lifted_ref, ...), custom_call_target="tpu_custom_call" | custom-call | tf_op jit(solution)/shard_map/advance/pallas_call | solution.py:31
  48.8 1.1 collective-permute-start
  51.2 2.4 %collective-permute-done.1.after_ref = bf16[256,128]{1,0:T(8,128)(2,1)S(1)} collective-permute-done((bf16[256,128]{1,0:T(8,128)(2,1)S(1)}, bf16[256,128]{1,0:T(8,128)(2,1)S(1)}, u32[]{:S(2)}, u32[]{:S(2)}) %collective-permute-start.1) | collective-permute-done | bytes 65568 | tf_op jit(solution)/shard_map/ppermute | solution.py:365
  54.2 14.4 %all_to_all.36.received_ref = f32[32,16,128]{2,1,0:T(8,128)S(1)} all-to-all(f32[32,16,128]{2,1,0:T(8,128)S(1)} %get-tuple-element.33), channel_id=1, replica_groups=mesh['sub'=32,'load'=8] {'sub'}, dimensions={0} | all-to-all | bytes 524288 | tf_op jit(solution)/shard_map/all_to_all | solution.py:330
  68.9 15.3 %all_to_all.37.received_ref = f32[8,16,128]{2,1,0:T(8,128)S(1)} all-to-all(f32[8,16,128]{2,1,0:T(8,128)S(1)} %later_partial.2), channel_id=1, replica_groups=mesh['sub'=32,'load'=8] {'load'}, dimensions={0} | all-to-all | bytes 131072 | tf_op jit(solution)/shard_map/all_to_all | solution.py:330
  84.2 1.6 %advance.3 = (f32[1024,128]{1,0:T(8,128)S(1)}, bf16[1024,128]{1,0:T(8,128)(2,1)S(1)}, bf16[256,128]{1,0:T(8,128)(2,1)S(1)}, bf16[256,128]{1,0:T(8,128)(2,1)S(1)}) custom-call(f32[8,16,128]{2,1,0:T(8,128)S(1)} %all_to_all.37.received_ref, f32[1,128]{1,0:T(1,128)S(1)} %bitcast.2, bf16[1024,128]{1,0:T(8,128)(2,1)S(1)} %get-tuple-element.25.lifted_ref, ...), custom_call_target="tpu_custom_call" | custom-call | tf_op jit(solution)/shard_map/advance/pallas_call | solution.py:31
  85.8 1.0 collective-permute-start.2
  88.2 2.4 %collective-permute-done.3.after_ref = bf16[256,128]{1,0:T(8,128)(2,1)S(1)} collective-permute-done((bf16[256,128]{1,0:T(8,128)(2,1)S(1)}, bf16[256,128]{1,0:T(8,128)(2,1)S(1)}, u32[]{:S(2)}, u32[]{:S(2)}) %collective-permute-start.3) | collective-permute-done | bytes 65568 | tf_op jit(solution)/shard_map/ppermute | solution.py:365
  91.2 13.9 %all_to_all.38.received_ref = f32[32,16,128]{2,1,0:T(8,128)S(1)} all-to-all(f32[32,16,128]{2,1,0:T(8,128)S(1)} %get-tuple-element.40), channel_id=1, replica_groups=mesh['sub'=32,'load'=8] {'sub'}, dimensions={0} | all-to-all | bytes 524288 | tf_op jit(solution)/shard_map/all_to_all | solution.py:330
  105.3 15.9 %all_to_all.39.received_ref = f32[8,16,128]{2,1,0:T(8,128)S(1)} all-to-all(f32[8,16,128]{2,1,0:T(8,128)S(1)} %later_partial.3), channel_id=1, replica_groups=mesh['sub'=32,'load'=8] {'load'}, dimensions={0} | all-to-all | bytes 131072 | tf_op jit(solution)/shard_map/all_to_all | solution.py:330
  121.2 2.2 %gradients.1 = (f32[1,1024,128]{2,1,0:T(8,128)}, f32[32,16,128]{2,1,0:T(8,128)S(1)}) custom-call(f32[8,16,128]{2,1,0:T(8,128)S(1)} %all_to_all.39.received_ref, f32[1,128]{1,0:T(1,128)S(1)} %bitcast.3, bf16[1024,128]{1,0:T(8,128)(2,1)S(1)} %get-tuple-element.25.lifted_ref, f32[1024,128]{1,0:T(8,128)S(1)} %get-tuple-element.41.residual_ref, ...), custom_call_target="tpu_custom_call" | custom-call | tf_op jit(solution)/shard_map/gradients/pallas_call | solution.py:31
  123.4 13.8 %all_to_all.40 = f32[32,16,128]{2,1,0:T(8,128)S(1)} all-to-all(f32[32,16,128]{2,1,0:T(8,128)S(1)} %get-tuple-element.44), channel_id=1, replica_groups=mesh['sub'=32,'load'=8] {'sub'}, dimensions={0} | all-to-all | bytes 524288 | tf_op jit(solution)/shard_map/all_to_all | solution.py:330
  137.3 5.6 %collective-permute-start.5 = (f32[16,128]{1,0:T(8,128)S(1)}, f32[16,128]{1,0:T(8,128)S(1)}, u32[]{:S(2)}, u32[]{:S(2)}) collective-permute-start(f32[16,128]{1,0:T(8,128)S(1)} %reduce_sum.9.middle_ref), channel_id=1, source_target_pairs={{1,0},{2,1},{3,2},{4,3},{5,4},{6,5},{7,6},{9,8},{10,9},{11,10},{12... | collective-permute-start | bytes 24584 | tf_op jit(solution)/shard_map/ppermute | solution.py:304
  142.9 2.1 %collective-permute-start.4 = (f32[16,128]{1,0:T(8,128)S(1)}, f32[16,128]{1,0:T(8,128)S(1)}, u32[]{:S(2)}, u32[]{:S(2)}) collective-permute-start(f32[16,128]{1,0:T(8,128)S(1)} %reduce_sum.9.middle_ref), channel_id=1, source_target_pairs={{0,1},{1,2},{2,3},{3,4},{4,5},{5,6},{6,7},{8,9},{9,10},{10,11},{11... | collective-permute-start | bytes 24584 | tf_op jit(solution)/shard_map/ppermute | solution.py:304
  (52 shorter events, 11.3 us)
Async XLA Ops:
  0.6 1.0 copy-start
  1.7 0.8 copy-start.13
  2.4 0.9 copy-start.16
  30.2 13.2 %all-to-all-start.1 = ((f32[8,16,128]{2,1,0:T(8,128)}), f32[8,16,128]{2,1,0:T(8,128)S(1)}, u32[]{:S(2)}, u32[]{:S(2)}) async-start(f32[8,16,128]{2,1,0:T(8,128)} %get-tuple-element.24), calls=%async_computation.1 | async-start | bytes 131072 | tf_op jit(solution)/shard_map/all_to_all | solution.py:330
  39.9 3.4 %copy-start.18 = (f32[128]{0:T(128)S(1)}, f32[128]{0:T(128)}, u32[]{:S(2)}) copy-start(f32[128]{0:T(128)} %param.16) | copy-start | bytes 1540
  41.7 1.0 copy-start.5
  43.4 1.0 copy-start.1
  44.4 1.6 %copy-start.3 = (bf16[1,1024,1024]{2,1,0:T(8,128)(2,1)S(1)}, bf16[1,1024,1024]{2,1,0:T(8,128)(2,1)}, u32[]{:S(2)}) copy-start(bf16[1,1024,1024]{2,1,0:T(8,128)(2,1)} %operator_ref.3) | copy-start | bytes 6291460
  46.0 1.2 copy-start.6
  47.2 6.4 %copy-start.2 = (f32[1,1024,128]{2,1,0:T(8,128)S(1)}, f32[1,1024,128]{2,1,0:T(8,128)}, u32[]{:S(2)}) copy-start(f32[1,1024,128]{2,1,0:T(8,128)} %rhs_ref.5) | copy-start | bytes 1572868
  47.2 6.4 %copy-start.15 = (bf16[1,12,1024]{2,1,0:T(8,128)(2,1)S(1)}, bf16[1,12,1024]{2,1,0:T(8,128)(2,1)}, u32[]{:S(2)}) copy-start(bf16[1,12,1024]{2,1,0:T(8,128)(2,1)} %basis_ref.7) | copy-start | bytes 73732
  48.8 2.4 %collective-permute-start = (bf16[256,128]{1,0:T(8,128)(2,1)S(1)}, bf16[256,128]{1,0:T(8,128)(2,1)S(1)}, u32[]{:S(2)}, u32[]{:S(2)}) collective-permute-start(bf16[256,128]{1,0:T(8,128)(2,1)S(1)} %get-tuple-element.31), channel_id=1, source_target_pairs={{0,1},{1,2},{2,3},{3,4},{4,5},{5,6},{6,7},{7,8},{8,9},{9,10},{10,1... | collective-permute-start | bytes 196616 | tf_op jit(solution)/shard_map/ppermute | solution.py:364
  49.9 3.7 %collective-permute-start.1 = (bf16[256,128]{1,0:T(8,128)(2,1)S(1)}, bf16[256,128]{1,0:T(8,128)(2,1)S(1)}, u32[]{:S(2)}, u32[]{:S(2)}) collective-permute-start(bf16[256,128]{1,0:T(8,128)(2,1)S(1)} %get-tuple-element.32), channel_id=1, source_target_pairs={{1,0},{2,1},{3,2},{4,3},{5,4},{6,5},{7,6},{8,7},{9,8},{10,9},{11,1... | collective-permute-start | bytes 196616 | tf_op jit(solution)/shard_map/ppermute | solution.py:365
  50.6 18.0 %copy-start.10 = (bf16[128,1024]{1,0:T(8,128)(2,1)S(1)}, bf16[128,1024]{1,0:T(8,128)(2,1)}, u32[]{:S(2)}) copy-start(bf16[128,1024]{1,0:T(8,128)(2,1)} %copy-done.9) | copy-start | bytes 786436
  50.6 33.6 %copy-start.4 = (bf16[1,1024,1024]{2,1,0:T(8,128)(2,1)S(1)}, bf16[1,1024,1024]{2,1,0:T(8,128)(2,1)}, u32[]{:S(2)}) copy-start(bf16[1,1024,1024]{2,1,0:T(8,128)(2,1)} %operator_ref.3) | copy-start | bytes 6291460
  50.6 33.6 %copy-start.7 = (bf16[512,1024]{1,0:T(8,128)(2,1)S(1)}, bf16[512,1024]{1,0:T(8,128)(2,1)}, u32[]{:S(2)}) copy-start(bf16[512,1024]{1,0:T(8,128)(2,1)} %copy-done.5) | copy-start | bytes 3145732
  85.8 2.4 %collective-permute-start.2 = (bf16[256,128]{1,0:T(8,128)(2,1)S(1)}, bf16[256,128]{1,0:T(8,128)(2,1)S(1)}, u32[]{:S(2)}, u32[]{:S(2)}) collective-permute-start(bf16[256,128]{1,0:T(8,128)(2,1)S(1)} %get-tuple-element.38), channel_id=1, source_target_pairs={{0,1},{1,2},{2,3},{3,4},{4,5},{5,6},{6,7},{7,8},{8,9},{9,10},{10,1... | collective-permute-start | bytes 196616 | tf_op jit(solution)/shard_map/ppermute | solution.py:364
  86.9 3.7 %collective-permute-start.3 = (bf16[256,128]{1,0:T(8,128)(2,1)S(1)}, bf16[256,128]{1,0:T(8,128)(2,1)S(1)}, u32[]{:S(2)}, u32[]{:S(2)}) collective-permute-start(bf16[256,128]{1,0:T(8,128)(2,1)S(1)} %get-tuple-element.39), channel_id=1, source_target_pairs={{1,0},{2,1},{3,2},{4,3},{5,4},{6,5},{7,6},{8,7},{9,8},{10,9},{11,1... | collective-permute-start | bytes 196616 | tf_op jit(solution)/shard_map/ppermute | solution.py:365
  87.6 33.6 %copy-start.8 = (bf16[1,1536,1024]{2,1,0:T(8,128)(2,1)S(1)}, bf16[1,1536,1024]{2,1,0:T(8,128)(2,1)}, u32[]{:S(2)}) copy-start(bf16[1,1536,1024]{2,1,0:T(8,128)(2,1)} %recovery_ref.1) | copy-start | bytes 9437188
  87.6 33.6 %copy-start.11 = (bf16[1,1536,128]{2,1,0:T(8,128)(2,1)S(1)}, bf16[1,1536,128]{2,1,0:T(8,128)(2,1)}, u32[]{:S(2)}) copy-start(bf16[1,1536,128]{2,1,0:T(8,128)(2,1)} %base_ref.1) | copy-start | bytes 1179652
  87.6 33.6 %copy-start.12 = (bf16[1,1536,128]{2,1,0:T(8,128)(2,1)S(1)}, bf16[1,1536,128]{2,1,0:T(8,128)(2,1)}, u32[]{:S(2)}) copy-start(bf16[1,1536,128]{2,1,0:T(8,128)(2,1)} %adjoint_ref.1) | copy-start | bytes 1179652
  87.6 33.6 %copy-start.19 = (s32[1,128]{1,0:T(1,128)S(1)}, s32[1,128]{1,0:T(1,128)}, u32[]{:S(2)}) copy-start(s32[1,128]{1,0:T(1,128)} %voxel_ref.1) | copy-start | bytes 1540
  137.3 7.7 %collective-permute-start.5 = (f32[16,128]{1,0:T(8,128)S(1)}, f32[16,128]{1,0:T(8,128)S(1)}, u32[]{:S(2)}, u32[]{:S(2)}) collective-permute-start(f32[16,128]{1,0:T(8,128)S(1)} %reduce_sum.9.middle_ref), channel_id=1, source_target_pairs={{1,0},{2,1},{3,2},{4,3},{5,4},{6,5},{7,6},{9,8},{10,9},{11,10},{12... | collective-permute-start | bytes 24584 | tf_op jit(solution)/shard_map/ppermute | solution.py:304
  142.9 3.1 %collective-permute-start.4 = (f32[16,128]{1,0:T(8,128)S(1)}, f32[16,128]{1,0:T(8,128)S(1)}, u32[]{:S(2)}, u32[]{:S(2)}) collective-permute-start(f32[16,128]{1,0:T(8,128)S(1)} %reduce_sum.9.middle_ref), channel_id=1, source_target_pairs={{0,1},{1,2},{2,3},{3,4},{4,5},{5,6},{6,7},{8,9},{9,10},{10,11},{11... | collective-permute-start | bytes 24584 | tf_op jit(solution)/shard_map/ppermute | solution.py:304
  (4 other events, 2.8 us)

commit v3 on v2

--- a/solution.py
+++ b/solution.py
@@ -17,6 +17,7 @@
 UNKNOWNS = 1536
 EDGE = 256
 MARK = 120
+FIRST = 16
 ENTRIES = SUB * LOAD * SPOTS
 GRID_ROWS = 256
 FIBRE_RATE = 0.3
@@ -27,12 +28,14 @@
 BF16 = jnp.bfloat16
 
 
-def call(kernel, outs, operands, name, flops=0, moved=0, limit=16, scratch=()):
+def call(kernel, outs, operands, name, flops=0, moved=16 * 2**20, limit=16, scratch=(), far=()):
+    vmem, hbm = pl.BlockSpec(memory_space=pltpu.VMEM), pl.BlockSpec(memory_space=pltpu.HBM)
     return pl.pallas_call(
         kernel,
+        in_specs=[hbm if place in far else vmem for place in range(len(operands))],
         out_shape=[jax.ShapeDtypeStruct(shape, dtype) for shape, dtype in outs],
         scratch_shapes=list(scratch),
-        compiler_params=pltpu.CompilerParams(vmem_limit_bytes=limit * 2**20),
+        compiler_params=pltpu.CompilerParams(vmem_limit_bytes=int(limit * 2**20)),
         cost_estimate=pl.CostEstimate(flops=flops, bytes_accessed=moved, transcendentals=0),
         name=name,
     )(*operands)
@@ -75,15 +78,37 @@
     return jnp.where(rows_of(terms.shape) == MODES, squares, terms)
 
 
-def first_terms(rhs_ref, basis_ref, inverse_ref, class_ref, out_ref):
-    rows = coarse_rows(basis_ref, rhs_ref[0])
-    classes = (class_ref[...] + 1).astype(F32)
-    row = rows_of(rows.shape)
-    rows = jnp.where(row == 13, classes[0:1], jnp.where(row == 14, classes[7:8], rows))
+def first_terms(
+    rhs_hbm,
+    basis_hbm,
+    inverse_hbm,
+    partner_hbm,
+    out_ref,
+    send_ref,
+    lifted_ref,
+    rhs_ref,
+    basis_ref,
+    inverse_ref,
+    partner_ref,
+    rhs_sem,
+    basis_sem,
+    inverse_sem,
+    partner_sem,
+):
+    copies = [
+        pltpu.make_async_copy(inverse_hbm, inverse_ref, inverse_sem),
+        pltpu.make_async_copy(basis_hbm, basis_ref, basis_sem),
+        pltpu.make_async_copy(rhs_hbm, rhs_ref, rhs_sem),
+        pltpu.make_async_copy(partner_hbm, partner_ref, partner_sem),
+    ]
+    for copy in copies:
+        copy.start()
+    copies[0].wait()
     inverse = inverse_ref[...]
     inverse = jnp.concatenate([inverse, inverse[:, :128]], axis=1)
     lanes = lanes_of((8, COLS))
     lane = lanes_of((1, COLS))
+    spares = []
     for peer in range(SUB):
         start = peer * LOAD * MODES
         tile, offset = start // 128, start % 128
@@ -97,8 +122,19 @@
         for place, turn in ((1, 96), (2, 0), (3, 32)):
             part = last[place : place + 1]
             spare = jnp.where(lane < 32 * place, spare, pltpu.roll(part, turn, axis=1) if turn else part)
-        out_ref[peer, :16, :] = jnp.where(row == 15, spare, rows)
         out_ref[peer, 16:, :] = jnp.where(lanes < 96, piece[:8], beside)
+        spares.append(spare)
+    copies[3].wait()
+    edge_rows(partner_ref[...].astype(F32), send_ref)
+    copies[1].wait()
+    basis = padded_basis(basis_ref, COLS).T
+    basis = basis + pltpu.roll(basis, 16, axis=1) + pltpu.roll(basis, 32, axis=1)
+    lifted_ref[...] = basis.astype(BF16)
+    copies[2].wait()
+    rows = coarse_rows(basis_ref, rhs_ref[0])
+    row = rows_of(rows.shape)
+    for peer in range(SUB):
+        out_ref[peer, :16, :] = jnp.where(row == 15, spares[peer], rows)
 
 
 def partial_rows(high, low, terms, out_ref):
@@ -109,7 +145,7 @@
         out_ref[peer] = jnp.concatenate([partial[MODES * peer : MODES * peer + MODES], last], axis=0)
 
 
-def first_partial(received_ref, class_ref, out_ref, block_ref, middle_ref):
+def first_partial(received_ref, out_ref, block_ref):
     terms = received_ref[:, :16, :].reshape(SUB * 16, COLS)
     packed = received_ref[:, 16:, :].reshape(SUB * 8, COLS)
     lanes = lanes_of((SUB * 8, COLS))
@@ -128,6 +164,15 @@
     block_ref[:, : SUB * 16] = high
     block_ref[:, SUB * 16 :] = low
     partial_rows(high, low, terms, out_ref)
+
+
+def later_partial(received_ref, block_ref, out_ref):
+    terms = received_ref[...].reshape(SUB * 16, COLS)
+    partial_rows(block_ref[:, : SUB * 16], block_ref[:, SUB * 16 :], terms, out_ref)
+
+
+def class_partial(received_ref, block_ref, class_ref, out_ref, middle_ref):
+    later_partial(received_ref, block_ref, out_ref)
     here = lax.axis_index("sub")
     above = received_ref[jnp.maximum(here - 1, 0)][14:15]
     below = received_ref[jnp.minimum(here + 1, SUB - 1)][13:14]
@@ -143,16 +188,7 @@
         out_ref[peer, 14:15, :] = sides[127:128]
 
 
-def later_partial(received_ref, block_ref, out_ref):
-    terms = received_ref[...].reshape(SUB * 16, COLS)
-    partial_rows(block_ref[:, : SUB * 16], block_ref[:, SUB * 16 :], terms, out_ref)
-
-
-def setup(partner_ref, basis_ref, send_ref, pick_ref, lifted_ref):
-    basis = padded_basis(basis_ref, COLS).T
-    basis = basis + pltpu.roll(basis, 16, axis=1) + pltpu.roll(basis, 32, axis=1)
-    lifted_ref[...] = basis.astype(BF16)
-    partners = partner_ref[...].astype(F32)
+def edge_rows(partners, send_ref):
     to_before = jnp.where(partners < SPOTS, 1.0, 0.0)
     to_after = jnp.where(partners >= 2 * SPOTS, 1.0, 0.0)
     sides = jnp.concatenate([to_before, to_after, jnp.zeros((14, SPOTS), F32)], axis=0)
@@ -162,6 +198,10 @@
     slots = rows_of((EDGE, SPOTS)).astype(F32)
     send_ref[:EDGE, :] = jnp.where(slots == place[0:1], 1.0, 0.0).astype(BF16)
     send_ref[EDGE:, :] = jnp.where(slots == place[1:2], 1.0, 0.0).astype(BF16)
+
+
+def first_inner(images_ref, partner_ref, out_ref, pick_ref):
+    partners = partner_ref[...].astype(F32)
     lanes = lanes_of((128, 128)).astype(F32)
     for block in range(SPOTS // 128):
         here = slice(128 * block, 128 * block + 128)
@@ -179,6 +219,7 @@
             else:
                 hit = rank == lanes + (start - EDGE - SPOTS + 3 * EDGE)
             pick_ref[here, start : start + 128] = jnp.where(hit, 1.0, 0.0).astype(BF16)
+    inner_pairs(images_ref, pick_ref, out_ref)
 
 
 def step_parts(received_ref, damping_ref, lifted_ref):
@@ -225,12 +266,17 @@
     inner_pairs(images_ref, pick_ref, out_ref)
 
 
-def residual_terms(rhs_ref, images_ref, inner_ref, pick_ref, before_ref, after_ref, basis_ref, residual_ref, out_ref):
+def residual_terms(
+    rhs_ref, images_ref, inner_ref, pick_ref, before_ref, after_ref, basis_ref, class_ref, residual_ref, out_ref
+):
     partners = inner_ref[...] + dot(pick_ref[:, :EDGE], before_ref[...])
     partners = partners + dot(pick_ref[:, EDGE + SPOTS :], after_ref[...])
     residual = rhs_ref[0] - (images_ref[...].astype(F32) + partners)
     residual_ref[...] = residual
     rows = coarse_rows(basis_ref, residual)
+    classes = (class_ref[...] + 1).astype(F32)
+    row = rows_of(rows.shape)
+    rows = jnp.where(row == 13, classes[0:1], jnp.where(row == 14, classes[7:8], rows))
     for peer in range(SUB):
         out_ref[peer] = rows
 
@@ -329,25 +375,26 @@
     def over(value, axis):
         return lax.all_to_all(value, axis, 0, 0, tiled=True)
 
-    (sent,) = call(
+    sent, send, lifted = call(
         first_terms,
-        [((SUB, 24, COLS), F32)],
-        (dual_rhs, coarse_basis, coarse_inverse, fibre_class),
+        [((SUB, 24, COLS), F32), ((2 * EDGE, SPOTS), BF16), ((SPOTS, COLS), BF16)],
+        (dual_rhs, coarse_basis, coarse_inverse, partner),
         "first_terms",
+        scratch=[
+            pltpu.VMEM(dual_rhs.shape, F32),
+            pltpu.VMEM(coarse_basis.shape, BF16),
+            pltpu.VMEM(coarse_inverse.shape, F32),
+            pltpu.VMEM(partner.shape, jnp.int32),
+        ]
+        + [pltpu.SemaphoreType.DMA] * 4,
+        far=(0, 1, 2, 3),
+        limit=FIRST,
     )
     received = over(sent, "sub")
-    send, pick, lifted = call(
-        setup,
-        [((2 * EDGE, SPOTS), BF16), ((SPOTS, SPOTS + 2 * EDGE), BF16), ((SPOTS, COLS), BF16)],
-        (partner, coarse_basis),
-        "setup",
-        flops=2 * SPOTS * SPOTS * 1024,
-        moved=16 * 2**20,
-    )
-    partial, block, middle = call(
+    partial, block = call(
         first_partial,
-        [to_load, ((COLS, 2 * SUB * 16), BF16), ((16, COLS), F32)],
-        (received, fibre_class),
+        [to_load, ((COLS, 2 * SUB * 16), BF16)],
+        (received,),
         "first_partial",
     )
     residual = dual_rhs
@@ -363,26 +410,29 @@
         before = (iterate,)
         from_before = lax.ppermute(upper, whole, up)
         from_after = lax.ppermute(lower, whole, down)
-        more = (received, middle) if iteration == 0 else ()
-        inner = call(
-            inner_pairs if iteration else inner_classes,
-            [tall] if iteration else [tall, ((16, 2 * COLS), F32)],
-            (images, pick) + more,
-            "inner_pairs",
-            flops=2 * SPOTS * SPOTS * 256,
-            moved=4 * 2**20,
-        )
         if iteration == 0:
-            classes = inner[1]
-        inner = inner[0]
+            inner, pick = call(
+                first_inner, [tall, ((SPOTS, SPOTS + 2 * EDGE), BF16)], (images, partner), "first_inner",
+                flops=2 * SPOTS * SPOTS * 1024, moved=8 * 2**20,
+            )
+        else:
+            inner, classes = call(
+                inner_classes, [tall, ((16, 2 * COLS), F32)], (images, pick, received, middle), "inner_classes",
+                flops=2 * SPOTS * SPOTS * 256, moved=4 * 2**20,
+            )
         residual, sent = call(
             residual_terms,
             [tall, to_sub],
-            (dual_rhs, images, inner, pick, from_before, from_after, coarse_basis),
+            (dual_rhs, images, inner, pick, from_before, from_after, coarse_basis, fibre_class),
             "residual_terms",
         )
         received = over(sent, "sub")
-        (partial,) = call(later_partial, [to_load], (received, block), "later_partial")
+        if iteration == 0:
+            partial, middle = call(
+                class_partial, [to_load, ((16, COLS), F32)], (received, block, fibre_class), "class_partial"
+            )
+        else:
+            (partial,) = call(later_partial, [to_load], (received, block), "later_partial")
     received = over(partial, "load")
     multipliers, sent = call(
         gradients,

time: 148 us -> 147 us (level)
  blocking collectives: 96.6 us -> 110 us
  starting transfers between devices: 18 us -> 9.71 us
  local copies, waits for them, and re-layouts: 10.4 us -> 6.74 us
  waiting for transfers between devices: 7.48 us -> 5.97 us
    all_to_all x6 -> x7, blocking collectives: 96.6 us -> 110 us  [over(): return lax.all_to_all(value, axis, 0, 0, tiled=True)]
    all_to_all x1 -> x0, starting transfers between devices: 8.3 us -> none  [over(): return lax.all_to_all(value, axis, 0, 0, tiled=True)]
    unnamed x42 -> x32, local copies, waits for them, and re-layouts: 10.4 us -> 6.74 us
    pallas_call x13 -> x12, Pallas kernels: 13.3 us -> 13.1 us  [call(): pl.pallas_call(kernel, in_specs=[hbm if place in far else vmem for place...]
  transfers between devices with their start and end apart: 7 -> 6, of which waited for: 6 -> 4; matrix products, arithmetic and copies ran while one was open for 0% -> 0% of each run, Pallas kernels for 2% -> 2%
where the time goes in v3:
time: 147 us; the launch traced here: 146 us
  blocking collectives  110 us (75%)
  Pallas kernels  13.1 us (9%)
  starting transfers between devices  9.71 us (7%)
  local copies, waits for them, and re-layouts  6.74 us (5%)
  waiting for transfers between devices  5.97 us (4%)
    all_to_all x7, blocking collectives, over(): return lax.all_to_all(value, axis, 0, 0, tiled=True)  110 us
    pallas_call x12, Pallas kernels, call(): pl.pallas_call(kernel, in_specs=[hbm if place in far else vmem for place...  13.1 us
    ppermute x2, starting transfers between devices, both_ways(): return (lax.ppermute(value, axes, up), lax.ppermute(value, axes, down))  7.65 us
    unnamed x32, local copies, waits for them, and re-layouts  6.74 us
    ppermute x2, waiting for transfers between devices, on_device(): from_after = lax.ppermute(lower, whole, down)  4.43 us
  transfers between devices with their start and end apart: 6, of which 4 were waited for; matrix products, arithmetic and copies ran while one was open for 0% of the time, Pallas kernels for 2%

profile of v3, /device:TPU:1, one launch (start us, length us, event | category | flops | bytes accessed | tf_op | source)
XLA Modules:
  0.0 145.9 jit_solution(4727708903970056581)
XLA Ops:
  0.6 1.0 copy-done.2
  2.4 0.9 copy-done.10
  4.0 2.3 %first_terms.1 = (f32[32,24,128]{2,1,0:T(8,128)S(1)}, bf16[512,1024]{1,0:T(8,128)(2,1)S(1)}, bf16[1024,128]{1,0:T(8,128)(2,1)S(1)}) custom-call(f32[1,1024,128]{2,1,0:T(8,128)S(1)} %copy-done.2, bf16[1,12,1024]{2,1,0:T(8,128)(2,1)S(1)} %copy-done.8, f32[12,3072]{1,0:T(8,128)S(1)} %copy-done.10, s32[1,1024]{1,0:T(1,128)S(1)} %copy-done.14), custom_call_target="tpu_custom_call" | custom-call | bytes 16777216 | tf_op jit(solution)/shard_map/first_terms/pallas_call | solution.py:33
  6.4 23.3 %all_to_all.35.received_ref = f32[32,24,128]{2,1,0:T(8,128)S(1)} all-to-all(f32[32,24,128]{2,1,0:T(8,128)S(1)} %get-tuple-element.27), channel_id=1, replica_groups=mesh['sub'=32,'load'=8] {'sub'}, dimensions={0} | all-to-all | bytes 786432 | tf_op jit(solution)/shard_map/all_to_all | solution.py:376
  30.2 13.0 %all_to_all.36.received_ref = f32[8,16,128]{2,1,0:T(8,128)S(1)} all-to-all(f32[8,16,128]{2,1,0:T(8,128)S(1)} %get-tuple-element.28), channel_id=1, replica_groups=mesh['sub'=32,'load'=8] {'load'}, dimensions={0} | all-to-all | bytes 131072 | tf_op jit(solution)/shard_map/all_to_all | solution.py:376
  43.1 1.6 %copy-done = bf16[1,1024,1024]{2,1,0:T(8,128)(2,1)S(1)} copy-done((bf16[1,1024,1024]{2,1,0:T(8,128)(2,1)S(1)}, bf16[1,1024,1024]{2,1,0:T(8,128)(2,1)}, u32[]{:S(2)}) %copy-start) | copy-done | bytes 2097176
  44.7 1.0 copy-done.3
  46.4 1.6 %advance.2 = (f32[1024,128]{1,0:T(8,128)S(1)}, bf16[1024,128]{1,0:T(8,128)(2,1)S(1)}, bf16[256,128]{1,0:T(8,128)(2,1)S(1)}, bf16[256,128]{1,0:T(8,128)(2,1)S(1)}) custom-call(f32[8,16,128]{2,1,0:T(8,128)S(1)} %all_to_all.36.received_ref, f32[1,128]{1,0:T(1,128)S(1)} %bitcast.1, bf16[1024,128]{1,0:T(8,128)(2,1)S(1)} %get-tuple-element.29.lifted_ref, ...), custom_call_target="tpu_custom_call" | custom-call | bytes 16777216 | tf_op jit(solution)/shard_map/advance/pallas_call | solution.py:33
  48.1 1.0 collective-permute-start
  49.1 1.6 %first_inner.1 = (f32[1024,128]{1,0:T(8,128)S(1)}, bf16[1024,1536]{1,0:T(8,128)(2,1)S(1)}) custom-call(bf16[1024,128]{1,0:T(8,128)(2,1)S(1)} %get-tuple-element.31.images_ref, s32[1,1024]{1,0:T(1,128)S(1)} %copy-done.14), custom_call_target="tpu_custom_call" | custom-call | flops 2147483648 | bytes 8388608 | tf_op jit(solution)/shard_map/first_inner/pallas_call | solution.py:33
  50.7 2.1 %collective-permute-done.1.after_ref = bf16[256,128]{1,0:T(8,128)(2,1)S(1)} collective-permute-done((bf16[256,128]{1,0:T(8,128)(2,1)S(1)}, bf16[256,128]{1,0:T(8,128)(2,1)S(1)}, u32[]{:S(2)}, u32[]{:S(2)}) %collective-permute-start.1) | collective-permute-done | bytes 65568 | tf_op jit(solution)/shard_map/ppermute | solution.py:412
  53.4 14.4 %all_to_all.37.received_ref = f32[32,16,128]{2,1,0:T(8,128)S(1)} all-to-all(f32[32,16,128]{2,1,0:T(8,128)S(1)} %get-tuple-element.36), channel_id=1, replica_groups=mesh['sub'=32,'load'=8] {'sub'}, dimensions={0} | all-to-all | bytes 524288 | tf_op jit(solution)/shard_map/all_to_all | solution.py:376
  68.1 15.3 %all_to_all.38.received_ref = f32[8,16,128]{2,1,0:T(8,128)S(1)} all-to-all(f32[8,16,128]{2,1,0:T(8,128)S(1)} %get-tuple-element.38), channel_id=1, replica_groups=mesh['sub'=32,'load'=8] {'load'}, dimensions={0} | all-to-all | bytes 131072 | tf_op jit(solution)/shard_map/all_to_all | solution.py:376
  83.4 1.6 %advance.3 = (f32[1024,128]{1,0:T(8,128)S(1)}, bf16[1024,128]{1,0:T(8,128)(2,1)S(1)}, bf16[256,128]{1,0:T(8,128)(2,1)S(1)}, bf16[256,128]{1,0:T(8,128)(2,1)S(1)}) custom-call(f32[8,16,128]{2,1,0:T(8,128)S(1)} %all_to_all.38.received_ref, f32[1,128]{1,0:T(1,128)S(1)} %bitcast.2, bf16[1024,128]{1,0:T(8,128)(2,1)S(1)} %get-tuple-element.29.lifted_ref, ...), custom_call_target="tpu_custom_call" | custom-call | bytes 16777216 | tf_op jit(solution)/shard_map/advance/pallas_call | solution.py:33
  85.0 1.0 collective-permute-start.2
  87.4 2.4 %collective-permute-done.3.after_ref = bf16[256,128]{1,0:T(8,128)(2,1)S(1)} collective-permute-done((bf16[256,128]{1,0:T(8,128)(2,1)S(1)}, bf16[256,128]{1,0:T(8,128)(2,1)S(1)}, u32[]{:S(2)}, u32[]{:S(2)}) %collective-permute-start.3) | collective-permute-done | bytes 65568 | tf_op jit(solution)/shard_map/ppermute | solution.py:412
  90.4 13.9 %all_to_all.39.received_ref = f32[32,16,128]{2,1,0:T(8,128)S(1)} all-to-all(f32[32,16,128]{2,1,0:T(8,128)S(1)} %get-tuple-element.46), channel_id=1, replica_groups=mesh['sub'=32,'load'=8] {'sub'}, dimensions={0} | all-to-all | bytes 524288 | tf_op jit(solution)/shard_map/all_to_all | solution.py:376
  104.5 15.9 %all_to_all.40.received_ref = f32[8,16,128]{2,1,0:T(8,128)S(1)} all-to-all(f32[8,16,128]{2,1,0:T(8,128)S(1)} %later_partial.1), channel_id=1, replica_groups=mesh['sub'=32,'load'=8] {'load'}, dimensions={0} | all-to-all | bytes 131072 | tf_op jit(solution)/shard_map/all_to_all | solution.py:376
  120.4 2.2 %gradients.1 = (f32[1,1024,128]{2,1,0:T(8,128)}, f32[32,16,128]{2,1,0:T(8,128)S(1)}) custom-call(f32[8,16,128]{2,1,0:T(8,128)S(1)} %all_to_all.40.received_ref, f32[1,128]{1,0:T(1,128)S(1)} %bitcast.3, bf16[1024,128]{1,0:T(8,128)(2,1)S(1)} %get-tuple-element.29.lifted_ref, f32[1024,128]{1,0:T(8,128)S(1)} %get-tuple-element.47.residual_ref, ...), custom_call_target="tpu_custom_call" | custom-call | bytes 16777216 | tf_op jit(solution)/shard_map/gradients/pallas_call | solution.py:33
  122.6 13.8 %all_to_all.41 = f32[32,16,128]{2,1,0:T(8,128)S(1)} all-to-all(f32[32,16,128]{2,1,0:T(8,128)S(1)} %get-tuple-element.50), channel_id=1, replica_groups=mesh['sub'=32,'load'=8] {'sub'}, dimensions={0} | all-to-all | bytes 524288 | tf_op jit(solution)/shard_map/all_to_all | solution.py:376
  136.5 5.6 %collective-permute-start.5 = (f32[16,128]{1,0:T(8,128)S(1)}, f32[16,128]{1,0:T(8,128)S(1)}, u32[]{:S(2)}, u32[]{:S(2)}) collective-permute-start(f32[16,128]{1,0:T(8,128)S(1)} %reduce_sum.9.middle_ref), channel_id=1, source_target_pairs={{1,0},{2,1},{3,2},{4,3},{5,4},{6,5},{7,6},{9,8},{10,9},{11,10},{12... | collective-permute-start | bytes 24584 | tf_op jit(solution)/shard_map/ppermute | solution.py:350
  142.1 2.1 %collective-permute-start.4 = (f32[16,128]{1,0:T(8,128)S(1)}, f32[16,128]{1,0:T(8,128)S(1)}, u32[]{:S(2)}, u32[]{:S(2)}) collective-permute-start(f32[16,128]{1,0:T(8,128)S(1)} %reduce_sum.9.middle_ref), channel_id=1, source_target_pairs={{0,1},{1,2},{2,3},{3,4},{4,5},{5,6},{6,7},{8,9},{9,10},{10,11},{11... | collective-permute-start | bytes 24584 | tf_op jit(solution)/shard_map/ppermute | solution.py:350
  144.2 1.0 collective-permute-done.4.left_ref
  145.2 0.8 smooth.1
  (40 shorter events, 5.7 us)
Async XLA Ops:
  0.6 1.0 copy-start.2
  1.7 0.8 copy-start.8
  2.4 0.9 copy-start.10
  3.4 0.7 copy-start.14
  43.1 1.6 %copy-start = (bf16[1,1024,1024]{2,1,0:T(8,128)(2,1)S(1)}, bf16[1,1024,1024]{2,1,0:T(8,128)(2,1)}, u32[]{:S(2)}) copy-start(bf16[1,1024,1024]{2,1,0:T(8,128)(2,1)} %operator_ref.3) | copy-start | bytes 6291460
  44.7 1.0 copy-start.3
  45.8 0.7 copy-start.12
  48.1 2.6 %collective-permute-start = (bf16[256,128]{1,0:T(8,128)(2,1)S(1)}, bf16[256,128]{1,0:T(8,128)(2,1)S(1)}, u32[]{:S(2)}, u32[]{:S(2)}) collective-permute-start(bf16[256,128]{1,0:T(8,128)(2,1)S(1)} %get-tuple-element.34), channel_id=1, source_target_pairs={{0,1},{1,2},{2,3},{3,4},{4,5},{5,6},{6,7},{7,8},{8,9},{9,10},{10,1... | collective-permute-start | bytes 196616 | tf_op jit(solution)/shard_map/ppermute | solution.py:411
  49.1 3.7 %collective-permute-start.1 = (bf16[256,128]{1,0:T(8,128)(2,1)S(1)}, bf16[256,128]{1,0:T(8,128)(2,1)S(1)}, u32[]{:S(2)}, u32[]{:S(2)}) collective-permute-start(bf16[256,128]{1,0:T(8,128)(2,1)S(1)} %get-tuple-element.35), channel_id=1, source_target_pairs={{1,0},{2,1},{3,2},{4,3},{5,4},{6,5},{7,6},{8,7},{9,8},{10,9},{11,1... | collective-permute-start | bytes 196616 | tf_op jit(solution)/shard_map/ppermute | solution.py:412
  49.1 3.7 %copy-start.4 = (f32[1,1024,128]{2,1,0:T(8,128)S(1)}, f32[1,1024,128]{2,1,0:T(8,128)}, u32[]{:S(2)}) copy-start(f32[1,1024,128]{2,1,0:T(8,128)} %rhs_ref.3) | copy-start | bytes 1572868
  49.1 3.7 %copy-start.11 = (s32[8,128]{1,0:T(8,128)S(1)}, s32[8,128]{1,0:T(8,128)}, u32[]{:S(2)}) copy-start(s32[8,128]{1,0:T(8,128)} %class_ref.5) | copy-start | bytes 12292
  50.7 32.8 %copy-start.1 = (bf16[1,1024,1024]{2,1,0:T(8,128)(2,1)S(1)}, bf16[1,1024,1024]{2,1,0:T(8,128)(2,1)}, u32[]{:S(2)}) copy-start(bf16[1,1024,1024]{2,1,0:T(8,128)(2,1)} %operator_ref.3) | copy-start | bytes 6291460
  50.7 32.7 %copy-start.13 = (f32[128]{0:T(128)S(1)}, f32[128]{0:T(128)}, u32[]{:S(2)}) copy-start(f32[128]{0:T(128)} %param.16) | copy-start | bytes 1540
  83.4 6.3 %copy-start.9 = (bf16[1,12,1024]{2,1,0:T(8,128)(2,1)S(1)}, bf16[1,12,1024]{2,1,0:T(8,128)(2,1)}, u32[]{:S(2)}) copy-start(bf16[1,12,1024]{2,1,0:T(8,128)(2,1)} %basis_ref.3) | copy-start | bytes 73732
  85.0 2.4 %collective-permute-start.2 = (bf16[256,128]{1,0:T(8,128)(2,1)S(1)}, bf16[256,128]{1,0:T(8,128)(2,1)S(1)}, u32[]{:S(2)}, u32[]{:S(2)}) collective-permute-start(bf16[256,128]{1,0:T(8,128)(2,1)S(1)} %get-tuple-element.44), channel_id=1, source_target_pairs={{0,1},{1,2},{2,3},{3,4},{4,5},{5,6},{6,7},{7,8},{8,9},{9,10},{10,1... | collective-permute-start | bytes 196616 | tf_op jit(solution)/shard_map/ppermute | solution.py:411
  86.1 3.7 %collective-permute-start.3 = (bf16[256,128]{1,0:T(8,128)(2,1)S(1)}, bf16[256,128]{1,0:T(8,128)(2,1)S(1)}, u32[]{:S(2)}, u32[]{:S(2)}) collective-permute-start(bf16[256,128]{1,0:T(8,128)(2,1)S(1)} %get-tuple-element.45), channel_id=1, source_target_pairs={{1,0},{2,1},{3,2},{4,3},{5,4},{6,5},{7,6},{8,7},{9,8},{10,9},{11,1... | collective-permute-start | bytes 196616 | tf_op jit(solution)/shard_map/ppermute | solution.py:412
  86.8 33.6 %copy-start.5 = (bf16[1,1536,1024]{2,1,0:T(8,128)(2,1)S(1)}, bf16[1,1536,1024]{2,1,0:T(8,128)(2,1)}, u32[]{:S(2)}) copy-start(bf16[1,1536,1024]{2,1,0:T(8,128)(2,1)} %recovery_ref.1) | copy-start | bytes 9437188
  86.8 33.6 %copy-start.6 = (bf16[1,1536,128]{2,1,0:T(8,128)(2,1)S(1)}, bf16[1,1536,128]{2,1,0:T(8,128)(2,1)}, u32[]{:S(2)}) copy-start(bf16[1,1536,128]{2,1,0:T(8,128)(2,1)} %base_ref.1) | copy-start | bytes 1179652
  86.8 33.6 %copy-start.7 = (bf16[1,1536,128]{2,1,0:T(8,128)(2,1)S(1)}, bf16[1,1536,128]{2,1,0:T(8,128)(2,1)}, u32[]{:S(2)}) copy-start(bf16[1,1536,128]{2,1,0:T(8,128)(2,1)} %adjoint_ref.1) | copy-start | bytes 1179652
  86.8 33.6 %copy-start.15 = (s32[1,128]{1,0:T(1,128)S(1)}, s32[1,128]{1,0:T(1,128)}, u32[]{:S(2)}) copy-start(s32[1,128]{1,0:T(1,128)} %voxel_ref.1) | copy-start | bytes 1540
  136.5 7.7 %collective-permute-start.5 = (f32[16,128]{1,0:T(8,128)S(1)}, f32[16,128]{1,0:T(8,128)S(1)}, u32[]{:S(2)}, u32[]{:S(2)}) collective-permute-start(f32[16,128]{1,0:T(8,128)S(1)} %reduce_sum.9.middle_ref), channel_id=1, source_target_pairs={{1,0},{2,1},{3,2},{4,3},{5,4},{6,5},{7,6},{9,8},{10,9},{11,10},{12... | collective-permute-start | bytes 24584 | tf_op jit(solution)/shard_map/ppermute | solution.py:350
  142.1 3.1 %collective-permute-start.4 = (f32[16,128]{1,0:T(8,128)S(1)}, f32[16,128]{1,0:T(8,128)S(1)}, u32[]{:S(2)}, u32[]{:S(2)}) collective-permute-start(f32[16,128]{1,0:T(8,128)S(1)} %reduce_sum.9.middle_ref), channel_id=1, source_target_pairs={{0,1},{1,2},{2,3},{3,4},{4,5},{5,6},{6,7},{8,9},{9,10},{10,11},{11... | collective-permute-start | bytes 24584 | tf_op jit(solution)/shard_map/ppermute | solution.py:350

commit v4 on v3

--- a/solution.py
+++ b/solution.py
@@ -17,7 +17,8 @@
 UNKNOWNS = 1536
 EDGE = 256
 MARK = 120
-FIRST = 16
+FIRST = 60
+PART = 40
 ENTRIES = SUB * LOAD * SPOTS
 GRID_ROWS = 256
 FIBRE_RATE = 0.3
@@ -145,7 +146,15 @@
         out_ref[peer] = jnp.concatenate([partial[MODES * peer : MODES * peer + MODES], last], axis=0)
 
 
-def first_partial(received_ref, out_ref, block_ref):
+def first_partial(
+    received_ref, operator_hbm, rhs_hbm, out_ref, block_ref, operator_ref, rhs_ref, operator_sem, rhs_sem
+):
+    copies = [
+        pltpu.make_async_copy(operator_hbm, operator_ref, operator_sem),
+        pltpu.make_async_copy(rhs_hbm, rhs_ref, rhs_sem),
+    ]
+    for copy in copies:
+        copy.start()
     terms = received_ref[:, :16, :].reshape(SUB * 16, COLS)
     packed = received_ref[:, 16:, :].reshape(SUB * 8, COLS)
     lanes = lanes_of((SUB * 8, COLS))
@@ -164,6 +173,8 @@
     block_ref[:, : SUB * 16] = high
     block_ref[:, SUB * 16 :] = low
     partial_rows(high, low, terms, out_ref)
+    for copy in copies:
+        copy.wait()
 
 
 def later_partial(received_ref, block_ref, out_ref):
@@ -391,20 +402,22 @@
         limit=FIRST,
     )
     received = over(sent, "sub")
-    partial, block = call(
+    partial, block, operator, residual = call(
         first_partial,
-        [to_load, ((COLS, 2 * SUB * 16), BF16)],
-        (received,),
+        [to_load, ((COLS, 2 * SUB * 16), BF16), (dual_ops.shape, BF16), (dual_rhs.shape, F32)],
+        (received, dual_ops, dual_rhs),
         "first_partial",
-    )
-    residual = dual_rhs
+        scratch=[pltpu.SemaphoreType.DMA] * 2,
+        far=(1, 2),
+        limit=PART,
+    )
     before = ()
     for iteration in range(2):
         received = over(partial, "load")
         iterate, images, lower, upper = call(
             functools.partial(advance, iteration == 0),
             [tall, ((SPOTS, COLS), BF16), edge, edge],
-            (received, damping, lifted, dual_ops, send, residual) + before,
+            (received, damping, lifted, (operator, dual_ops)[iteration], send, residual) + before,
             "advance",
         )
         before = (iterate,)

time: 147 us -> 145 us (0.986)
  local copies, waits for them, and re-layouts: 6.74 us -> 2.68 us
  Pallas kernels: 13.1 us -> 14.8 us
    unnamed x32 -> x24, local copies, waits for them, and re-layouts: 6.74 us -> 2.68 us
    pallas_call x12, Pallas kernels: 13.1 us -> 14.8 us  [call(): pl.pallas_call(kernel, in_specs=[hbm if place in far else vmem for place...]
where the time goes in v4:
time: 145 us; the launch traced here: 144 us
  blocking collectives  110 us (76%)
  Pallas kernels  14.8 us (10%)
  starting transfers between devices  9.71 us (7%)
  waiting for transfers between devices  5.98 us (4%)
  local copies, waits for them, and re-layouts  2.68 us (2%)
    all_to_all x7, blocking collectives, over(): return lax.all_to_all(value, axis, 0, 0, tiled=True)  110 us
    pallas_call x12, Pallas kernels, call(): pl.pallas_call(kernel, in_specs=[hbm if place in far else vmem for place...  14.8 us
    ppermute x2, starting transfers between devices, both_ways(): return (lax.ppermute(value, axes, up), lax.ppermute(value, axes, down))  7.66 us
    ppermute x2, waiting for transfers between devices, on_device(): from_after = lax.ppermute(lower, whole, down)  4.45 us
  transfers between devices with their start and end apart: 6, of which 4 were waited for; matrix products, arithmetic and copies ran while one was open for 0% of the time, Pallas kernels for 2%

profile of v4, /device:TPU:1, one launch (start us, length us, event | category | flops | bytes accessed | tf_op | source)
XLA Modules:
  0.0 144.0 jit_solution(7742188236550697188)
XLA Ops:
  0.6 3.9 %first_terms.1 = (f32[32,24,128]{2,1,0:T(8,128)}, bf16[512,1024]{1,0:T(8,128)(2,1)}, bf16[1024,128]{1,0:T(8,128)(2,1)}) custom-call(f32[1,1024,128]{2,1,0:T(8,128)} %rhs_ref.3, bf16[1,12,1024]{2,1,0:T(8,128)(2,1)} %basis_ref.3, f32[12,3072]{1,0:T(8,128)} %inverse_hbm.1, s32[1,1024]{1,0:T(1,128)} %partner_ref.1), custom_call_target="tpu_custom_call" | custom-call | bytes 16777216 | tf_op jit(solution)/shard_map/first_terms/pallas_call | solution.py:34
  4.5 23.7 %all_to_all.35.received_ref = f32[32,24,128]{2,1,0:T(8,128)S(1)} all-to-all(f32[32,24,128]{2,1,0:T(8,128)} %get-tuple-element.29), channel_id=1, replica_groups=mesh['sub'=32,'load'=8] {'sub'}, dimensions={0} | all-to-all | bytes 786432 | tf_op jit(solution)/shard_map/all_to_all | solution.py:387
  28.2 1.6 %copy-done = bf16[1,1024,1024]{2,1,0:T(8,128)(2,1)S(1)} copy-done((bf16[1,1024,1024]{2,1,0:T(8,128)(2,1)S(1)}, bf16[1,1024,1024]{2,1,0:T(8,128)(2,1)}, u32[]{:S(2)}) %copy-start) | copy-done | bytes 2097176
  29.8 1.0 copy-done.1
  30.8 0.7 first_partial.1
  31.5 12.9 %all_to_all.36.received_ref = f32[8,16,128]{2,1,0:T(8,128)S(1)} all-to-all(f32[8,16,128]{2,1,0:T(8,128)S(1)} %get-tuple-element.30), channel_id=1, replica_groups=mesh['sub'=32,'load'=8] {'load'}, dimensions={0} | all-to-all | bytes 131072 | tf_op jit(solution)/shard_map/all_to_all | solution.py:387
  44.5 1.6 %advance.2 = (f32[1024,128]{1,0:T(8,128)S(1)}, bf16[1024,128]{1,0:T(8,128)(2,1)S(1)}, bf16[256,128]{1,0:T(8,128)(2,1)S(1)}, bf16[256,128]{1,0:T(8,128)(2,1)S(1)}) custom-call(f32[8,16,128]{2,1,0:T(8,128)S(1)} %all_to_all.36.received_ref, f32[1,128]{1,0:T(1,128)S(1)} %bitcast.1, bf16[1024,128]{1,0:T(8,128)(2,1)S(1)} %copy-done.4, ...), custom_call_target="tpu_custom_call" | custom-call | bytes 16777216 | tf_op jit(solution)/shard_map/advance/pallas_call | solution.py:34
  46.1 1.0 collective-permute-start
  47.1 1.6 %first_inner.1 = (f32[1024,128]{1,0:T(8,128)S(1)}, bf16[1024,1536]{1,0:T(8,128)(2,1)S(1)}) custom-call(bf16[1024,128]{1,0:T(8,128)(2,1)S(1)} %get-tuple-element.35.images_ref, s32[1,1024]{1,0:T(1,128)S(1)} %copy-done.10), custom_call_target="tpu_custom_call" | custom-call | flops 2147483648 | bytes 8388608 | tf_op jit(solution)/shard_map/first_inner/pallas_call | solution.py:34
  48.7 2.1 %collective-permute-done.1.after_ref = bf16[256,128]{1,0:T(8,128)(2,1)S(1)} collective-permute-done((bf16[256,128]{1,0:T(8,128)(2,1)S(1)}, bf16[256,128]{1,0:T(8,128)(2,1)S(1)}, u32[]{:S(2)}, u32[]{:S(2)}) %collective-permute-start.1) | collective-permute-done | bytes 65568 | tf_op jit(solution)/shard_map/ppermute | solution.py:425
  51.4 14.4 %all_to_all.37.received_ref = f32[32,16,128]{2,1,0:T(8,128)S(1)} all-to-all(f32[32,16,128]{2,1,0:T(8,128)S(1)} %get-tuple-element.40), channel_id=1, replica_groups=mesh['sub'=32,'load'=8] {'sub'}, dimensions={0} | all-to-all | bytes 524288 | tf_op jit(solution)/shard_map/all_to_all | solution.py:387
  66.1 15.3 %all_to_all.38.received_ref = f32[8,16,128]{2,1,0:T(8,128)S(1)} all-to-all(f32[8,16,128]{2,1,0:T(8,128)S(1)} %get-tuple-element.42), channel_id=1, replica_groups=mesh['sub'=32,'load'=8] {'load'}, dimensions={0} | all-to-all | bytes 131072 | tf_op jit(solution)/shard_map/all_to_all | solution.py:387
  81.4 1.6 %advance.3 = (f32[1024,128]{1,0:T(8,128)S(1)}, bf16[1024,128]{1,0:T(8,128)(2,1)S(1)}, bf16[256,128]{1,0:T(8,128)(2,1)S(1)}, bf16[256,128]{1,0:T(8,128)(2,1)S(1)}) custom-call(f32[8,16,128]{2,1,0:T(8,128)S(1)} %all_to_all.38.received_ref, f32[1,128]{1,0:T(1,128)S(1)} %bitcast.2, bf16[1024,128]{1,0:T(8,128)(2,1)S(1)} %copy-done.4, ...), custom_call_target="tpu_custom_call" | custom-call | bytes 16777216 | tf_op jit(solution)/shard_map/advance/pallas_call | solution.py:34
  83.1 1.0 collective-permute-start.2
  84.1 0.7 inner_classes.1
  85.4 2.4 %collective-permute-done.3.after_ref = bf16[256,128]{1,0:T(8,128)(2,1)S(1)} collective-permute-done((bf16[256,128]{1,0:T(8,128)(2,1)S(1)}, bf16[256,128]{1,0:T(8,128)(2,1)S(1)}, u32[]{:S(2)}, u32[]{:S(2)}) %collective-permute-start.3) | collective-permute-done | bytes 65568 | tf_op jit(solution)/shard_map/ppermute | solution.py:425
  88.4 13.9 %all_to_all.39.received_ref = f32[32,16,128]{2,1,0:T(8,128)S(1)} all-to-all(f32[32,16,128]{2,1,0:T(8,128)S(1)} %get-tuple-element.50), channel_id=1, replica_groups=mesh['sub'=32,'load'=8] {'sub'}, dimensions={0} | all-to-all | bytes 524288 | tf_op jit(solution)/shard_map/all_to_all | solution.py:387
  102.5 15.9 %all_to_all.40.received_ref = f32[8,16,128]{2,1,0:T(8,128)S(1)} all-to-all(f32[8,16,128]{2,1,0:T(8,128)S(1)} %later_partial.1), channel_id=1, replica_groups=mesh['sub'=32,'load'=8] {'load'}, dimensions={0} | all-to-all | bytes 131072 | tf_op jit(solution)/shard_map/all_to_all | solution.py:387
  118.4 2.2 %gradients.1 = (f32[1,1024,128]{2,1,0:T(8,128)}, f32[32,16,128]{2,1,0:T(8,128)S(1)}) custom-call(f32[8,16,128]{2,1,0:T(8,128)S(1)} %all_to_all.40.received_ref, f32[1,128]{1,0:T(1,128)S(1)} %bitcast.3, bf16[1024,128]{1,0:T(8,128)(2,1)S(1)} %copy-done.4, f32[1024,128]{1,0:T(8,128)S(1)} %get-tuple-element.51.residual_ref, ...), custom_call_target="tpu_custom_call" | custom-call | bytes 16777216 | tf_op jit(solution)/shard_map/gradients/pallas_call | solution.py:34
  120.7 13.8 %all_to_all.41 = f32[32,16,128]{2,1,0:T(8,128)S(1)} all-to-all(f32[32,16,128]{2,1,0:T(8,128)S(1)} %get-tuple-element.54), channel_id=1, replica_groups=mesh['sub'=32,'load'=8] {'sub'}, dimensions={0} | all-to-all | bytes 524288 | tf_op jit(solution)/shard_map/all_to_all | solution.py:387
  134.5 5.6 %collective-permute-start.5 = (f32[16,128]{1,0:T(8,128)S(1)}, f32[16,128]{1,0:T(8,128)S(1)}, u32[]{:S(2)}, u32[]{:S(2)}) collective-permute-start(f32[16,128]{1,0:T(8,128)S(1)} %reduce_sum.9.middle_ref), channel_id=1, source_target_pairs={{1,0},{2,1},{3,2},{4,3},{5,4},{6,5},{7,6},{9,8},{10,9},{11,10},{12... | collective-permute-start | bytes 24584 | tf_op jit(solution)/shard_map/ppermute | solution.py:361
  140.1 2.1 %collective-permute-start.4 = (f32[16,128]{1,0:T(8,128)S(1)}, f32[16,128]{1,0:T(8,128)S(1)}, u32[]{:S(2)}, u32[]{:S(2)}) collective-permute-start(f32[16,128]{1,0:T(8,128)S(1)} %reduce_sum.9.middle_ref), channel_id=1, source_target_pairs={{0,1},{1,2},{2,3},{3,4},{4,5},{5,6},{6,7},{8,9},{9,10},{10,11},{11... | collective-permute-start | bytes 24584 | tf_op jit(solution)/shard_map/ppermute | solution.py:361
  142.2 1.0 collective-permute-done.4.left_ref
  143.2 0.8 smooth.1
  (32 shorter events, 2.4 us)
Async XLA Ops:
  0.6 43.8 %copy-start.9 = (f32[128]{0:T(128)S(1)}, f32[128]{0:T(128)}, u32[]{:S(2)}) copy-start(f32[128]{0:T(128)} %param.16) | copy-start | bytes 1540
  4.5 39.9 %copy-start.4 = (bf16[1024,128]{1,0:T(8,128)(2,1)S(1)}, bf16[1024,128]{1,0:T(8,128)(2,1)}, u32[]{:S(2)}) copy-start(bf16[1024,128]{1,0:T(8,128)(2,1)} %get-tuple-element.31.lifted_ref) | copy-start | bytes 786436
  28.2 1.6 %copy-start = (bf16[1,1024,1024]{2,1,0:T(8,128)(2,1)S(1)}, bf16[1,1024,1024]{2,1,0:T(8,128)(2,1)}, u32[]{:S(2)}) copy-start(bf16[1,1024,1024]{2,1,0:T(8,128)(2,1)} %operator_ref.1) | copy-start | bytes 6291460
  29.8 1.0 copy-start.1
  30.8 13.6 %copy-start.2 = (bf16[512,1024]{1,0:T(8,128)(2,1)S(1)}, bf16[512,1024]{1,0:T(8,128)(2,1)}, u32[]{:S(2)}) copy-start(bf16[512,1024]{1,0:T(8,128)(2,1)} %get-tuple-element.33.send_ref) | copy-start | bytes 3145732
  30.8 16.3 %copy-start.10 = (s32[1,1024]{1,0:T(1,128)S(1)}, s32[1,1024]{1,0:T(1,128)}, u32[]{:S(2)}) copy-start(s32[1,1024]{1,0:T(1,128)} %partner_ref.1) | copy-start | bytes 12292
  46.1 2.6 %collective-permute-start = (bf16[256,128]{1,0:T(8,128)(2,1)S(1)}, bf16[256,128]{1,0:T(8,128)(2,1)S(1)}, u32[]{:S(2)}, u32[]{:S(2)}) collective-permute-start(bf16[256,128]{1,0:T(8,128)(2,1)S(1)} %get-tuple-element.38), channel_id=1, source_target_pairs={{0,1},{1,2},{2,3},{3,4},{4,5},{5,6},{6,7},{7,8},{8,9},{9,10},{10,1... | collective-permute-start | bytes 196616 | tf_op jit(solution)/shard_map/ppermute | solution.py:424
  47.1 3.7 %collective-permute-start.1 = (bf16[256,128]{1,0:T(8,128)(2,1)S(1)}, bf16[256,128]{1,0:T(8,128)(2,1)S(1)}, u32[]{:S(2)}, u32[]{:S(2)}) collective-permute-start(bf16[256,128]{1,0:T(8,128)(2,1)S(1)} %get-tuple-element.39), channel_id=1, source_target_pairs={{1,0},{2,1},{3,2},{4,3},{5,4},{6,5},{7,6},{8,7},{9,8},{10,9},{11,1... | collective-permute-start | bytes 196616 | tf_op jit(solution)/shard_map/ppermute | solution.py:425
  47.1 3.7 %copy-start.7 = (bf16[1,12,1024]{2,1,0:T(8,128)(2,1)S(1)}, bf16[1,12,1024]{2,1,0:T(8,128)(2,1)}, u32[]{:S(2)}) copy-start(bf16[1,12,1024]{2,1,0:T(8,128)(2,1)} %basis_ref.3) | copy-start | bytes 73732
  47.1 3.7 %copy-start.8 = (s32[8,128]{1,0:T(8,128)S(1)}, s32[8,128]{1,0:T(8,128)}, u32[]{:S(2)}) copy-start(s32[8,128]{1,0:T(8,128)} %class_ref.5) | copy-start | bytes 12292
  83.1 2.4 %collective-permute-start.2 = (bf16[256,128]{1,0:T(8,128)(2,1)S(1)}, bf16[256,128]{1,0:T(8,128)(2,1)S(1)}, u32[]{:S(2)}, u32[]{:S(2)}) collective-permute-start(bf16[256,128]{1,0:T(8,128)(2,1)S(1)} %get-tuple-element.48), channel_id=1, source_target_pairs={{0,1},{1,2},{2,3},{3,4},{4,5},{5,6},{6,7},{7,8},{8,9},{9,10},{10,1... | collective-permute-start | bytes 196616 | tf_op jit(solution)/shard_map/ppermute | solution.py:424
  84.1 3.7 %collective-permute-start.3 = (bf16[256,128]{1,0:T(8,128)(2,1)S(1)}, bf16[256,128]{1,0:T(8,128)(2,1)S(1)}, u32[]{:S(2)}, u32[]{:S(2)}) collective-permute-start(bf16[256,128]{1,0:T(8,128)(2,1)S(1)} %get-tuple-element.49), channel_id=1, source_target_pairs={{1,0},{2,1},{3,2},{4,3},{5,4},{6,5},{7,6},{8,7},{9,8},{10,9},{11,1... | collective-permute-start | bytes 196616 | tf_op jit(solution)/shard_map/ppermute | solution.py:425
  84.8 33.6 %copy-start.3 = (bf16[1,1536,1024]{2,1,0:T(8,128)(2,1)S(1)}, bf16[1,1536,1024]{2,1,0:T(8,128)(2,1)}, u32[]{:S(2)}) copy-start(bf16[1,1536,1024]{2,1,0:T(8,128)(2,1)} %recovery_ref.1) | copy-start | bytes 9437188
  84.8 33.6 %copy-start.5 = (bf16[1,1536,128]{2,1,0:T(8,128)(2,1)S(1)}, bf16[1,1536,128]{2,1,0:T(8,128)(2,1)}, u32[]{:S(2)}) copy-start(bf16[1,1536,128]{2,1,0:T(8,128)(2,1)} %base_ref.1) | copy-start | bytes 1179652
  84.8 33.6 %copy-start.6 = (bf16[1,1536,128]{2,1,0:T(8,128)(2,1)S(1)}, bf16[1,1536,128]{2,1,0:T(8,128)(2,1)}, u32[]{:S(2)}) copy-start(bf16[1,1536,128]{2,1,0:T(8,128)(2,1)} %adjoint_ref.1) | copy-start | bytes 1179652
  84.8 33.6 %copy-start.11 = (s32[1,128]{1,0:T(1,128)S(1)}, s32[1,128]{1,0:T(1,128)}, u32[]{:S(2)}) copy-start(s32[1,128]{1,0:T(1,128)} %voxel_ref.1) | copy-start | bytes 1540
  134.5 7.7 %collective-permute-start.5 = (f32[16,128]{1,0:T(8,128)S(1)}, f32[16,128]{1,0:T(8,128)S(1)}, u32[]{:S(2)}, u32[]{:S(2)}) collective-permute-start(f32[16,128]{1,0:T(8,128)S(1)} %reduce_sum.9.middle_ref), channel_id=1, source_target_pairs={{1,0},{2,1},{3,2},{4,3},{5,4},{6,5},{7,6},{9,8},{10,9},{11,10},{12... | collective-permute-start | bytes 24584 | tf_op jit(solution)/shard_map/ppermute | solution.py:361
  140.1 3.1 %collective-permute-start.4 = (f32[16,128]{1,0:T(8,128)S(1)}, f32[16,128]{1,0:T(8,128)S(1)}, u32[]{:S(2)}, u32[]{:S(2)}) collective-permute-start(f32[16,128]{1,0:T(8,128)S(1)} %reduce_sum.9.middle_ref), channel_id=1, source_target_pairs={{0,1},{1,2},{2,3},{3,4},{4,5},{5,6},{6,7},{8,9},{9,10},{10,11},{11... | collective-permute-start | bytes 24584 | tf_op jit(solution)/shard_map/ppermute | solution.py:361

commit v5 on v3

--- a/solution.py
+++ b/solution.py
@@ -17,7 +17,8 @@
 UNKNOWNS = 1536
 EDGE = 256
 MARK = 120
-FIRST = 16
+FIRST = 60
+PART = 50
 ENTRIES = SUB * LOAD * SPOTS
 GRID_ROWS = 256
 FIBRE_RATE = 0.3
@@ -145,7 +146,11 @@
         out_ref[peer] = jnp.concatenate([partial[MODES * peer : MODES * peer + MODES], last], axis=0)
 
 
-def first_partial(received_ref, out_ref, block_ref):
+def first_partial(
+    received_ref, operator_hbm, out_ref, block_ref, operator_ref, operator_sem
+):
+    copy = pltpu.make_async_copy(operator_hbm, operator_ref, operator_sem)
+    copy.start()
     terms = received_ref[:, :16, :].reshape(SUB * 16, COLS)
     packed = received_ref[:, 16:, :].reshape(SUB * 8, COLS)
     lanes = lanes_of((SUB * 8, COLS))
@@ -164,6 +169,7 @@
     block_ref[:, : SUB * 16] = high
     block_ref[:, SUB * 16 :] = low
     partial_rows(high, low, terms, out_ref)
+    copy.wait()
 
 
 def later_partial(received_ref, block_ref, out_ref):
@@ -191,10 +197,13 @@
 def edge_rows(partners, send_ref):
     to_before = jnp.where(partners < SPOTS, 1.0, 0.0)
     to_after = jnp.where(partners >= 2 * SPOTS, 1.0, 0.0)
-    sides = jnp.concatenate([to_before, to_after, jnp.zeros((14, SPOTS), F32)], axis=0)
-    earlier = jnp.where(rows_of((SPOTS, SPOTS)) < lanes_of((SPOTS, SPOTS)), 1.0, 0.0).astype(BF16)
-    place = dot(sides.astype(BF16), earlier)
-    place = jnp.where(sides > 0.0, place, -1.0)
+    sides = jnp.concatenate([to_before, to_after, jnp.zeros((6, SPOTS), F32)], axis=0)
+    lanes = lanes_of(sides.shape)
+    place = sides
+    for power in range(10):
+        earlier = pltpu.roll(place, 1 << power, axis=1)
+        place = place + jnp.where(lanes >= 1 << power, earlier, 0.0)
+    place = jnp.where(sides > 0.0, place - 1.0, -1.0)
     slots = rows_of((EDGE, SPOTS)).astype(F32)
     send_ref[:EDGE, :] = jnp.where(slots == place[0:1], 1.0, 0.0).astype(BF16)
     send_ref[EDGE:, :] = jnp.where(slots == place[1:2], 1.0, 0.0).astype(BF16)
@@ -391,11 +400,14 @@
         limit=FIRST,
     )
     received = over(sent, "sub")
-    partial, block = call(
+    partial, block, operator = call(
         first_partial,
-        [to_load, ((COLS, 2 * SUB * 16), BF16)],
-        (received,),
+        [to_load, ((COLS, 2 * SUB * 16), BF16), (dual_ops.shape, BF16)],
+        (received, dual_ops),
         "first_partial",
+        scratch=[pltpu.SemaphoreType.DMA],
+        far=(1,),
+        limit=PART,
     )
     residual = dual_rhs
     before = ()
@@ -404,7 +416,7 @@
         iterate, images, lower, upper = call(
             functools.partial(advance, iteration == 0),
             [tall, ((SPOTS, COLS), BF16), edge, edge],
-            (received, damping, lifted, dual_ops, send, residual) + before,
+            (received, damping, lifted, (operator, dual_ops)[iteration], send, residual) + before,
             "advance",
         )
         before = (iterate,)

time: 147 us -> 143 us (0.973)
  local copies, waits for them, and re-layouts: 6.74 us -> 0.06 us
  Pallas kernels: 13.1 us -> 16 us
    unnamed x32 -> x24, local copies, waits for them, and re-layouts: 6.74 us -> 0.06 us
    pallas_call x12, Pallas kernels: 13.1 us -> 16 us  [call(): pl.pallas_call(kernel, in_specs=[hbm if place in far else vmem for place...]
where the time goes in v5:
time: 143 us
  blocking collectives  110 us (77%)
  Pallas kernels  16 us (11%)
  starting transfers between devices  9.71 us (7%)
  waiting for transfers between devices  5.97 us (4%)
    all_to_all x7, blocking collectives, over(): return lax.all_to_all(value, axis, 0, 0, tiled=True)  110 us
    pallas_call x12, Pallas kernels, call(): pl.pallas_call(kernel, in_specs=[hbm if place in far else vmem for place...  16 us
    ppermute x2, starting transfers between devices, both_ways(): return (lax.ppermute(value, axes, up), lax.ppermute(value, axes, down))  7.66 us
    ppermute x2, waiting for transfers between devices, on_device(): from_after = lax.ppermute(lower, whole, down)  4.44 us
  transfers between devices with their start and end apart: 6, of which 4 were waited for; matrix products, arithmetic and copies ran while one was open for 0% of the time, Pallas kernels for 2%

profile of v5, /device:TPU:1, one launch (start us, length us, event | category | flops | bytes accessed | tf_op | source)
XLA Modules:
  0.0 142.6 jit_solution(329493448926715903)
XLA Ops:
  0.7 4.2 %first_terms.1 = (f32[32,24,128]{2,1,0:T(8,128)}, bf16[512,1024]{1,0:T(8,128)(2,1)}, bf16[1024,128]{1,0:T(8,128)(2,1)}) custom-call(f32[1,1024,128]{2,1,0:T(8,128)} %rhs_ref.3, bf16[1,12,1024]{2,1,0:T(8,128)(2,1)} %basis_ref.3, f32[12,3072]{1,0:T(8,128)} %inverse_hbm.1, s32[1,1024]{1,0:T(1,128)} %partner_ref.1), custom_call_target="tpu_custom_call" | custom-call | bytes 16777216 | tf_op jit(solution)/shard_map/first_terms/pallas_call | solution.py:34
  4.8 23.7 %all_to_all.35.received_ref = f32[32,24,128]{2,1,0:T(8,128)S(1)} all-to-all(f32[32,24,128]{2,1,0:T(8,128)} %get-tuple-element.28), channel_id=1, replica_groups=mesh['sub'=32,'load'=8] {'sub'}, dimensions={0} | all-to-all | bytes 786432 | tf_op jit(solution)/shard_map/all_to_all | solution.py:385
  28.5 1.6 %first_partial.1 = (f32[8,16,128]{2,1,0:T(8,128)S(1)}, bf16[128,1024]{1,0:T(8,128)(2,1)S(1)}, bf16[1,1024,1024]{2,1,0:T(8,128)(2,1)S(1)}) custom-call(f32[32,24,128]{2,1,0:T(8,128)S(1)} %all_to_all.35.received_ref, bf16[1,1024,1024]{2,1,0:T(8,128)(2,1)} %operator_ref.1), custom_call_target="tpu_custom_call" | custom-call | bytes 16777216 | tf_op jit(solution)/shard_map/first_partial/pallas_call | solution.py:34
  30.1 12.9 %all_to_all.36.received_ref = f32[8,16,128]{2,1,0:T(8,128)S(1)} all-to-all(f32[8,16,128]{2,1,0:T(8,128)S(1)} %get-tuple-element.29), channel_id=1, replica_groups=mesh['sub'=32,'load'=8] {'load'}, dimensions={0} | all-to-all | bytes 131072 | tf_op jit(solution)/shard_map/all_to_all | solution.py:385
  43.1 1.6 %advance.2 = (f32[1024,128]{1,0:T(8,128)S(1)}, bf16[1024,128]{1,0:T(8,128)(2,1)S(1)}, bf16[256,128]{1,0:T(8,128)(2,1)S(1)}, bf16[256,128]{1,0:T(8,128)(2,1)S(1)}) custom-call(f32[8,16,128]{2,1,0:T(8,128)S(1)} %all_to_all.36.received_ref, f32[1,128]{1,0:T(1,128)S(1)} %bitcast.1, bf16[1024,128]{1,0:T(8,128)(2,1)S(1)} %copy-done.4, ...), custom_call_target="tpu_custom_call" | custom-call | bytes 16777216 | tf_op jit(solution)/shard_map/advance/pallas_call | solution.py:34
  44.7 1.0 collective-permute-start
  45.7 1.6 %first_inner.1 = (f32[1024,128]{1,0:T(8,128)S(1)}, bf16[1024,1536]{1,0:T(8,128)(2,1)S(1)}) custom-call(bf16[1024,128]{1,0:T(8,128)(2,1)S(1)} %get-tuple-element.33.images_ref, s32[1,1024]{1,0:T(1,128)S(1)} %copy-done.10), custom_call_target="tpu_custom_call" | custom-call | flops 2147483648 | bytes 8388608 | tf_op jit(solution)/shard_map/first_inner/pallas_call | solution.py:34
  47.3 2.1 %collective-permute-done.1.after_ref = bf16[256,128]{1,0:T(8,128)(2,1)S(1)} collective-permute-done((bf16[256,128]{1,0:T(8,128)(2,1)S(1)}, bf16[256,128]{1,0:T(8,128)(2,1)S(1)}, u32[]{:S(2)}, u32[]{:S(2)}) %collective-permute-start.1) | collective-permute-done | bytes 65568 | tf_op jit(solution)/shard_map/ppermute | solution.py:424
  49.4 0.6 residual_terms.2
  50.0 14.4 %all_to_all.37.received_ref = f32[32,16,128]{2,1,0:T(8,128)S(1)} all-to-all(f32[32,16,128]{2,1,0:T(8,128)S(1)} %get-tuple-element.38), channel_id=1, replica_groups=mesh['sub'=32,'load'=8] {'sub'}, dimensions={0} | all-to-all | bytes 524288 | tf_op jit(solution)/shard_map/all_to_all | solution.py:385
  64.7 15.3 %all_to_all.38.received_ref = f32[8,16,128]{2,1,0:T(8,128)S(1)} all-to-all(f32[8,16,128]{2,1,0:T(8,128)S(1)} %get-tuple-element.40), channel_id=1, replica_groups=mesh['sub'=32,'load'=8] {'load'}, dimensions={0} | all-to-all | bytes 131072 | tf_op jit(solution)/shard_map/all_to_all | solution.py:385
  80.1 1.6 %advance.3 = (f32[1024,128]{1,0:T(8,128)S(1)}, bf16[1024,128]{1,0:T(8,128)(2,1)S(1)}, bf16[256,128]{1,0:T(8,128)(2,1)S(1)}, bf16[256,128]{1,0:T(8,128)(2,1)S(1)}) custom-call(f32[8,16,128]{2,1,0:T(8,128)S(1)} %all_to_all.38.received_ref, f32[1,128]{1,0:T(1,128)S(1)} %bitcast.2, bf16[1024,128]{1,0:T(8,128)(2,1)S(1)} %copy-done.4, ...), custom_call_target="tpu_custom_call" | custom-call | bytes 16777216 | tf_op jit(solution)/shard_map/advance/pallas_call | solution.py:34
  81.7 1.0 collective-permute-start.2
  82.7 0.7 inner_classes.1
  84.1 2.4 %collective-permute-done.3.after_ref = bf16[256,128]{1,0:T(8,128)(2,1)S(1)} collective-permute-done((bf16[256,128]{1,0:T(8,128)(2,1)S(1)}, bf16[256,128]{1,0:T(8,128)(2,1)S(1)}, u32[]{:S(2)}, u32[]{:S(2)}) %collective-permute-start.3) | collective-permute-done | bytes 65568 | tf_op jit(solution)/shard_map/ppermute | solution.py:424
  86.4 0.6 residual_terms.3
  87.0 13.9 %all_to_all.39.received_ref = f32[32,16,128]{2,1,0:T(8,128)S(1)} all-to-all(f32[32,16,128]{2,1,0:T(8,128)S(1)} %get-tuple-element.48), channel_id=1, replica_groups=mesh['sub'=32,'load'=8] {'sub'}, dimensions={0} | all-to-all | bytes 524288 | tf_op jit(solution)/shard_map/all_to_all | solution.py:385
  101.2 15.9 %all_to_all.40.received_ref = f32[8,16,128]{2,1,0:T(8,128)S(1)} all-to-all(f32[8,16,128]{2,1,0:T(8,128)S(1)} %later_partial.1), channel_id=1, replica_groups=mesh['sub'=32,'load'=8] {'load'}, dimensions={0} | all-to-all | bytes 131072 | tf_op jit(solution)/shard_map/all_to_all | solution.py:385
  117.1 2.2 %gradients.1 = (f32[1,1024,128]{2,1,0:T(8,128)}, f32[32,16,128]{2,1,0:T(8,128)S(1)}) custom-call(f32[8,16,128]{2,1,0:T(8,128)S(1)} %all_to_all.40.received_ref, f32[1,128]{1,0:T(1,128)S(1)} %bitcast.3, bf16[1024,128]{1,0:T(8,128)(2,1)S(1)} %copy-done.4, f32[1024,128]{1,0:T(8,128)S(1)} %get-tuple-element.49.residual_ref, ...), custom_call_target="tpu_custom_call" | custom-call | bytes 16777216 | tf_op jit(solution)/shard_map/gradients/pallas_call | solution.py:34
  119.3 13.8 %all_to_all.41 = f32[32,16,128]{2,1,0:T(8,128)S(1)} all-to-all(f32[32,16,128]{2,1,0:T(8,128)S(1)} %get-tuple-element.52), channel_id=1, replica_groups=mesh['sub'=32,'load'=8] {'sub'}, dimensions={0} | all-to-all | bytes 524288 | tf_op jit(solution)/shard_map/all_to_all | solution.py:385
  133.2 5.6 %collective-permute-start.5 = (f32[16,128]{1,0:T(8,128)S(1)}, f32[16,128]{1,0:T(8,128)S(1)}, u32[]{:S(2)}, u32[]{:S(2)}) collective-permute-start(f32[16,128]{1,0:T(8,128)S(1)} %reduce_sum.9.middle_ref), channel_id=1, source_target_pairs={{1,0},{2,1},{3,2},{4,3},{5,4},{6,5},{7,6},{9,8},{10,9},{11,10},{12... | collective-permute-start | bytes 24584 | tf_op jit(solution)/shard_map/ppermute | solution.py:359
  138.7 2.1 %collective-permute-start.4 = (f32[16,128]{1,0:T(8,128)S(1)}, f32[16,128]{1,0:T(8,128)S(1)}, u32[]{:S(2)}, u32[]{:S(2)}) collective-permute-start(f32[16,128]{1,0:T(8,128)S(1)} %reduce_sum.9.middle_ref), channel_id=1, source_target_pairs={{0,1},{1,2},{2,3},{3,4},{4,5},{5,6},{6,7},{8,9},{9,10},{10,11},{11... | collective-permute-start | bytes 24584 | tf_op jit(solution)/shard_map/ppermute | solution.py:359
  140.8 1.0 collective-permute-done.4.left_ref
  141.8 0.8 smooth.1
  (32 shorter events, 1.2 us)
Async XLA Ops:
  0.6 42.4 %copy-start.1 = (f32[1,1024,128]{2,1,0:T(8,128)S(1)}, f32[1,1024,128]{2,1,0:T(8,128)}, u32[]{:S(2)}) copy-start(f32[1,1024,128]{2,1,0:T(8,128)} %rhs_ref.3) | copy-start | bytes 1572868
  0.6 42.4 %copy-start.9 = (f32[128]{0:T(128)S(1)}, f32[128]{0:T(128)}, u32[]{:S(2)}) copy-start(f32[128]{0:T(128)} %param.16) | copy-start | bytes 1540
  4.8 38.3 %copy-start.2 = (bf16[512,1024]{1,0:T(8,128)(2,1)S(1)}, bf16[512,1024]{1,0:T(8,128)(2,1)}, u32[]{:S(2)}) copy-start(bf16[512,1024]{1,0:T(8,128)(2,1)} %get-tuple-element.32.send_ref) | copy-start | bytes 3145732
  4.8 38.3 %copy-start.4 = (bf16[1024,128]{1,0:T(8,128)(2,1)S(1)}, bf16[1024,128]{1,0:T(8,128)(2,1)}, u32[]{:S(2)}) copy-start(bf16[1024,128]{1,0:T(8,128)(2,1)} %get-tuple-element.30.lifted_ref) | copy-start | bytes 786436
  28.5 17.2 %copy-start.10 = (s32[1,1024]{1,0:T(1,128)S(1)}, s32[1,1024]{1,0:T(1,128)}, u32[]{:S(2)}) copy-start(s32[1,1024]{1,0:T(1,128)} %partner_ref.1) | copy-start | bytes 12292
  44.7 2.6 %collective-permute-start = (bf16[256,128]{1,0:T(8,128)(2,1)S(1)}, bf16[256,128]{1,0:T(8,128)(2,1)S(1)}, u32[]{:S(2)}, u32[]{:S(2)}) collective-permute-start(bf16[256,128]{1,0:T(8,128)(2,1)S(1)} %get-tuple-element.36), channel_id=1, source_target_pairs={{0,1},{1,2},{2,3},{3,4},{4,5},{5,6},{6,7},{7,8},{8,9},{9,10},{10,1... | collective-permute-start | bytes 196616 | tf_op jit(solution)/shard_map/ppermute | solution.py:423
  45.7 3.7 %collective-permute-start.1 = (bf16[256,128]{1,0:T(8,128)(2,1)S(1)}, bf16[256,128]{1,0:T(8,128)(2,1)S(1)}, u32[]{:S(2)}, u32[]{:S(2)}) collective-permute-start(bf16[256,128]{1,0:T(8,128)(2,1)S(1)} %get-tuple-element.37), channel_id=1, source_target_pairs={{1,0},{2,1},{3,2},{4,3},{5,4},{6,5},{7,6},{8,7},{9,8},{10,9},{11,1... | collective-permute-start | bytes 196616 | tf_op jit(solution)/shard_map/ppermute | solution.py:424
  45.7 3.7 %copy-start.7 = (bf16[1,12,1024]{2,1,0:T(8,128)(2,1)S(1)}, bf16[1,12,1024]{2,1,0:T(8,128)(2,1)}, u32[]{:S(2)}) copy-start(bf16[1,12,1024]{2,1,0:T(8,128)(2,1)} %basis_ref.3) | copy-start | bytes 73732
  45.7 3.7 %copy-start.8 = (s32[8,128]{1,0:T(8,128)S(1)}, s32[8,128]{1,0:T(8,128)}, u32[]{:S(2)}) copy-start(s32[8,128]{1,0:T(8,128)} %class_ref.5) | copy-start | bytes 12292
  47.3 32.7 %copy-start = (bf16[1,1024,1024]{2,1,0:T(8,128)(2,1)S(1)}, bf16[1,1024,1024]{2,1,0:T(8,128)(2,1)}, u32[]{:S(2)}) copy-start(bf16[1,1024,1024]{2,1,0:T(8,128)(2,1)} %operator_ref.1) | copy-start | bytes 6291460
  81.7 2.4 %collective-permute-start.2 = (bf16[256,128]{1,0:T(8,128)(2,1)S(1)}, bf16[256,128]{1,0:T(8,128)(2,1)S(1)}, u32[]{:S(2)}, u32[]{:S(2)}) collective-permute-start(bf16[256,128]{1,0:T(8,128)(2,1)S(1)} %get-tuple-element.46), channel_id=1, source_target_pairs={{0,1},{1,2},{2,3},{3,4},{4,5},{5,6},{6,7},{7,8},{8,9},{9,10},{10,1... | collective-permute-start | bytes 196616 | tf_op jit(solution)/shard_map/ppermute | solution.py:423
  82.7 3.7 %collective-permute-start.3 = (bf16[256,128]{1,0:T(8,128)(2,1)S(1)}, bf16[256,128]{1,0:T(8,128)(2,1)S(1)}, u32[]{:S(2)}, u32[]{:S(2)}) collective-permute-start(bf16[256,128]{1,0:T(8,128)(2,1)S(1)} %get-tuple-element.47), channel_id=1, source_target_pairs={{1,0},{2,1},{3,2},{4,3},{5,4},{6,5},{7,6},{8,7},{9,8},{10,9},{11,1... | collective-permute-start | bytes 196616 | tf_op jit(solution)/shard_map/ppermute | solution.py:424
  83.4 33.6 %copy-start.3 = (bf16[1,1536,1024]{2,1,0:T(8,128)(2,1)S(1)}, bf16[1,1536,1024]{2,1,0:T(8,128)(2,1)}, u32[]{:S(2)}) copy-start(bf16[1,1536,1024]{2,1,0:T(8,128)(2,1)} %recovery_ref.1) | copy-start | bytes 9437188
  83.4 33.6 %copy-start.5 = (bf16[1,1536,128]{2,1,0:T(8,128)(2,1)S(1)}, bf16[1,1536,128]{2,1,0:T(8,128)(2,1)}, u32[]{:S(2)}) copy-start(bf16[1,1536,128]{2,1,0:T(8,128)(2,1)} %base_ref.1) | copy-start | bytes 1179652
  83.5 33.6 %copy-start.6 = (bf16[1,1536,128]{2,1,0:T(8,128)(2,1)S(1)}, bf16[1,1536,128]{2,1,0:T(8,128)(2,1)}, u32[]{:S(2)}) copy-start(bf16[1,1536,128]{2,1,0:T(8,128)(2,1)} %adjoint_ref.1) | copy-start | bytes 1179652
  83.5 33.6 %copy-start.11 = (s32[1,128]{1,0:T(1,128)S(1)}, s32[1,128]{1,0:T(1,128)}, u32[]{:S(2)}) copy-start(s32[1,128]{1,0:T(1,128)} %voxel_ref.1) | copy-start | bytes 1540
  133.2 7.7 %collective-permute-start.5 = (f32[16,128]{1,0:T(8,128)S(1)}, f32[16,128]{1,0:T(8,128)S(1)}, u32[]{:S(2)}, u32[]{:S(2)}) collective-permute-start(f32[16,128]{1,0:T(8,128)S(1)} %reduce_sum.9.middle_ref), channel_id=1, source_target_pairs={{1,0},{2,1},{3,2},{4,3},{5,4},{6,5},{7,6},{9,8},{10,9},{11,10},{12... | collective-permute-start | bytes 24584 | tf_op jit(solution)/shard_map/ppermute | solution.py:359
  138.7 3.1 %collective-permute-start.4 = (f32[16,128]{1,0:T(8,128)S(1)}, f32[16,128]{1,0:T(8,128)S(1)}, u32[]{:S(2)}, u32[]{:S(2)}) collective-permute-start(f32[16,128]{1,0:T(8,128)S(1)} %reduce_sum.9.middle_ref), channel_id=1, source_target_pairs={{0,1},{1,2},{2,3},{3,4},{4,5},{5,6},{6,7},{8,9},{9,10},{10,11},{11... | collective-permute-start | bytes 24584 | tf_op jit(solution)/shard_map/ppermute | solution.py:359

commit v6 on v5

--- a/solution.py
+++ b/solution.py
@@ -16,7 +16,6 @@
 COLS = 128
 UNKNOWNS = 1536
 EDGE = 256
-MARK = 120
 FIRST = 60
 PART = 50
 ENTRIES = SUB * LOAD * SPOTS
@@ -29,11 +28,12 @@
 BF16 = jnp.bfloat16
 
 
-def call(kernel, outs, operands, name, flops=0, moved=16 * 2**20, limit=16, scratch=(), far=()):
+def call(kernel, outs, operands, name, flops=0, moved=16 * 2**20, limit=16, scratch=(), far=(), far_out=()):
     vmem, hbm = pl.BlockSpec(memory_space=pltpu.VMEM), pl.BlockSpec(memory_space=pltpu.HBM)
     return pl.pallas_call(
         kernel,
         in_specs=[hbm if place in far else vmem for place in range(len(operands))],
+        out_specs=[hbm if place in far_out else vmem for place in range(len(outs))],
         out_shape=[jax.ShapeDtypeStruct(shape, dtype) for shape, dtype in outs],
         scratch_shapes=list(scratch),
         compiler_params=pltpu.CompilerParams(vmem_limit_bytes=int(limit * 2**20)),
@@ -107,24 +107,27 @@
     copies[0].wait()
     inverse = inverse_ref[...]
     inverse = jnp.concatenate([inverse, inverse[:, :128]], axis=1)
-    lanes = lanes_of((8, COLS))
-    lane = lanes_of((1, COLS))
-    spares = []
-    for peer in range(SUB):
-        start = peer * LOAD * MODES
+    pieces = []
+    for group in range(SUB):
+        start = group * LOAD * MODES
         tile, offset = start // 128, start % 128
         piece = inverse[:, 128 * tile : 128 * tile + 256]
         if offset:
             piece = pltpu.roll(piece, 256 - offset, axis=1)
-        piece = piece[:, :128]
-        last = piece[8:12]
-        beside = jnp.concatenate([pltpu.roll(last, 96, axis=1), pltpu.roll(last, 64, axis=1)], axis=0)
-        spare = pltpu.roll(last[0:1], 64, axis=1)
-        for place, turn in ((1, 96), (2, 0), (3, 32)):
-            part = last[place : place + 1]
-            spare = jnp.where(lane < 32 * place, spare, pltpu.roll(part, turn, axis=1) if turn else part)
-        out_ref[peer, 16:, :] = jnp.where(lanes < 96, piece[:8], beside)
-        spares.append(spare)
+        pieces.append(piece[:, :128])
+    lanes = lanes_of((MODES, COLS))
+    masks = [(lanes >= 16 * slot) & (lanes < 16 * slot + MODES) for slot in range(8)]
+    for peer in range(LOAD):
+        tiles = []
+        for tile in range(4):
+            chosen = jnp.zeros((MODES, COLS), F32)
+            for slot in range(8):
+                turn = (16 * slot - MODES * peer) % 128
+                piece = pieces[8 * tile + slot]
+                piece = pltpu.roll(piece, turn, axis=1) if turn else piece
+                chosen = jnp.where(masks[slot], piece, chosen)
+            tiles.append(chosen)
+        out_ref[peer, 16:, :] = jnp.concatenate(tiles, axis=0)
     copies[3].wait()
     edge_rows(partner_ref[...].astype(F32), send_ref)
     copies[1].wait()
@@ -133,65 +136,54 @@
     lifted_ref[...] = basis.astype(BF16)
     copies[2].wait()
     rows = coarse_rows(basis_ref, rhs_ref[0])
-    row = rows_of(rows.shape)
-    for peer in range(SUB):
-        out_ref[peer, :16, :] = jnp.where(row == 15, spares[peer], rows)
+    for peer in range(LOAD):
+        out_ref[peer, :16, :] = rows
 
 
 def partial_rows(high, low, terms, out_ref):
     terms_high, terms_low = split2(terms)
     partial = dot(high, terms_high) + dot(high, terms_low) + dot(low, terms_high)
-    last = jnp.concatenate([partial[MARK : MARK + 1], jnp.zeros((3, COLS), F32)], axis=0)
-    for peer in range(LOAD):
-        out_ref[peer] = jnp.concatenate([partial[MODES * peer : MODES * peer + MODES], last], axis=0)
-
-
-def first_partial(
-    received_ref, operator_hbm, out_ref, block_ref, operator_ref, operator_sem
-):
+    out_ref[...] = partial.reshape(SUB, 16, COLS)
+
+
+def first_partial(received_ref, operator_hbm, out_ref, block_ref, operator_ref, operator_sem):
     copy = pltpu.make_async_copy(operator_hbm, operator_ref, operator_sem)
     copy.start()
-    terms = received_ref[:, :16, :].reshape(SUB * 16, COLS)
-    packed = received_ref[:, 16:, :].reshape(SUB * 8, COLS)
-    lanes = lanes_of((SUB * 8, COLS))
-    upper = jnp.where(lanes < 96, packed, 0.0).reshape(SUB, 8, COLS)
-    first = pltpu.roll(packed, 32, axis=1).reshape(SUB, 8, COLS)[:, :4]
-    second = pltpu.roll(packed, 64, axis=1).reshape(SUB, 8, COLS)[:, 4:]
-    spare = received_ref[:, 15, :]
-    third = [pltpu.roll(spare, 64, axis=1), pltpu.roll(spare, 32, axis=1), spare, pltpu.roll(spare, 96, axis=1)]
-    third = jnp.concatenate([part.reshape(SUB, 1, COLS) for part in third], axis=1)
-    lanes = lax.broadcasted_iota(jnp.int32, (SUB, 4, COLS), 2)
-    lower = jnp.where(lanes < 32, first, jnp.where(lanes < 64, second, jnp.where(lanes < 96, third, 0.0)))
-    places = lax.broadcasted_iota(jnp.int32, (SUB, 4, COLS), 1)
-    mark = jnp.where((places == 0) & (lanes == MARK), 1.0, 0.0)
-    block = jnp.concatenate([upper, jnp.concatenate([lower, mark], axis=1)], axis=1)
-    high, low = split2(block.reshape(SUB * 16, COLS).T)
-    block_ref[:, : SUB * 16] = high
-    block_ref[:, SUB * 16 :] = low
+    terms = received_ref[:, :16, :].reshape(LOAD * 16, COLS)
+    lanes = lax.broadcasted_iota(jnp.int32, (LOAD, 4, COLS), 2)
+    places = lax.broadcasted_iota(jnp.int32, (LOAD, 4, COLS), 1)
+    mark = jnp.where((places == 0) & (lanes % 16 == MODES), 1.0, 0.0)
+    blocks = []
+    for tile in range(4):
+        start = 16 + MODES * tile
+        rows = jnp.concatenate([received_ref[:, start : start + MODES, :], mark], axis=1)
+        blocks.append(rows.reshape(LOAD * 16, COLS).T)
+    high, low = split2(jnp.concatenate(blocks, axis=0))
+    block_ref[:, :COLS] = high
+    block_ref[:, COLS:] = low
     partial_rows(high, low, terms, out_ref)
     copy.wait()
 
 
 def later_partial(received_ref, block_ref, out_ref):
-    terms = received_ref[...].reshape(SUB * 16, COLS)
-    partial_rows(block_ref[:, : SUB * 16], block_ref[:, SUB * 16 :], terms, out_ref)
-
-
-def class_partial(received_ref, block_ref, class_ref, out_ref, middle_ref):
+    terms = received_ref[...].reshape(LOAD * 16, COLS)
+    partial_rows(block_ref[:, :COLS], block_ref[:, COLS:], terms, out_ref)
+
+
+def class_partial(received_ref, block_ref, class_ref, out_ref, sides_ref):
     later_partial(received_ref, block_ref, out_ref)
-    here = lax.axis_index("sub")
-    above = received_ref[jnp.maximum(here - 1, 0)][14:15]
-    below = received_ref[jnp.minimum(here + 1, SUB - 1)][13:14]
-    above = jnp.where(here > 0, above, 0.0)
-    below = jnp.where(here < SUB - 1, below, 0.0)
+    here = lax.axis_index("load")
+    right = received_ref[jnp.minimum(here + 1, LOAD - 1)][13:14]
+    left = received_ref[jnp.maximum(here - 1, 0)][14:15]
+    right = jnp.where(here < LOAD - 1, right, 0.0)
+    left = jnp.where(here > 0, left, 0.0)
+    lanes = lanes_of((1, COLS))
+    sides = jnp.where(lanes < 8, right, jnp.where(lanes < 16, pltpu.roll(left, 8, axis=1), 0.0))
     classes = (class_ref[...] + 1).astype(F32)
-    gap = jnp.zeros((1, COLS), F32)
-    middle = jnp.concatenate([gap, above, classes, below, gap, gap, gap, gap, gap], axis=0)
-    middle_ref[...] = middle
-    sides = jnp.concatenate([middle, jnp.zeros((COLS - 16, COLS), F32)], axis=0).T
-    for peer in range(LOAD):
-        out_ref[peer, 13:14, :] = sides[0:1]
-        out_ref[peer, 14:15, :] = sides[127:128]
+    edges = jnp.concatenate([classes[0:1], classes[7:8], sides], axis=0)
+    for peer in range(SUB):
+        out_ref[peer, 13:16, :] = edges
+    sides_ref[...] = jnp.broadcast_to(sides, sides_ref.shape)
 
 
 def edge_rows(partners, send_ref):
@@ -232,9 +224,7 @@
 
 
 def step_parts(received_ref, damping_ref, lifted_ref):
-    total = received_ref[0]
-    for peer in range(1, LOAD):
-        total = total + received_ref[peer]
+    total = jnp.sum(received_ref[...], axis=0)
     step = damping_ref[...] / jnp.sqrt(total[MODES : MODES + 1] / ENTRIES + EPSILON)
     correction = jnp.where(rows_of(total.shape) < MODES, total, 0.0)
     stacked = jnp.concatenate(split3(correction) + (jnp.zeros((COLS - 48, COLS), BF16),), axis=0)
@@ -261,17 +251,30 @@
     out_ref[...] = dot(pick_ref[:, EDGE : EDGE + SPOTS], images_ref[...])
 
 
-def inner_classes(images_ref, pick_ref, received_ref, middle_ref, out_ref, classes_ref):
-    here = lax.axis_index("load")
-    right = received_ref[jnp.minimum(here + 1, LOAD - 1)][13:14]
-    left = received_ref[jnp.maximum(here - 1, 0)][14:15]
-    right = jnp.where(here < LOAD - 1, right, 0.0)
-    left = jnp.where(here > 0, left, 0.0)
-    right = jnp.broadcast_to(right, (128, 128)).T[:16]
-    left = jnp.broadcast_to(left, (128, 128)).T[:16]
-    lanes = lanes_of((16, 128))
-    classes_ref[:, :128] = middle_ref[...]
-    classes_ref[:, 128:] = jnp.where(lanes == 0, right, jnp.where(lanes == 127, left, 0.0))
+def inner_classes(images_ref, pick_ref, received_ref, class_ref, sides_ref, out_ref, classes_ref):
+    here = lax.axis_index("sub")
+    above = jnp.where(here > 0, received_ref[jnp.maximum(here - 1, 0)], 0.0)
+    below = jnp.where(here < SUB - 1, received_ref[jnp.minimum(here + 1, SUB - 1)], 0.0)
+    classes = (class_ref[...] + 1).astype(F32)
+    gap = jnp.zeros((1, COLS), F32)
+    middle = jnp.concatenate([gap, above[14:15], classes, below[13:14], gap, gap, gap, gap, gap], axis=0)
+    lanes = lanes_of((1, COLS))
+
+    def column(offset):
+        def at(value, source, target):
+            turn = (target - source - offset) % 128
+            return pltpu.roll(value, turn, axis=1) if turn else value
+
+        own = at(sides_ref[0:1], 0, 2)
+        own = jnp.where((lanes >= 2) & (lanes < 10), own, 0.0)
+        own = jnp.where(lanes == 1, at(above[15:16], 7, 1), own)
+        own = jnp.where(lanes == 10, at(below[15:16], 0, 10), own)
+        return jnp.broadcast_to(own, (128, 128)).T[:16]
+
+    right, left = column(0), column(8)
+    wide = lanes_of((16, 128))
+    classes_ref[:, :128] = middle
+    classes_ref[:, 128:] = jnp.where(wide == 0, right, jnp.where(wide == 127, left, 0.0))
     inner_pairs(images_ref, pick_ref, out_ref)
 
 
@@ -285,8 +288,9 @@
     rows = coarse_rows(basis_ref, residual)
     classes = (class_ref[...] + 1).astype(F32)
     row = rows_of(rows.shape)
-    rows = jnp.where(row == 13, classes[0:1], jnp.where(row == 14, classes[7:8], rows))
-    for peer in range(SUB):
+    columns = jnp.concatenate([classes, jnp.zeros((COLS - 8, COLS), F32)], axis=0).T
+    rows = jnp.where(row == 13, columns[0:1], jnp.where(row == 14, columns[127:128], rows))
+    for peer in range(LOAD):
         out_ref[peer] = rows
 
 
@@ -300,12 +304,16 @@
     base_ref,
     adjoint_ref,
     voxel_ref,
+    multipliers_hbm,
+    out_ref,
     multipliers_ref,
-    out_ref,
+    multipliers_sem,
 ):
     step, lifted = step_parts(received_ref, damping_ref, lifted_ref)
     multipliers = iterate_ref[...] + step * (residual_ref[...] - lifted)
     multipliers_ref[0] = multipliers
+    copy = pltpu.make_async_copy(multipliers_ref, multipliers_hbm, multipliers_sem)
+    copy.start()
     displaced = base_ref[0].astype(F32) - dot(recovery_ref[0], multipliers.astype(BF16))
     products = displaced * adjoint_ref[0].astype(F32)
     first = EDOF * rows_of((128, UNKNOWNS))
@@ -322,6 +330,7 @@
     spread = parts[:, :COLS] + parts[:, COLS : 2 * COLS] + parts[:, 2 * COLS :]
     for peer in range(SUB):
         out_ref[peer] = spread[8 * peer : 8 * peer + 16]
+    copy.wait()
 
 
 def smooth(middle_ref, left_ref, right_ref, classes_ref, out_ref):
@@ -386,7 +395,7 @@
 
     sent, send, lifted = call(
         first_terms,
-        [((SUB, 24, COLS), F32), ((2 * EDGE, SPOTS), BF16), ((SPOTS, COLS), BF16)],
+        [((LOAD, 64, COLS), F32), ((2 * EDGE, SPOTS), BF16), ((SPOTS, COLS), BF16)],
         (dual_rhs, coarse_basis, coarse_inverse, partner),
         "first_terms",
         scratch=[
@@ -399,10 +408,10 @@
         far=(0, 1, 2, 3),
         limit=FIRST,
     )
-    received = over(sent, "sub")
+    received = over(sent, "load")
     partial, block, operator = call(
         first_partial,
-        [to_load, ((COLS, 2 * SUB * 16), BF16), (dual_ops.shape, BF16)],
+        [to_sub, ((SUB * 16, 2 * COLS), BF16), (dual_ops.shape, BF16)],
         (received, dual_ops),
         "first_partial",
         scratch=[pltpu.SemaphoreType.DMA],
@@ -412,7 +421,7 @@
     residual = dual_rhs
     before = ()
     for iteration in range(2):
-        received = over(partial, "load")
+        received = over(partial, "sub")
         iterate, images, lower, upper = call(
             functools.partial(advance, iteration == 0),
             [tall, ((SPOTS, COLS), BF16), edge, edge],
@@ -429,28 +438,30 @@
             )
         else:
             inner, classes = call(
-                inner_classes, [tall, ((16, 2 * COLS), F32)], (images, pick, received, middle), "inner_classes",
+                inner_classes, [tall, ((16, 2 * COLS), F32)], (images, pick, received, fibre_class, sides), "inner_classes",
                 flops=2 * SPOTS * SPOTS * 256, moved=4 * 2**20,
             )
         residual, sent = call(
             residual_terms,
-            [tall, to_sub],
+            [tall, to_load],
             (dual_rhs, images, inner, pick, from_before, from_after, coarse_basis, fibre_class),
             "residual_terms",
         )
-        received = over(sent, "sub")
+        received = over(sent, "load")
         if iteration == 0:
-            partial, middle = call(
-                class_partial, [to_load, ((16, COLS), F32)], (received, block, fibre_class), "class_partial"
+            partial, sides = call(
+                class_partial, [to_sub, ((8, COLS), F32)], (received, block, fibre_class), "class_partial"
             )
         else:
-            (partial,) = call(later_partial, [to_load], (received, block), "later_partial")
-    received = over(partial, "load")
+            (partial,) = call(later_partial, [to_sub], (received, block), "later_partial")
+    received = over(partial, "sub")
     multipliers, sent = call(
         gradients,
         [((1, SPOTS, COLS), F32), to_sub],
         (received, damping, lifted, residual, iterate, recovery, base_disp, adjoint, elem_voxel),
         "gradients",
+        scratch=[pltpu.VMEM((1, SPOTS, COLS), F32), pltpu.SemaphoreType.DMA],
+        far_out=(0,),
     )
     middle = jnp.sum(over(sent, "sub"), axis=0)
     left, right = both_ways(middle, "load", LOAD, False)

time: 143 us -> 147 us (1.028)
  starting transfers between devices: 9.71 us -> 15.4 us
  blocking collectives: 110 us -> 108 us
    ppermute x2, starting transfers between devices: 2.05 us -> 7.77 us  [on_device(): from_before = lax.ppermute(upper, whole, up)]
    all_to_all x7, blocking collectives: 110 us -> 108 us  [over(): return lax.all_to_all(value, axis, 0, 0, tiled=True)]
where the time goes in v6:
time: 147 us; the launch traced here: 146 us
  blocking collectives  108 us (73%)
  Pallas kernels  15.8 us (11%)
  starting transfers between devices  15.4 us (10%)
  waiting for transfers between devices  5.97 us (4%)
    all_to_all x7, blocking collectives, over(): return lax.all_to_all(value, axis, 0, 0, tiled=True)  108 us
    pallas_call x12, Pallas kernels, call(): pl.pallas_call(kernel, in_specs=[hbm if place in far else vmem for place...  15.8 us
    ppermute x2, starting transfers between devices, on_device(): from_before = lax.ppermute(upper, whole, up)  7.77 us
    ppermute x2, starting transfers between devices, both_ways(): return (lax.ppermute(value, axes, up), lax.ppermute(value, axes, down))  7.67 us
    ppermute x2, waiting for transfers between devices, on_device(): from_after = lax.ppermute(lower, whole, down)  4.44 us
  transfers between devices with their start and end apart: 6, of which 4 were waited for; matrix products, arithmetic and copies ran while one was open for 0% of the time, Pallas kernels for 2%

profile of v6, /device:TPU:1, one launch (start us, length us, event | category | flops | bytes accessed | tf_op | source)
XLA Modules:
  0.0 146.3 jit_solution(18254531927152564325)
XLA Ops:
  0.7 3.9 %first_terms.1 = (f32[8,64,128]{2,1,0:T(8,128)}, bf16[512,1024]{1,0:T(8,128)(2,1)}, bf16[1024,128]{1,0:T(8,128)(2,1)}) custom-call(f32[1,1024,128]{2,1,0:T(8,128)} %rhs_ref.3, bf16[1,12,1024]{2,1,0:T(8,128)(2,1)} %basis_ref.3, f32[12,3072]{1,0:T(8,128)} %inverse_hbm.1, s32[1,1024]{1,0:T(1,128)} %partner_ref.1), custom_call_target="tpu_custom_call" | custom-call | bytes 16777216 | tf_op jit(solution)/shard_map/first_terms/pallas_call | solution.py:33
  4.6 13.2 %all_to_all.35.received_ref = f32[8,64,128]{2,1,0:T(8,128)S(1)} all-to-all(f32[8,64,128]{2,1,0:T(8,128)} %get-tuple-element.28), channel_id=1, replica_groups=mesh['sub'=32,'load'=8] {'load'}, dimensions={0} | all-to-all | bytes 524288 | tf_op jit(solution)/shard_map/all_to_all | solution.py:394
  17.8 1.6 %first_partial.1 = (f32[32,16,128]{2,1,0:T(8,128)S(1)}, bf16[512,256]{1,0:T(8,128)(2,1)S(1)}, bf16[1,1024,1024]{2,1,0:T(8,128)(2,1)S(1)}) custom-call(f32[8,64,128]{2,1,0:T(8,128)S(1)} %all_to_all.35.received_ref, bf16[1,1024,1024]{2,1,0:T(8,128)(2,1)} %operator_ref.1), custom_call_target="tpu_custom_call" | custom-call | bytes 16777216 | tf_op jit(solution)/shard_map/first_partial/pallas_call | solution.py:33
  19.4 19.9 %all_to_all.36.received_ref = f32[32,16,128]{2,1,0:T(8,128)S(1)} all-to-all(f32[32,16,128]{2,1,0:T(8,128)S(1)} %get-tuple-element.29), channel_id=1, replica_groups=mesh['sub'=32,'load'=8] {'sub'}, dimensions={0} | all-to-all | bytes 524288 | tf_op jit(solution)/shard_map/all_to_all | solution.py:394
  39.3 1.6 %advance.2 = (f32[1024,128]{1,0:T(8,128)S(1)}, bf16[1024,128]{1,0:T(8,128)(2,1)S(1)}, bf16[256,128]{1,0:T(8,128)(2,1)S(1)}, bf16[256,128]{1,0:T(8,128)(2,1)S(1)}) custom-call(f32[32,16,128]{2,1,0:T(8,128)S(1)} %all_to_all.36.received_ref, f32[1,128]{1,0:T(1,128)S(1)} %bitcast.1, bf16[1024,128]{1,0:T(8,128)(2,1)S(1)} %copy-done.4, ...), custom_call_target="tpu_custom_call" | custom-call | bytes 16777216 | tf_op jit(solution)/shard_map/advance/pallas_call | solution.py:33
  41.0 3.9 %collective-permute-start = (bf16[256,128]{1,0:T(8,128)(2,1)S(1)}, bf16[256,128]{1,0:T(8,128)(2,1)S(1)}, u32[]{:S(2)}, u32[]{:S(2)}) collective-permute-start(bf16[256,128]{1,0:T(8,128)(2,1)S(1)} %get-tuple-element.36), channel_id=1, source_target_pairs={{0,1},{1,2},{2,3},{3,4},{4,5},{5,6},{6,7},{7,8},{8,9},{9,10},{10,1... | collective-permute-start | bytes 196616 | tf_op jit(solution)/shard_map/ppermute | solution.py:432
  44.9 1.6 %first_inner.1 = (f32[1024,128]{1,0:T(8,128)S(1)}, bf16[1024,1536]{1,0:T(8,128)(2,1)S(1)}) custom-call(bf16[1024,128]{1,0:T(8,128)(2,1)S(1)} %get-tuple-element.33.images_ref, s32[1,1024]{1,0:T(1,128)S(1)} %copy-done.10), custom_call_target="tpu_custom_call" | custom-call | flops 2147483648 | bytes 8388608 | tf_op jit(solution)/shard_map/first_inner/pallas_call | solution.py:33
  46.5 2.1 %collective-permute-done.1.after_ref = bf16[256,128]{1,0:T(8,128)(2,1)S(1)} collective-permute-done((bf16[256,128]{1,0:T(8,128)(2,1)S(1)}, bf16[256,128]{1,0:T(8,128)(2,1)S(1)}, u32[]{:S(2)}, u32[]{:S(2)}) %collective-permute-start.1) | collective-permute-done | bytes 65568 | tf_op jit(solution)/shard_map/ppermute | solution.py:433
  48.5 0.6 residual_terms.2
  49.1 12.5 %all_to_all.37.received_ref = f32[8,16,128]{2,1,0:T(8,128)S(1)} all-to-all(f32[8,16,128]{2,1,0:T(8,128)S(1)} %get-tuple-element.38), channel_id=1, replica_groups=mesh['sub'=32,'load'=8] {'load'}, dimensions={0} | all-to-all | bytes 131072 | tf_op jit(solution)/shard_map/all_to_all | solution.py:394
  61.9 17.3 %all_to_all.38.received_ref = f32[32,16,128]{2,1,0:T(8,128)S(1)} all-to-all(f32[32,16,128]{2,1,0:T(8,128)S(1)} %get-tuple-element.40), channel_id=1, replica_groups=mesh['sub'=32,'load'=8] {'sub'}, dimensions={0} | all-to-all | bytes 524288 | tf_op jit(solution)/shard_map/all_to_all | solution.py:394
  79.2 1.6 %advance.3 = (f32[1024,128]{1,0:T(8,128)S(1)}, bf16[1024,128]{1,0:T(8,128)(2,1)S(1)}, bf16[256,128]{1,0:T(8,128)(2,1)S(1)}, bf16[256,128]{1,0:T(8,128)(2,1)S(1)}) custom-call(f32[32,16,128]{2,1,0:T(8,128)S(1)} %all_to_all.38.received_ref, f32[1,128]{1,0:T(1,128)S(1)} %bitcast.2, bf16[1024,128]{1,0:T(8,128)(2,1)S(1)} %copy-done.4, ...), custom_call_target="tpu_custom_call" | custom-call | bytes 16777216 | tf_op jit(solution)/shard_map/advance/pallas_call | solution.py:33
  80.8 3.9 %collective-permute-start.2 = (bf16[256,128]{1,0:T(8,128)(2,1)S(1)}, bf16[256,128]{1,0:T(8,128)(2,1)S(1)}, u32[]{:S(2)}, u32[]{:S(2)}) collective-permute-start(bf16[256,128]{1,0:T(8,128)(2,1)S(1)} %get-tuple-element.46), channel_id=1, source_target_pairs={{0,1},{1,2},{2,3},{3,4},{4,5},{5,6},{6,7},{7,8},{8,9},{9,10},{10,1... | collective-permute-start | bytes 196616 | tf_op jit(solution)/shard_map/ppermute | solution.py:432
  84.7 0.7 inner_classes.1
  86.0 2.4 %collective-permute-done.3.after_ref = bf16[256,128]{1,0:T(8,128)(2,1)S(1)} collective-permute-done((bf16[256,128]{1,0:T(8,128)(2,1)S(1)}, bf16[256,128]{1,0:T(8,128)(2,1)S(1)}, u32[]{:S(2)}, u32[]{:S(2)}) %collective-permute-start.3) | collective-permute-done | bytes 65568 | tf_op jit(solution)/shard_map/ppermute | solution.py:433
  88.4 0.6 residual_terms.3
  89.0 12.5 %all_to_all.39.received_ref = f32[8,16,128]{2,1,0:T(8,128)S(1)} all-to-all(f32[8,16,128]{2,1,0:T(8,128)S(1)} %get-tuple-element.48), channel_id=1, replica_groups=mesh['sub'=32,'load'=8] {'load'}, dimensions={0} | all-to-all | bytes 131072 | tf_op jit(solution)/shard_map/all_to_all | solution.py:394
  101.7 17.3 %all_to_all.40.received_ref = f32[32,16,128]{2,1,0:T(8,128)S(1)} all-to-all(f32[32,16,128]{2,1,0:T(8,128)S(1)} %later_partial.1), channel_id=1, replica_groups=mesh['sub'=32,'load'=8] {'sub'}, dimensions={0} | all-to-all | bytes 524288 | tf_op jit(solution)/shard_map/all_to_all | solution.py:394
  119.0 2.3 %gradients.1 = (f32[1,1024,128]{2,1,0:T(8,128)}, f32[32,16,128]{2,1,0:T(8,128)S(1)}) custom-call(f32[32,16,128]{2,1,0:T(8,128)S(1)} %all_to_all.40.received_ref, f32[1,128]{1,0:T(1,128)S(1)} %bitcast.3, bf16[1024,128]{1,0:T(8,128)(2,1)S(1)} %copy-done.4, f32[1024,128]{1,0:T(8,128)S(1)} %get-tuple-element.49.residual_ref, ...), custom_call_target="tpu_custom_call" | custom-call | bytes 16777216 | tf_op jit(solution)/shard_map/gradients/pallas_call | solution.py:33
  121.3 15.5 %all_to_all.41 = f32[32,16,128]{2,1,0:T(8,128)S(1)} all-to-all(f32[32,16,128]{2,1,0:T(8,128)S(1)} %get-tuple-element.52), channel_id=1, replica_groups=mesh['sub'=32,'load'=8] {'sub'}, dimensions={0} | all-to-all | bytes 524288 | tf_op jit(solution)/shard_map/all_to_all | solution.py:394
  136.9 5.6 %collective-permute-start.5 = (f32[16,128]{1,0:T(8,128)S(1)}, f32[16,128]{1,0:T(8,128)S(1)}, u32[]{:S(2)}, u32[]{:S(2)}) collective-permute-start(f32[16,128]{1,0:T(8,128)S(1)} %reduce_sum.9.middle_ref), channel_id=1, source_target_pairs={{1,0},{2,1},{3,2},{4,3},{5,4},{6,5},{7,6},{9,8},{10,9},{11,10},{12... | collective-permute-start | bytes 24584 | tf_op jit(solution)/shard_map/ppermute | solution.py:368
  142.5 2.1 %collective-permute-start.4 = (f32[16,128]{1,0:T(8,128)S(1)}, f32[16,128]{1,0:T(8,128)S(1)}, u32[]{:S(2)}, u32[]{:S(2)}) collective-permute-start(f32[16,128]{1,0:T(8,128)S(1)} %reduce_sum.9.middle_ref), channel_id=1, source_target_pairs={{0,1},{1,2},{2,3},{3,4},{4,5},{5,6},{6,7},{8,9},{9,10},{10,11},{11... | collective-permute-start | bytes 24584 | tf_op jit(solution)/shard_map/ppermute | solution.py:368
  144.6 1.0 collective-permute-done.4.left_ref
  145.5 0.8 smooth.1
  (32 shorter events, 1.2 us)
Async XLA Ops:
  0.6 38.7 %copy-start.1 = (f32[1,1024,128]{2,1,0:T(8,128)S(1)}, f32[1,1024,128]{2,1,0:T(8,128)}, u32[]{:S(2)}) copy-start(f32[1,1024,128]{2,1,0:T(8,128)} %rhs_ref.3) | copy-start | bytes 1572868
  0.6 38.7 %copy-start.9 = (f32[128]{0:T(128)S(1)}, f32[128]{0:T(128)}, u32[]{:S(2)}) copy-start(f32[128]{0:T(128)} %param.16) | copy-start | bytes 1540
  4.6 34.8 %copy-start.2 = (bf16[512,1024]{1,0:T(8,128)(2,1)S(1)}, bf16[512,1024]{1,0:T(8,128)(2,1)}, u32[]{:S(2)}) copy-start(bf16[512,1024]{1,0:T(8,128)(2,1)} %get-tuple-element.32.send_ref) | copy-start | bytes 3145732
  4.6 34.8 %copy-start.4 = (bf16[1024,128]{1,0:T(8,128)(2,1)S(1)}, bf16[1024,128]{1,0:T(8,128)(2,1)}, u32[]{:S(2)}) copy-start(bf16[1024,128]{1,0:T(8,128)(2,1)} %get-tuple-element.30.lifted_ref) | copy-start | bytes 786436
  17.8 27.1 %copy-start.10 = (s32[1,1024]{1,0:T(1,128)S(1)}, s32[1,1024]{1,0:T(1,128)}, u32[]{:S(2)}) copy-start(s32[1,1024]{1,0:T(1,128)} %partner_ref.1) | copy-start | bytes 12292
  41.0 5.5 %collective-permute-start = (bf16[256,128]{1,0:T(8,128)(2,1)S(1)}, bf16[256,128]{1,0:T(8,128)(2,1)S(1)}, u32[]{:S(2)}, u32[]{:S(2)}) collective-permute-start(bf16[256,128]{1,0:T(8,128)(2,1)S(1)} %get-tuple-element.36), channel_id=1, source_target_pairs={{0,1},{1,2},{2,3},{3,4},{4,5},{5,6},{6,7},{7,8},{8,9},{9,10},{10,1... | collective-permute-start | bytes 196616 | tf_op jit(solution)/shard_map/ppermute | solution.py:432
  44.8 3.7 %collective-permute-start.1 = (bf16[256,128]{1,0:T(8,128)(2,1)S(1)}, bf16[256,128]{1,0:T(8,128)(2,1)S(1)}, u32[]{:S(2)}, u32[]{:S(2)}) collective-permute-start(bf16[256,128]{1,0:T(8,128)(2,1)S(1)} %get-tuple-element.37), channel_id=1, source_target_pairs={{1,0},{2,1},{3,2},{4,3},{5,4},{6,5},{7,6},{8,7},{9,8},{10,9},{11,1... | collective-permute-start | bytes 196616 | tf_op jit(solution)/shard_map/ppermute | solution.py:433
  44.9 3.7 %copy-start.7 = (bf16[1,12,1024]{2,1,0:T(8,128)(2,1)S(1)}, bf16[1,12,1024]{2,1,0:T(8,128)(2,1)}, u32[]{:S(2)}) copy-start(bf16[1,12,1024]{2,1,0:T(8,128)(2,1)} %basis_ref.3) | copy-start | bytes 73732
  44.9 3.7 %copy-start.8 = (s32[8,128]{1,0:T(8,128)S(1)}, s32[8,128]{1,0:T(8,128)}, u32[]{:S(2)}) copy-start(s32[8,128]{1,0:T(8,128)} %class_ref.7) | copy-start | bytes 12292
  46.4 32.7 %copy-start = (bf16[1,1024,1024]{2,1,0:T(8,128)(2,1)S(1)}, bf16[1,1024,1024]{2,1,0:T(8,128)(2,1)}, u32[]{:S(2)}) copy-start(bf16[1,1024,1024]{2,1,0:T(8,128)(2,1)} %operator_ref.1) | copy-start | bytes 6291460
  80.8 5.2 %collective-permute-start.2 = (bf16[256,128]{1,0:T(8,128)(2,1)S(1)}, bf16[256,128]{1,0:T(8,128)(2,1)S(1)}, u32[]{:S(2)}, u32[]{:S(2)}) collective-permute-start(bf16[256,128]{1,0:T(8,128)(2,1)S(1)} %get-tuple-element.46), channel_id=1, source_target_pairs={{0,1},{1,2},{2,3},{3,4},{4,5},{5,6},{6,7},{7,8},{8,9},{9,10},{10,1... | collective-permute-start | bytes 196616 | tf_op jit(solution)/shard_map/ppermute | solution.py:432
  84.7 3.7 %collective-permute-start.3 = (bf16[256,128]{1,0:T(8,128)(2,1)S(1)}, bf16[256,128]{1,0:T(8,128)(2,1)S(1)}, u32[]{:S(2)}, u32[]{:S(2)}) collective-permute-start(bf16[256,128]{1,0:T(8,128)(2,1)S(1)} %get-tuple-element.47), channel_id=1, source_target_pairs={{1,0},{2,1},{3,2},{4,3},{5,4},{6,5},{7,6},{8,7},{9,8},{10,9},{11,1... | collective-permute-start | bytes 196616 | tf_op jit(solution)/shard_map/ppermute | solution.py:433
  85.4 33.6 %copy-start.3 = (bf16[1,1536,1024]{2,1,0:T(8,128)(2,1)S(1)}, bf16[1,1536,1024]{2,1,0:T(8,128)(2,1)}, u32[]{:S(2)}) copy-start(bf16[1,1536,1024]{2,1,0:T(8,128)(2,1)} %recovery_ref.1) | copy-start | bytes 9437188
  85.4 33.6 %copy-start.5 = (bf16[1,1536,128]{2,1,0:T(8,128)(2,1)S(1)}, bf16[1,1536,128]{2,1,0:T(8,128)(2,1)}, u32[]{:S(2)}) copy-start(bf16[1,1536,128]{2,1,0:T(8,128)(2,1)} %base_ref.1) | copy-start | bytes 1179652
  85.4 33.6 %copy-start.6 = (bf16[1,1536,128]{2,1,0:T(8,128)(2,1)S(1)}, bf16[1,1536,128]{2,1,0:T(8,128)(2,1)}, u32[]{:S(2)}) copy-start(bf16[1,1536,128]{2,1,0:T(8,128)(2,1)} %adjoint_ref.1) | copy-start | bytes 1179652
  85.5 33.6 %copy-start.11 = (s32[1,128]{1,0:T(1,128)S(1)}, s32[1,128]{1,0:T(1,128)}, u32[]{:S(2)}) copy-start(s32[1,128]{1,0:T(1,128)} %voxel_ref.1) | copy-start | bytes 1540
  136.9 7.7 %collective-permute-start.5 = (f32[16,128]{1,0:T(8,128)S(1)}, f32[16,128]{1,0:T(8,128)S(1)}, u32[]{:S(2)}, u32[]{:S(2)}) collective-permute-start(f32[16,128]{1,0:T(8,128)S(1)} %reduce_sum.9.middle_ref), channel_id=1, source_target_pairs={{1,0},{2,1},{3,2},{4,3},{5,4},{6,5},{7,6},{9,8},{10,9},{11,10},{12... | collective-permute-start | bytes 24584 | tf_op jit(solution)/shard_map/ppermute | solution.py:368
  142.5 3.1 %collective-permute-start.4 = (f32[16,128]{1,0:T(8,128)S(1)}, f32[16,128]{1,0:T(8,128)S(1)}, u32[]{:S(2)}, u32[]{:S(2)}) collective-permute-start(f32[16,128]{1,0:T(8,128)S(1)} %reduce_sum.9.middle_ref), channel_id=1, source_target_pairs={{0,1},{1,2},{2,3},{3,4},{4,5},{5,6},{6,7},{8,9},{9,10},{10,11},{11... | collective-permute-start | bytes 24584 | tf_op jit(solution)/shard_map/ppermute | solution.py:368

commit v7 on v5

--- a/solution.py
+++ b/solution.py
@@ -16,7 +16,6 @@
 COLS = 128
 UNKNOWNS = 1536
 EDGE = 256
-MARK = 120
 FIRST = 60
 PART = 50
 ENTRIES = SUB * LOAD * SPOTS
@@ -29,11 +28,12 @@
 BF16 = jnp.bfloat16
 
 
-def call(kernel, outs, operands, name, flops=0, moved=16 * 2**20, limit=16, scratch=(), far=()):
+def call(kernel, outs, operands, name, flops=0, moved=16 * 2**20, limit=16, scratch=(), far=(), far_out=()):
     vmem, hbm = pl.BlockSpec(memory_space=pltpu.VMEM), pl.BlockSpec(memory_space=pltpu.HBM)
     return pl.pallas_call(
         kernel,
         in_specs=[hbm if place in far else vmem for place in range(len(operands))],
+        out_specs=[hbm if place in far_out else vmem for place in range(len(outs))],
         out_shape=[jax.ShapeDtypeStruct(shape, dtype) for shape, dtype in outs],
         scratch_shapes=list(scratch),
         compiler_params=pltpu.CompilerParams(vmem_limit_bytes=int(limit * 2**20)),
@@ -107,24 +107,27 @@
     copies[0].wait()
     inverse = inverse_ref[...]
     inverse = jnp.concatenate([inverse, inverse[:, :128]], axis=1)
-    lanes = lanes_of((8, COLS))
-    lane = lanes_of((1, COLS))
-    spares = []
-    for peer in range(SUB):
-        start = peer * LOAD * MODES
+    pieces = []
+    for group in range(SUB):
+        start = group * LOAD * MODES
         tile, offset = start // 128, start % 128
         piece = inverse[:, 128 * tile : 128 * tile + 256]
         if offset:
             piece = pltpu.roll(piece, 256 - offset, axis=1)
-        piece = piece[:, :128]
-        last = piece[8:12]
-        beside = jnp.concatenate([pltpu.roll(last, 96, axis=1), pltpu.roll(last, 64, axis=1)], axis=0)
-        spare = pltpu.roll(last[0:1], 64, axis=1)
-        for place, turn in ((1, 96), (2, 0), (3, 32)):
-            part = last[place : place + 1]
-            spare = jnp.where(lane < 32 * place, spare, pltpu.roll(part, turn, axis=1) if turn else part)
-        out_ref[peer, 16:, :] = jnp.where(lanes < 96, piece[:8], beside)
-        spares.append(spare)
+        pieces.append(piece[:, :128])
+    lanes = lanes_of((MODES, COLS))
+    masks = [(lanes >= 16 * slot) & (lanes < 16 * slot + MODES) for slot in range(8)]
+    for peer in range(LOAD):
+        tiles = []
+        for tile in range(4):
+            chosen = jnp.zeros((MODES, COLS), F32)
+            for slot in range(8):
+                turn = (16 * slot - MODES * peer) % 128
+                piece = pieces[8 * tile + slot]
+                piece = pltpu.roll(piece, turn, axis=1) if turn else piece
+                chosen = jnp.where(masks[slot], piece, chosen)
+            tiles.append(chosen)
+        out_ref[peer, 16:, :] = jnp.concatenate(tiles, axis=0)
     copies[3].wait()
     edge_rows(partner_ref[...].astype(F32), send_ref)
     copies[1].wait()
@@ -133,41 +136,32 @@
     lifted_ref[...] = basis.astype(BF16)
     copies[2].wait()
     rows = coarse_rows(basis_ref, rhs_ref[0])
-    row = rows_of(rows.shape)
-    for peer in range(SUB):
-        out_ref[peer, :16, :] = jnp.where(row == 15, spares[peer], rows)
+    for peer in range(LOAD):
+        out_ref[peer, :16, :] = rows
 
 
 def partial_rows(high, low, terms, out_ref):
     terms_high, terms_low = split2(terms)
     partial = dot(high, terms_high) + dot(high, terms_low) + dot(low, terms_high)
-    last = jnp.concatenate([partial[MARK : MARK + 1], jnp.zeros((3, COLS), F32)], axis=0)
-    for peer in range(LOAD):
-        out_ref[peer] = jnp.concatenate([partial[MODES * peer : MODES * peer + MODES], last], axis=0)
-
-
-def first_partial(
-    received_ref, operator_hbm, out_ref, block_ref, operator_ref, operator_sem
-):
+    out_ref[...] = partial.reshape(out_ref.shape)
+
+
+def first_partial(received_ref, operator_hbm, out_ref, block_ref, operator_ref, operator_sem):
     copy = pltpu.make_async_copy(operator_hbm, operator_ref, operator_sem)
     copy.start()
-    terms = received_ref[:, :16, :].reshape(SUB * 16, COLS)
-    packed = received_ref[:, 16:, :].reshape(SUB * 8, COLS)
-    lanes = lanes_of((SUB * 8, COLS))
-    upper = jnp.where(lanes < 96, packed, 0.0).reshape(SUB, 8, COLS)
-    first = pltpu.roll(packed, 32, axis=1).reshape(SUB, 8, COLS)[:, :4]
-    second = pltpu.roll(packed, 64, axis=1).reshape(SUB, 8, COLS)[:, 4:]
-    spare = received_ref[:, 15, :]
-    third = [pltpu.roll(spare, 64, axis=1), pltpu.roll(spare, 32, axis=1), spare, pltpu.roll(spare, 96, axis=1)]
-    third = jnp.concatenate([part.reshape(SUB, 1, COLS) for part in third], axis=1)
-    lanes = lax.broadcasted_iota(jnp.int32, (SUB, 4, COLS), 2)
-    lower = jnp.where(lanes < 32, first, jnp.where(lanes < 64, second, jnp.where(lanes < 96, third, 0.0)))
-    places = lax.broadcasted_iota(jnp.int32, (SUB, 4, COLS), 1)
-    mark = jnp.where((places == 0) & (lanes == MARK), 1.0, 0.0)
-    block = jnp.concatenate([upper, jnp.concatenate([lower, mark], axis=1)], axis=1)
-    high, low = split2(block.reshape(SUB * 16, COLS).T)
+    terms = received_ref[:, :16, :].reshape(LOAD * 16, COLS)
+    lanes = lax.broadcasted_iota(jnp.int32, (LOAD, 4, COLS), 2)
+    places = lax.broadcasted_iota(jnp.int32, (LOAD, 4, COLS), 1)
+    mark = jnp.where((places == 0) & (lanes % 16 == MODES), 1.0, 0.0)
+    tiles = []
+    for tile in range(4):
+        start = 16 + MODES * tile
+        rows = jnp.concatenate([received_ref[:, start : start + MODES, :], mark], axis=1)
+        tiles.append(rows.reshape(LOAD * 16, COLS))
+    high, low = split2(jnp.concatenate(tiles, axis=1))
     block_ref[:, : SUB * 16] = high
     block_ref[:, SUB * 16 :] = low
+    high, low = split2(jnp.concatenate([tile.T for tile in tiles], axis=0))
     partial_rows(high, low, terms, out_ref)
     copy.wait()
 
@@ -232,9 +226,7 @@
 
 
 def step_parts(received_ref, damping_ref, lifted_ref):
-    total = received_ref[0]
-    for peer in range(1, LOAD):
-        total = total + received_ref[peer]
+    total = jnp.sum(received_ref[...], axis=0)
     step = damping_ref[...] / jnp.sqrt(total[MODES : MODES + 1] / ENTRIES + EPSILON)
     correction = jnp.where(rows_of(total.shape) < MODES, total, 0.0)
     stacked = jnp.concatenate(split3(correction) + (jnp.zeros((COLS - 48, COLS), BF16),), axis=0)
@@ -300,12 +292,16 @@
     base_ref,
     adjoint_ref,
     voxel_ref,
+    multipliers_hbm,
+    out_ref,
     multipliers_ref,
-    out_ref,
+    multipliers_sem,
 ):
     step, lifted = step_parts(received_ref, damping_ref, lifted_ref)
     multipliers = iterate_ref[...] + step * (residual_ref[...] - lifted)
     multipliers_ref[0] = multipliers
+    copy = pltpu.make_async_copy(multipliers_ref, multipliers_hbm, multipliers_sem)
+    copy.start()
     displaced = base_ref[0].astype(F32) - dot(recovery_ref[0], multipliers.astype(BF16))
     products = displaced * adjoint_ref[0].astype(F32)
     first = EDOF * rows_of((128, UNKNOWNS))
@@ -322,6 +318,7 @@
     spread = parts[:, :COLS] + parts[:, COLS : 2 * COLS] + parts[:, 2 * COLS :]
     for peer in range(SUB):
         out_ref[peer] = spread[8 * peer : 8 * peer + 16]
+    copy.wait()
 
 
 def smooth(middle_ref, left_ref, right_ref, classes_ref, out_ref):
@@ -386,7 +383,7 @@
 
     sent, send, lifted = call(
         first_terms,
-        [((SUB, 24, COLS), F32), ((2 * EDGE, SPOTS), BF16), ((SPOTS, COLS), BF16)],
+        [((LOAD, 64, COLS), F32), ((2 * EDGE, SPOTS), BF16), ((SPOTS, COLS), BF16)],
         (dual_rhs, coarse_basis, coarse_inverse, partner),
         "first_terms",
         scratch=[
@@ -399,10 +396,10 @@
         far=(0, 1, 2, 3),
         limit=FIRST,
     )
-    received = over(sent, "sub")
+    received = over(sent, "load")
     partial, block, operator = call(
         first_partial,
-        [to_load, ((COLS, 2 * SUB * 16), BF16), (dual_ops.shape, BF16)],
+        [to_sub, ((COLS, 2 * SUB * 16), BF16), (dual_ops.shape, BF16)],
         (received, dual_ops),
         "first_partial",
         scratch=[pltpu.SemaphoreType.DMA],
@@ -412,7 +409,7 @@
     residual = dual_rhs
     before = ()
     for iteration in range(2):
-        received = over(partial, "load")
+        received = over(partial, "load" if iteration else "sub")
         iterate, images, lower, upper = call(
             functools.partial(advance, iteration == 0),
             [tall, ((SPOTS, COLS), BF16), edge, edge],
@@ -451,6 +448,8 @@
         [((1, SPOTS, COLS), F32), to_sub],
         (received, damping, lifted, residual, iterate, recovery, base_disp, adjoint, elem_voxel),
         "gradients",
+        scratch=[pltpu.VMEM((1, SPOTS, COLS), F32), pltpu.SemaphoreType.DMA],
+        far_out=(0,),
     )
     middle = jnp.sum(over(sent, "sub"), axis=0)
     left, right = both_ways(middle, "load", LOAD, False)

time: 143 us -> 142 us (level)
  blocking collectives: 110 us -> 106 us
  starting transfers between devices: 9.71 us -> 12.5 us
    all_to_all x7, blocking collectives: 110 us -> 106 us  [over(): return lax.all_to_all(value, axis, 0, 0, tiled=True)]
    ppermute x2, starting transfers between devices: 2.05 us -> 4.89 us  [on_device(): from_before = lax.ppermute(upper, whole, up)]
where the time goes in v7:
time: 142 us
  blocking collectives  106 us (75%)
  Pallas kernels  15.8 us (11%)
  starting transfers between devices  12.5 us (9%)
  waiting for transfers between devices  5.97 us (4%)
    all_to_all x7, blocking collectives, over(): return lax.all_to_all(value, axis, 0, 0, tiled=True)  106 us
    pallas_call x12, Pallas kernels, call(): pl.pallas_call(kernel, in_specs=[hbm if place in far else vmem for place...  15.8 us
    ppermute x2, starting transfers between devices, both_ways(): return (lax.ppermute(value, axes, up), lax.ppermute(value, axes, down))  7.66 us
    ppermute x2, starting transfers between devices, on_device(): from_before = lax.ppermute(upper, whole, up)  4.89 us
    ppermute x2, waiting for transfers between devices, on_device(): from_after = lax.ppermute(lower, whole, down)  4.44 us
  transfers between devices with their start and end apart: 6, of which 4 were waited for; matrix products, arithmetic and copies ran while one was open for 0% of the time, Pallas kernels for 2%

profile of v7, /device:TPU:1, one launch (start us, length us, event | category | flops | bytes accessed | tf_op | source)
XLA Modules:
  0.0 141.7 jit_solution(17761035304310821110)
XLA Ops:
  0.7 3.9 %first_terms.1 = (f32[8,64,128]{2,1,0:T(8,128)}, bf16[512,1024]{1,0:T(8,128)(2,1)}, bf16[1024,128]{1,0:T(8,128)(2,1)}) custom-call(f32[1,1024,128]{2,1,0:T(8,128)} %rhs_ref.3, bf16[1,12,1024]{2,1,0:T(8,128)(2,1)} %basis_ref.3, f32[12,3072]{1,0:T(8,128)} %inverse_hbm.1, s32[1,1024]{1,0:T(1,128)} %partner_ref.1), custom_call_target="tpu_custom_call" | custom-call | bytes 16777216 | tf_op jit(solution)/shard_map/first_terms/pallas_call | solution.py:33
  4.6 13.2 %all_to_all.35.received_ref = f32[8,64,128]{2,1,0:T(8,128)S(1)} all-to-all(f32[8,64,128]{2,1,0:T(8,128)} %get-tuple-element.28), channel_id=1, replica_groups=mesh['sub'=32,'load'=8] {'load'}, dimensions={0} | all-to-all | bytes 524288 | tf_op jit(solution)/shard_map/all_to_all | solution.py:382
  17.8 1.6 %first_partial.1 = (f32[32,16,128]{2,1,0:T(8,128)S(1)}, bf16[128,1024]{1,0:T(8,128)(2,1)S(1)}, bf16[1,1024,1024]{2,1,0:T(8,128)(2,1)S(1)}) custom-call(f32[8,64,128]{2,1,0:T(8,128)S(1)} %all_to_all.35.received_ref, bf16[1,1024,1024]{2,1,0:T(8,128)(2,1)} %operator_ref.1), custom_call_target="tpu_custom_call" | custom-call | bytes 16777216 | tf_op jit(solution)/shard_map/first_partial/pallas_call | solution.py:33
  19.4 19.9 %all_to_all.36.received_ref = f32[32,16,128]{2,1,0:T(8,128)S(1)} all-to-all(f32[32,16,128]{2,1,0:T(8,128)S(1)} %get-tuple-element.29), channel_id=1, replica_groups=mesh['sub'=32,'load'=8] {'sub'}, dimensions={0} | all-to-all | bytes 524288 | tf_op jit(solution)/shard_map/all_to_all | solution.py:382
  39.3 1.6 %advance.2 = (f32[1024,128]{1,0:T(8,128)S(1)}, bf16[1024,128]{1,0:T(8,128)(2,1)S(1)}, bf16[256,128]{1,0:T(8,128)(2,1)S(1)}, bf16[256,128]{1,0:T(8,128)(2,1)S(1)}) custom-call(f32[32,16,128]{2,1,0:T(8,128)S(1)} %all_to_all.36.received_ref, f32[1,128]{1,0:T(1,128)S(1)} %bitcast.1, bf16[1024,128]{1,0:T(8,128)(2,1)S(1)} %copy-done.4, ...), custom_call_target="tpu_custom_call" | custom-call | bytes 16777216 | tf_op jit(solution)/shard_map/advance/pallas_call | solution.py:33
  41.0 3.9 %collective-permute-start = (bf16[256,128]{1,0:T(8,128)(2,1)S(1)}, bf16[256,128]{1,0:T(8,128)(2,1)S(1)}, u32[]{:S(2)}, u32[]{:S(2)}) collective-permute-start(bf16[256,128]{1,0:T(8,128)(2,1)S(1)} %get-tuple-element.36), channel_id=1, source_target_pairs={{0,1},{1,2},{2,3},{3,4},{4,5},{5,6},{6,7},{7,8},{8,9},{9,10},{10,1... | collective-permute-start | bytes 196616 | tf_op jit(solution)/shard_map/ppermute | solution.py:420
  44.9 1.6 %first_inner.1 = (f32[1024,128]{1,0:T(8,128)S(1)}, bf16[1024,1536]{1,0:T(8,128)(2,1)S(1)}) custom-call(bf16[1024,128]{1,0:T(8,128)(2,1)S(1)} %get-tuple-element.33.images_ref, s32[1,1024]{1,0:T(1,128)S(1)} %copy-done.10), custom_call_target="tpu_custom_call" | custom-call | flops 2147483648 | bytes 8388608 | tf_op jit(solution)/shard_map/first_inner/pallas_call | solution.py:33
  46.5 2.1 %collective-permute-done.1.after_ref = bf16[256,128]{1,0:T(8,128)(2,1)S(1)} collective-permute-done((bf16[256,128]{1,0:T(8,128)(2,1)S(1)}, bf16[256,128]{1,0:T(8,128)(2,1)S(1)}, u32[]{:S(2)}, u32[]{:S(2)}) %collective-permute-start.1) | collective-permute-done | bytes 65568 | tf_op jit(solution)/shard_map/ppermute | solution.py:421
  48.5 0.6 residual_terms.2
  49.1 13.7 %all_to_all.37.received_ref = f32[32,16,128]{2,1,0:T(8,128)S(1)} all-to-all(f32[32,16,128]{2,1,0:T(8,128)S(1)} %get-tuple-element.38), channel_id=1, replica_groups=mesh['sub'=32,'load'=8] {'sub'}, dimensions={0} | all-to-all | bytes 524288 | tf_op jit(solution)/shard_map/all_to_all | solution.py:382
  63.1 16.1 %all_to_all.38.received_ref = f32[8,16,128]{2,1,0:T(8,128)S(1)} all-to-all(f32[8,16,128]{2,1,0:T(8,128)S(1)} %get-tuple-element.40), channel_id=1, replica_groups=mesh['sub'=32,'load'=8] {'load'}, dimensions={0} | all-to-all | bytes 131072 | tf_op jit(solution)/shard_map/all_to_all | solution.py:382
  79.2 1.6 %advance.3 = (f32[1024,128]{1,0:T(8,128)S(1)}, bf16[1024,128]{1,0:T(8,128)(2,1)S(1)}, bf16[256,128]{1,0:T(8,128)(2,1)S(1)}, bf16[256,128]{1,0:T(8,128)(2,1)S(1)}) custom-call(f32[8,16,128]{2,1,0:T(8,128)S(1)} %all_to_all.38.received_ref, f32[1,128]{1,0:T(1,128)S(1)} %bitcast.2, bf16[1024,128]{1,0:T(8,128)(2,1)S(1)} %copy-done.4, ...), custom_call_target="tpu_custom_call" | custom-call | bytes 16777216 | tf_op jit(solution)/shard_map/advance/pallas_call | solution.py:33
  80.8 1.0 collective-permute-start.2
  81.8 0.7 inner_classes.1
  83.2 2.4 %collective-permute-done.3.after_ref = bf16[256,128]{1,0:T(8,128)(2,1)S(1)} collective-permute-done((bf16[256,128]{1,0:T(8,128)(2,1)S(1)}, bf16[256,128]{1,0:T(8,128)(2,1)S(1)}, u32[]{:S(2)}, u32[]{:S(2)}) %collective-permute-start.3) | collective-permute-done | bytes 65568 | tf_op jit(solution)/shard_map/ppermute | solution.py:421
  85.5 0.6 residual_terms.3
  86.1 13.9 %all_to_all.39.received_ref = f32[32,16,128]{2,1,0:T(8,128)S(1)} all-to-all(f32[32,16,128]{2,1,0:T(8,128)S(1)} %get-tuple-element.48), channel_id=1, replica_groups=mesh['sub'=32,'load'=8] {'sub'}, dimensions={0} | all-to-all | bytes 524288 | tf_op jit(solution)/shard_map/all_to_all | solution.py:382
  100.3 15.9 %all_to_all.40.received_ref = f32[8,16,128]{2,1,0:T(8,128)S(1)} all-to-all(f32[8,16,128]{2,1,0:T(8,128)S(1)} %later_partial.1), channel_id=1, replica_groups=mesh['sub'=32,'load'=8] {'load'}, dimensions={0} | all-to-all | bytes 131072 | tf_op jit(solution)/shard_map/all_to_all | solution.py:382
  116.2 2.2 %gradients.1 = (f32[1,1024,128]{2,1,0:T(8,128)}, f32[32,16,128]{2,1,0:T(8,128)S(1)}) custom-call(f32[8,16,128]{2,1,0:T(8,128)S(1)} %all_to_all.40.received_ref, f32[1,128]{1,0:T(1,128)S(1)} %bitcast.3, bf16[1024,128]{1,0:T(8,128)(2,1)S(1)} %copy-done.4, f32[1024,128]{1,0:T(8,128)S(1)} %get-tuple-element.49.residual_ref, ...), custom_call_target="tpu_custom_call" | custom-call | bytes 16777216 | tf_op jit(solution)/shard_map/gradients/pallas_call | solution.py:33
  118.4 13.8 %all_to_all.41 = f32[32,16,128]{2,1,0:T(8,128)S(1)} all-to-all(f32[32,16,128]{2,1,0:T(8,128)S(1)} %get-tuple-element.52), channel_id=1, replica_groups=mesh['sub'=32,'load'=8] {'sub'}, dimensions={0} | all-to-all | bytes 524288 | tf_op jit(solution)/shard_map/all_to_all | solution.py:382
  132.3 5.6 %collective-permute-start.5 = (f32[16,128]{1,0:T(8,128)S(1)}, f32[16,128]{1,0:T(8,128)S(1)}, u32[]{:S(2)}, u32[]{:S(2)}) collective-permute-start(f32[16,128]{1,0:T(8,128)S(1)} %reduce_sum.9.middle_ref), channel_id=1, source_target_pairs={{1,0},{2,1},{3,2},{4,3},{5,4},{6,5},{7,6},{9,8},{10,9},{11,10},{12... | collective-permute-start | bytes 24584 | tf_op jit(solution)/shard_map/ppermute | solution.py:356
  137.9 2.1 %collective-permute-start.4 = (f32[16,128]{1,0:T(8,128)S(1)}, f32[16,128]{1,0:T(8,128)S(1)}, u32[]{:S(2)}, u32[]{:S(2)}) collective-permute-start(f32[16,128]{1,0:T(8,128)S(1)} %reduce_sum.9.middle_ref), channel_id=1, source_target_pairs={{0,1},{1,2},{2,3},{3,4},{4,5},{5,6},{6,7},{8,9},{9,10},{10,11},{11... | collective-permute-start | bytes 24584 | tf_op jit(solution)/shard_map/ppermute | solution.py:356
  140.0 1.0 collective-permute-done.4.left_ref
  140.9 0.8 smooth.1
  (32 shorter events, 1.2 us)
Async XLA Ops:
  0.6 38.7 %copy-start.1 = (f32[1,1024,128]{2,1,0:T(8,128)S(1)}, f32[1,1024,128]{2,1,0:T(8,128)}, u32[]{:S(2)}) copy-start(f32[1,1024,128]{2,1,0:T(8,128)} %rhs_ref.3) | copy-start | bytes 1572868
  0.6 38.7 %copy-start.9 = (f32[128]{0:T(128)S(1)}, f32[128]{0:T(128)}, u32[]{:S(2)}) copy-start(f32[128]{0:T(128)} %param.16) | copy-start | bytes 1540
  4.6 34.8 %copy-start.2 = (bf16[512,1024]{1,0:T(8,128)(2,1)S(1)}, bf16[512,1024]{1,0:T(8,128)(2,1)}, u32[]{:S(2)}) copy-start(bf16[512,1024]{1,0:T(8,128)(2,1)} %get-tuple-element.32.send_ref) | copy-start | bytes 3145732
  4.6 34.8 %copy-start.4 = (bf16[1024,128]{1,0:T(8,128)(2,1)S(1)}, bf16[1024,128]{1,0:T(8,128)(2,1)}, u32[]{:S(2)}) copy-start(bf16[1024,128]{1,0:T(8,128)(2,1)} %get-tuple-element.30.lifted_ref) | copy-start | bytes 786436
  17.8 27.1 %copy-start.10 = (s32[1,1024]{1,0:T(1,128)S(1)}, s32[1,1024]{1,0:T(1,128)}, u32[]{:S(2)}) copy-start(s32[1,1024]{1,0:T(1,128)} %partner_ref.1) | copy-start | bytes 12292
  41.0 5.5 %collective-permute-start = (bf16[256,128]{1,0:T(8,128)(2,1)S(1)}, bf16[256,128]{1,0:T(8,128)(2,1)S(1)}, u32[]{:S(2)}, u32[]{:S(2)}) collective-permute-start(bf16[256,128]{1,0:T(8,128)(2,1)S(1)} %get-tuple-element.36), channel_id=1, source_target_pairs={{0,1},{1,2},{2,3},{3,4},{4,5},{5,6},{6,7},{7,8},{8,9},{9,10},{10,1... | collective-permute-start | bytes 196616 | tf_op jit(solution)/shard_map/ppermute | solution.py:420
  44.8 3.7 %collective-permute-start.1 = (bf16[256,128]{1,0:T(8,128)(2,1)S(1)}, bf16[256,128]{1,0:T(8,128)(2,1)S(1)}, u32[]{:S(2)}, u32[]{:S(2)}) collective-permute-start(bf16[256,128]{1,0:T(8,128)(2,1)S(1)} %get-tuple-element.37), channel_id=1, source_target_pairs={{1,0},{2,1},{3,2},{4,3},{5,4},{6,5},{7,6},{8,7},{9,8},{10,9},{11,1... | collective-permute-start | bytes 196616 | tf_op jit(solution)/shard_map/ppermute | solution.py:421
  44.9 3.7 %copy-start.7 = (bf16[1,12,1024]{2,1,0:T(8,128)(2,1)S(1)}, bf16[1,12,1024]{2,1,0:T(8,128)(2,1)}, u32[]{:S(2)}) copy-start(bf16[1,12,1024]{2,1,0:T(8,128)(2,1)} %basis_ref.3) | copy-start | bytes 73732
  44.9 3.7 %copy-start.8 = (s32[8,128]{1,0:T(8,128)S(1)}, s32[8,128]{1,0:T(8,128)}, u32[]{:S(2)}) copy-start(s32[8,128]{1,0:T(8,128)} %class_ref.5) | copy-start | bytes 12292
  46.4 32.7 %copy-start = (bf16[1,1024,1024]{2,1,0:T(8,128)(2,1)S(1)}, bf16[1,1024,1024]{2,1,0:T(8,128)(2,1)}, u32[]{:S(2)}) copy-start(bf16[1,1024,1024]{2,1,0:T(8,128)(2,1)} %operator_ref.1) | copy-start | bytes 6291460
  80.8 2.4 %collective-permute-start.2 = (bf16[256,128]{1,0:T(8,128)(2,1)S(1)}, bf16[256,128]{1,0:T(8,128)(2,1)S(1)}, u32[]{:S(2)}, u32[]{:S(2)}) collective-permute-start(bf16[256,128]{1,0:T(8,128)(2,1)S(1)} %get-tuple-element.46), channel_id=1, source_target_pairs={{0,1},{1,2},{2,3},{3,4},{4,5},{5,6},{6,7},{7,8},{8,9},{9,10},{10,1... | collective-permute-start | bytes 196616 | tf_op jit(solution)/shard_map/ppermute | solution.py:420
  81.8 3.7 %collective-permute-start.3 = (bf16[256,128]{1,0:T(8,128)(2,1)S(1)}, bf16[256,128]{1,0:T(8,128)(2,1)S(1)}, u32[]{:S(2)}, u32[]{:S(2)}) collective-permute-start(bf16[256,128]{1,0:T(8,128)(2,1)S(1)} %get-tuple-element.47), channel_id=1, source_target_pairs={{1,0},{2,1},{3,2},{4,3},{5,4},{6,5},{7,6},{8,7},{9,8},{10,9},{11,1... | collective-permute-start | bytes 196616 | tf_op jit(solution)/shard_map/ppermute | solution.py:421
  82.5 33.6 %copy-start.3 = (bf16[1,1536,1024]{2,1,0:T(8,128)(2,1)S(1)}, bf16[1,1536,1024]{2,1,0:T(8,128)(2,1)}, u32[]{:S(2)}) copy-start(bf16[1,1536,1024]{2,1,0:T(8,128)(2,1)} %recovery_ref.1) | copy-start | bytes 9437188
  82.5 33.6 %copy-start.5 = (bf16[1,1536,128]{2,1,0:T(8,128)(2,1)S(1)}, bf16[1,1536,128]{2,1,0:T(8,128)(2,1)}, u32[]{:S(2)}) copy-start(bf16[1,1536,128]{2,1,0:T(8,128)(2,1)} %base_ref.1) | copy-start | bytes 1179652
  82.6 33.6 %copy-start.6 = (bf16[1,1536,128]{2,1,0:T(8,128)(2,1)S(1)}, bf16[1,1536,128]{2,1,0:T(8,128)(2,1)}, u32[]{:S(2)}) copy-start(bf16[1,1536,128]{2,1,0:T(8,128)(2,1)} %adjoint_ref.1) | copy-start | bytes 1179652
  82.6 33.6 %copy-start.11 = (s32[1,128]{1,0:T(1,128)S(1)}, s32[1,128]{1,0:T(1,128)}, u32[]{:S(2)}) copy-start(s32[1,128]{1,0:T(1,128)} %voxel_ref.1) | copy-start | bytes 1540
  132.3 7.7 %collective-permute-start.5 = (f32[16,128]{1,0:T(8,128)S(1)}, f32[16,128]{1,0:T(8,128)S(1)}, u32[]{:S(2)}, u32[]{:S(2)}) collective-permute-start(f32[16,128]{1,0:T(8,128)S(1)} %reduce_sum.9.middle_ref), channel_id=1, source_target_pairs={{1,0},{2,1},{3,2},{4,3},{5,4},{6,5},{7,6},{9,8},{10,9},{11,10},{12... | collective-permute-start | bytes 24584 | tf_op jit(solution)/shard_map/ppermute | solution.py:356
  137.9 3.1 %collective-permute-start.4 = (f32[16,128]{1,0:T(8,128)S(1)}, f32[16,128]{1,0:T(8,128)S(1)}, u32[]{:S(2)}, u32[]{:S(2)}) collective-permute-start(f32[16,128]{1,0:T(8,128)S(1)} %reduce_sum.9.middle_ref), channel_id=1, source_target_pairs={{0,1},{1,2},{2,3},{3,4},{4,5},{5,6},{6,7},{8,9},{9,10},{10,11},{11... | collective-permute-start | bytes 24584 | tf_op jit(solution)/shard_map/ppermute | solution.py:356

commit v8 on v7

--- a/solution.py
+++ b/solution.py
@@ -84,18 +84,31 @@
     basis_hbm,
     inverse_hbm,
     partner_hbm,
-    out_ref,
-    send_ref,
-    lifted_ref,
+    out_hbm,
+    send_hbm,
+    lifted_hbm,
     rhs_ref,
     basis_ref,
     inverse_ref,
     partner_ref,
+    out_ref,
+    send_ref,
+    lifted_ref,
     rhs_sem,
     basis_sem,
     inverse_sem,
     partner_sem,
+    rows_sem,
+    tiles_sem,
+    send_sem,
+    lifted_sem,
 ):
+    results = [
+        pltpu.make_async_copy(out_ref.at[:, pl.ds(16, 48), :], out_hbm.at[:, pl.ds(16, 48), :], tiles_sem),
+        pltpu.make_async_copy(send_ref, send_hbm, send_sem),
+        pltpu.make_async_copy(lifted_ref, lifted_hbm, lifted_sem),
+        pltpu.make_async_copy(out_ref.at[:, pl.ds(0, 16), :], out_hbm.at[:, pl.ds(0, 16), :], rows_sem),
+    ]
     copies = [
         pltpu.make_async_copy(inverse_hbm, inverse_ref, inverse_sem),
         pltpu.make_async_copy(basis_hbm, basis_ref, basis_sem),
@@ -128,16 +141,22 @@
                 chosen = jnp.where(masks[slot], piece, chosen)
             tiles.append(chosen)
         out_ref[peer, 16:, :] = jnp.concatenate(tiles, axis=0)
+    results[0].start()
     copies[3].wait()
     edge_rows(partner_ref[...].astype(F32), send_ref)
+    results[1].start()
     copies[1].wait()
     basis = padded_basis(basis_ref, COLS).T
     basis = basis + pltpu.roll(basis, 16, axis=1) + pltpu.roll(basis, 32, axis=1)
     lifted_ref[...] = basis.astype(BF16)
+    results[2].start()
     copies[2].wait()
     rows = coarse_rows(basis_ref, rhs_ref[0])
     for peer in range(LOAD):
         out_ref[peer, :16, :] = rows
+    results[3].start()
+    for copy in results:
+        copy.wait()
 
 
 def partial_rows(high, low, terms, out_ref):
@@ -391,9 +410,13 @@
             pltpu.VMEM(coarse_basis.shape, BF16),
             pltpu.VMEM(coarse_inverse.shape, F32),
             pltpu.VMEM(partner.shape, jnp.int32),
+            pltpu.VMEM((LOAD, 64, COLS), F32),
+            pltpu.VMEM((2 * EDGE, SPOTS), BF16),
+            pltpu.VMEM((SPOTS, COLS), BF16),
         ]
-        + [pltpu.SemaphoreType.DMA] * 4,
+        + [pltpu.SemaphoreType.DMA] * 8,
         far=(0, 1, 2, 3),
+        far_out=(0, 1, 2),
         limit=FIRST,
     )
     received = over(sent, "load")

time: 142 us -> 142 us (level)
  no operation moved by 1% of the time
where the time goes in v8:
time: 142 us
  blocking collectives  106 us (75%)
  Pallas kernels  15.6 us (11%)
  starting transfers between devices  12.5 us (9%)
  waiting for transfers between devices  5.97 us (4%)
    all_to_all x7, blocking collectives, over(): return lax.all_to_all(value, axis, 0, 0, tiled=True)  106 us
    pallas_call x12, Pallas kernels, call(): pl.pallas_call(kernel, in_specs=[hbm if place in far else vmem for place...  15.6 us
    ppermute x2, starting transfers between devices, both_ways(): return (lax.ppermute(value, axes, up), lax.ppermute(value, axes, down))  7.65 us
    ppermute x2, starting transfers between devices, on_device(): from_before = lax.ppermute(upper, whole, up)  4.89 us
    ppermute x2, waiting for transfers between devices, on_device(): from_after = lax.ppermute(lower, whole, down)  4.44 us
  transfers between devices with their start and end apart: 6, of which 4 were waited for; matrix products, arithmetic and copies ran while one was open for 0% of the time, Pallas kernels for 2%

profile of v8, /device:TPU:1, one launch (start us, length us, event | category | flops | bytes accessed | tf_op | source)
XLA Modules:
  0.0 141.5 jit_solution(18223325083850238551)
XLA Ops:
  0.7 3.7 %first_terms.1 = (f32[8,64,128]{2,1,0:T(8,128)}, bf16[512,1024]{1,0:T(8,128)(2,1)}, bf16[1024,128]{1,0:T(8,128)(2,1)}) custom-call(f32[1,1024,128]{2,1,0:T(8,128)} %rhs_ref.3, bf16[1,12,1024]{2,1,0:T(8,128)(2,1)} %basis_ref.3, f32[12,3072]{1,0:T(8,128)} %inverse_hbm.1, s32[1,1024]{1,0:T(1,128)} %partner_ref.1), custom_call_target="tpu_custom_call" | custom-call | bytes 16777216 | tf_op jit(solution)/shard_map/first_terms/pallas_call | solution.py:33
  4.4 13.2 %all_to_all.35.received_ref = f32[8,64,128]{2,1,0:T(8,128)S(1)} all-to-all(f32[8,64,128]{2,1,0:T(8,128)} %get-tuple-element.28), channel_id=1, replica_groups=mesh['sub'=32,'load'=8] {'load'}, dimensions={0} | all-to-all | bytes 524288 | tf_op jit(solution)/shard_map/all_to_all | solution.py:401
  17.6 1.6 %first_partial.1 = (f32[32,16,128]{2,1,0:T(8,128)S(1)}, bf16[128,1024]{1,0:T(8,128)(2,1)S(1)}, bf16[1,1024,1024]{2,1,0:T(8,128)(2,1)S(1)}) custom-call(f32[8,64,128]{2,1,0:T(8,128)S(1)} %all_to_all.35.received_ref, bf16[1,1024,1024]{2,1,0:T(8,128)(2,1)} %operator_ref.1), custom_call_target="tpu_custom_call" | custom-call | bytes 16777216 | tf_op jit(solution)/shard_map/first_partial/pallas_call | solution.py:33
  19.2 19.9 %all_to_all.36.received_ref = f32[32,16,128]{2,1,0:T(8,128)S(1)} all-to-all(f32[32,16,128]{2,1,0:T(8,128)S(1)} %get-tuple-element.29), channel_id=1, replica_groups=mesh['sub'=32,'load'=8] {'sub'}, dimensions={0} | all-to-all | bytes 524288 | tf_op jit(solution)/shard_map/all_to_all | solution.py:401
  39.1 1.6 %advance.2 = (f32[1024,128]{1,0:T(8,128)S(1)}, bf16[1024,128]{1,0:T(8,128)(2,1)S(1)}, bf16[256,128]{1,0:T(8,128)(2,1)S(1)}, bf16[256,128]{1,0:T(8,128)(2,1)S(1)}) custom-call(f32[32,16,128]{2,1,0:T(8,128)S(1)} %all_to_all.36.received_ref, f32[1,128]{1,0:T(1,128)S(1)} %bitcast.1, bf16[1024,128]{1,0:T(8,128)(2,1)S(1)} %copy-done.4, ...), custom_call_target="tpu_custom_call" | custom-call | bytes 16777216 | tf_op jit(solution)/shard_map/advance/pallas_call | solution.py:33
  40.8 3.9 %collective-permute-start = (bf16[256,128]{1,0:T(8,128)(2,1)S(1)}, bf16[256,128]{1,0:T(8,128)(2,1)S(1)}, u32[]{:S(2)}, u32[]{:S(2)}) collective-permute-start(bf16[256,128]{1,0:T(8,128)(2,1)S(1)} %get-tuple-element.36), channel_id=1, source_target_pairs={{0,1},{1,2},{2,3},{3,4},{4,5},{5,6},{6,7},{7,8},{8,9},{9,10},{10,1... | collective-permute-start | bytes 196616 | tf_op jit(solution)/shard_map/ppermute | solution.py:443
  44.7 1.6 %first_inner.1 = (f32[1024,128]{1,0:T(8,128)S(1)}, bf16[1024,1536]{1,0:T(8,128)(2,1)S(1)}) custom-call(bf16[1024,128]{1,0:T(8,128)(2,1)S(1)} %get-tuple-element.33.images_ref, s32[1,1024]{1,0:T(1,128)S(1)} %copy-done.10), custom_call_target="tpu_custom_call" | custom-call | flops 2147483648 | bytes 8388608 | tf_op jit(solution)/shard_map/first_inner/pallas_call | solution.py:33
  46.2 2.1 %collective-permute-done.1.after_ref = bf16[256,128]{1,0:T(8,128)(2,1)S(1)} collective-permute-done((bf16[256,128]{1,0:T(8,128)(2,1)S(1)}, bf16[256,128]{1,0:T(8,128)(2,1)S(1)}, u32[]{:S(2)}, u32[]{:S(2)}) %collective-permute-start.1) | collective-permute-done | bytes 65568 | tf_op jit(solution)/shard_map/ppermute | solution.py:444
  48.3 0.6 residual_terms.2
  48.9 13.7 %all_to_all.37.received_ref = f32[32,16,128]{2,1,0:T(8,128)S(1)} all-to-all(f32[32,16,128]{2,1,0:T(8,128)S(1)} %get-tuple-element.38), channel_id=1, replica_groups=mesh['sub'=32,'load'=8] {'sub'}, dimensions={0} | all-to-all | bytes 524288 | tf_op jit(solution)/shard_map/all_to_all | solution.py:401
  62.9 16.1 %all_to_all.38.received_ref = f32[8,16,128]{2,1,0:T(8,128)S(1)} all-to-all(f32[8,16,128]{2,1,0:T(8,128)S(1)} %get-tuple-element.40), channel_id=1, replica_groups=mesh['sub'=32,'load'=8] {'load'}, dimensions={0} | all-to-all | bytes 131072 | tf_op jit(solution)/shard_map/all_to_all | solution.py:401
  79.0 1.6 %advance.3 = (f32[1024,128]{1,0:T(8,128)S(1)}, bf16[1024,128]{1,0:T(8,128)(2,1)S(1)}, bf16[256,128]{1,0:T(8,128)(2,1)S(1)}, bf16[256,128]{1,0:T(8,128)(2,1)S(1)}) custom-call(f32[8,16,128]{2,1,0:T(8,128)S(1)} %all_to_all.38.received_ref, f32[1,128]{1,0:T(1,128)S(1)} %bitcast.2, bf16[1024,128]{1,0:T(8,128)(2,1)S(1)} %copy-done.4, ...), custom_call_target="tpu_custom_call" | custom-call | bytes 16777216 | tf_op jit(solution)/shard_map/advance/pallas_call | solution.py:33
  80.6 1.0 collective-permute-start.2
  81.6 0.7 inner_classes.1
  83.0 2.4 %collective-permute-done.3.after_ref = bf16[256,128]{1,0:T(8,128)(2,1)S(1)} collective-permute-done((bf16[256,128]{1,0:T(8,128)(2,1)S(1)}, bf16[256,128]{1,0:T(8,128)(2,1)S(1)}, u32[]{:S(2)}, u32[]{:S(2)}) %collective-permute-start.3) | collective-permute-done | bytes 65568 | tf_op jit(solution)/shard_map/ppermute | solution.py:444
  85.3 0.6 residual_terms.3
  85.9 13.9 %all_to_all.39.received_ref = f32[32,16,128]{2,1,0:T(8,128)S(1)} all-to-all(f32[32,16,128]{2,1,0:T(8,128)S(1)} %get-tuple-element.48), channel_id=1, replica_groups=mesh['sub'=32,'load'=8] {'sub'}, dimensions={0} | all-to-all | bytes 524288 | tf_op jit(solution)/shard_map/all_to_all | solution.py:401
  100.1 15.9 %all_to_all.40.received_ref = f32[8,16,128]{2,1,0:T(8,128)S(1)} all-to-all(f32[8,16,128]{2,1,0:T(8,128)S(1)} %later_partial.1), channel_id=1, replica_groups=mesh['sub'=32,'load'=8] {'load'}, dimensions={0} | all-to-all | bytes 131072 | tf_op jit(solution)/shard_map/all_to_all | solution.py:401
  116.0 2.2 %gradients.1 = (f32[1,1024,128]{2,1,0:T(8,128)}, f32[32,16,128]{2,1,0:T(8,128)S(1)}) custom-call(f32[8,16,128]{2,1,0:T(8,128)S(1)} %all_to_all.40.received_ref, f32[1,128]{1,0:T(1,128)S(1)} %bitcast.3, bf16[1024,128]{1,0:T(8,128)(2,1)S(1)} %copy-done.4, f32[1024,128]{1,0:T(8,128)S(1)} %get-tuple-element.49.residual_ref, ...), custom_call_target="tpu_custom_call" | custom-call | bytes 16777216 | tf_op jit(solution)/shard_map/gradients/pallas_call | solution.py:33
  118.2 13.8 %all_to_all.41 = f32[32,16,128]{2,1,0:T(8,128)S(1)} all-to-all(f32[32,16,128]{2,1,0:T(8,128)S(1)} %get-tuple-element.52), channel_id=1, replica_groups=mesh['sub'=32,'load'=8] {'sub'}, dimensions={0} | all-to-all | bytes 524288 | tf_op jit(solution)/shard_map/all_to_all | solution.py:401
  132.1 5.6 %collective-permute-start.5 = (f32[16,128]{1,0:T(8,128)S(1)}, f32[16,128]{1,0:T(8,128)S(1)}, u32[]{:S(2)}, u32[]{:S(2)}) collective-permute-start(f32[16,128]{1,0:T(8,128)S(1)} %reduce_sum.9.middle_ref), channel_id=1, source_target_pairs={{1,0},{2,1},{3,2},{4,3},{5,4},{6,5},{7,6},{9,8},{10,9},{11,10},{12... | collective-permute-start | bytes 24584 | tf_op jit(solution)/shard_map/ppermute | solution.py:375
  137.7 2.1 %collective-permute-start.4 = (f32[16,128]{1,0:T(8,128)S(1)}, f32[16,128]{1,0:T(8,128)S(1)}, u32[]{:S(2)}, u32[]{:S(2)}) collective-permute-start(f32[16,128]{1,0:T(8,128)S(1)} %reduce_sum.9.middle_ref), channel_id=1, source_target_pairs={{0,1},{1,2},{2,3},{3,4},{4,5},{5,6},{6,7},{8,9},{9,10},{10,11},{11... | collective-permute-start | bytes 24584 | tf_op jit(solution)/shard_map/ppermute | solution.py:375
  139.8 1.0 collective-permute-done.4.left_ref
  140.7 0.8 smooth.1
  (32 shorter events, 1.2 us)
Async XLA Ops:
  0.6 38.5 %copy-start.1 = (f32[1,1024,128]{2,1,0:T(8,128)S(1)}, f32[1,1024,128]{2,1,0:T(8,128)}, u32[]{:S(2)}) copy-start(f32[1,1024,128]{2,1,0:T(8,128)} %rhs_ref.3) | copy-start | bytes 1572868
  0.6 38.5 %copy-start.9 = (f32[128]{0:T(128)S(1)}, f32[128]{0:T(128)}, u32[]{:S(2)}) copy-start(f32[128]{0:T(128)} %param.16) | copy-start | bytes 1540
  4.3 34.8 %copy-start.2 = (bf16[512,1024]{1,0:T(8,128)(2,1)S(1)}, bf16[512,1024]{1,0:T(8,128)(2,1)}, u32[]{:S(2)}) copy-start(bf16[512,1024]{1,0:T(8,128)(2,1)} %get-tuple-element.32.send_ref) | copy-start | bytes 3145732
  4.4 34.8 %copy-start.4 = (bf16[1024,128]{1,0:T(8,128)(2,1)S(1)}, bf16[1024,128]{1,0:T(8,128)(2,1)}, u32[]{:S(2)}) copy-start(bf16[1024,128]{1,0:T(8,128)(2,1)} %get-tuple-element.30.lifted_ref) | copy-start | bytes 786436
  17.6 27.1 %copy-start.10 = (s32[1,1024]{1,0:T(1,128)S(1)}, s32[1,1024]{1,0:T(1,128)}, u32[]{:S(2)}) copy-start(s32[1,1024]{1,0:T(1,128)} %partner_ref.1) | copy-start | bytes 12292
  40.8 5.5 %collective-permute-start = (bf16[256,128]{1,0:T(8,128)(2,1)S(1)}, bf16[256,128]{1,0:T(8,128)(2,1)S(1)}, u32[]{:S(2)}, u32[]{:S(2)}) collective-permute-start(bf16[256,128]{1,0:T(8,128)(2,1)S(1)} %get-tuple-element.36), channel_id=1, source_target_pairs={{0,1},{1,2},{2,3},{3,4},{4,5},{5,6},{6,7},{7,8},{8,9},{9,10},{10,1... | collective-permute-start | bytes 196616 | tf_op jit(solution)/shard_map/ppermute | solution.py:443
  44.6 3.7 %collective-permute-start.1 = (bf16[256,128]{1,0:T(8,128)(2,1)S(1)}, bf16[256,128]{1,0:T(8,128)(2,1)S(1)}, u32[]{:S(2)}, u32[]{:S(2)}) collective-permute-start(bf16[256,128]{1,0:T(8,128)(2,1)S(1)} %get-tuple-element.37), channel_id=1, source_target_pairs={{1,0},{2,1},{3,2},{4,3},{5,4},{6,5},{7,6},{8,7},{9,8},{10,9},{11,1... | collective-permute-start | bytes 196616 | tf_op jit(solution)/shard_map/ppermute | solution.py:444
  44.6 3.7 %copy-start.7 = (bf16[1,12,1024]{2,1,0:T(8,128)(2,1)S(1)}, bf16[1,12,1024]{2,1,0:T(8,128)(2,1)}, u32[]{:S(2)}) copy-start(bf16[1,12,1024]{2,1,0:T(8,128)(2,1)} %basis_ref.3) | copy-start | bytes 73732
  44.6 3.7 %copy-start.8 = (s32[8,128]{1,0:T(8,128)S(1)}, s32[8,128]{1,0:T(8,128)}, u32[]{:S(2)}) copy-start(s32[8,128]{1,0:T(8,128)} %class_ref.5) | copy-start | bytes 12292
  46.2 32.7 %copy-start = (bf16[1,1024,1024]{2,1,0:T(8,128)(2,1)S(1)}, bf16[1,1024,1024]{2,1,0:T(8,128)(2,1)}, u32[]{:S(2)}) copy-start(bf16[1,1024,1024]{2,1,0:T(8,128)(2,1)} %operator_ref.1) | copy-start | bytes 6291460
  80.6 2.4 %collective-permute-start.2 = (bf16[256,128]{1,0:T(8,128)(2,1)S(1)}, bf16[256,128]{1,0:T(8,128)(2,1)S(1)}, u32[]{:S(2)}, u32[]{:S(2)}) collective-permute-start(bf16[256,128]{1,0:T(8,128)(2,1)S(1)} %get-tuple-element.46), channel_id=1, source_target_pairs={{0,1},{1,2},{2,3},{3,4},{4,5},{5,6},{6,7},{7,8},{8,9},{9,10},{10,1... | collective-permute-start | bytes 196616 | tf_op jit(solution)/shard_map/ppermute | solution.py:443
  81.6 3.7 %collective-permute-start.3 = (bf16[256,128]{1,0:T(8,128)(2,1)S(1)}, bf16[256,128]{1,0:T(8,128)(2,1)S(1)}, u32[]{:S(2)}, u32[]{:S(2)}) collective-permute-start(bf16[256,128]{1,0:T(8,128)(2,1)S(1)} %get-tuple-element.47), channel_id=1, source_target_pairs={{1,0},{2,1},{3,2},{4,3},{5,4},{6,5},{7,6},{8,7},{9,8},{10,9},{11,1... | collective-permute-start | bytes 196616 | tf_op jit(solution)/shard_map/ppermute | solution.py:444
  82.3 33.6 %copy-start.3 = (bf16[1,1536,1024]{2,1,0:T(8,128)(2,1)S(1)}, bf16[1,1536,1024]{2,1,0:T(8,128)(2,1)}, u32[]{:S(2)}) copy-start(bf16[1,1536,1024]{2,1,0:T(8,128)(2,1)} %recovery_ref.1) | copy-start | bytes 9437188
  82.3 33.6 %copy-start.5 = (bf16[1,1536,128]{2,1,0:T(8,128)(2,1)S(1)}, bf16[1,1536,128]{2,1,0:T(8,128)(2,1)}, u32[]{:S(2)}) copy-start(bf16[1,1536,128]{2,1,0:T(8,128)(2,1)} %base_ref.1) | copy-start | bytes 1179652
  82.4 33.6 %copy-start.6 = (bf16[1,1536,128]{2,1,0:T(8,128)(2,1)S(1)}, bf16[1,1536,128]{2,1,0:T(8,128)(2,1)}, u32[]{:S(2)}) copy-start(bf16[1,1536,128]{2,1,0:T(8,128)(2,1)} %adjoint_ref.1) | copy-start | bytes 1179652
  82.4 33.6 %copy-start.11 = (s32[1,128]{1,0:T(1,128)S(1)}, s32[1,128]{1,0:T(1,128)}, u32[]{:S(2)}) copy-start(s32[1,128]{1,0:T(1,128)} %voxel_ref.1) | copy-start | bytes 1540
  132.1 7.7 %collective-permute-start.5 = (f32[16,128]{1,0:T(8,128)S(1)}, f32[16,128]{1,0:T(8,128)S(1)}, u32[]{:S(2)}, u32[]{:S(2)}) collective-permute-start(f32[16,128]{1,0:T(8,128)S(1)} %reduce_sum.9.middle_ref), channel_id=1, source_target_pairs={{1,0},{2,1},{3,2},{4,3},{5,4},{6,5},{7,6},{9,8},{10,9},{11,10},{12... | collective-permute-start | bytes 24584 | tf_op jit(solution)/shard_map/ppermute | solution.py:375
  137.7 3.1 %collective-permute-start.4 = (f32[16,128]{1,0:T(8,128)S(1)}, f32[16,128]{1,0:T(8,128)S(1)}, u32[]{:S(2)}, u32[]{:S(2)}) collective-permute-start(f32[16,128]{1,0:T(8,128)S(1)} %reduce_sum.9.middle_ref), channel_id=1, source_target_pairs={{0,1},{1,2},{2,3},{3,4},{4,5},{5,6},{6,7},{8,9},{9,10},{10,11},{11... | collective-permute-start | bytes 24584 | tf_op jit(solution)/shard_map/ppermute | solution.py:375

commit v9 on v8

--- a/solution.py
+++ b/solution.py
@@ -165,9 +165,13 @@
     out_ref[...] = partial.reshape(out_ref.shape)
 
 
-def first_partial(received_ref, operator_hbm, out_ref, block_ref, operator_ref, operator_sem):
-    copy = pltpu.make_async_copy(operator_hbm, operator_ref, operator_sem)
-    copy.start()
+def first_partial(received_ref, operator_hbm, out_ref, block_ref, operator_ref, *operator_sems):
+    copies = []
+    for part, semaphore in enumerate(operator_sems):
+        rows = pl.ds(256 * part, 256)
+        copies.append(pltpu.make_async_copy(operator_hbm.at[:, rows, :], operator_ref.at[:, rows, :], semaphore))
+    for copy in copies:
+        copy.start()
     terms = received_ref[:, :16, :].reshape(LOAD * 16, COLS)
     lanes = lax.broadcasted_iota(jnp.int32, (LOAD, 4, COLS), 2)
     places = lax.broadcasted_iota(jnp.int32, (LOAD, 4, COLS), 1)
@@ -182,7 +186,8 @@
     block_ref[:, SUB * 16 :] = low
     high, low = split2(jnp.concatenate([tile.T for tile in tiles], axis=0))
     partial_rows(high, low, terms, out_ref)
-    copy.wait()
+    for copy in copies:
+        copy.wait()
 
 
 def later_partial(received_ref, block_ref, out_ref):
@@ -425,7 +430,7 @@
         [to_sub, ((COLS, 2 * SUB * 16), BF16), (dual_ops.shape, BF16)],
         (received, dual_ops),
         "first_partial",
-        scratch=[pltpu.SemaphoreType.DMA],
+        scratch=[pltpu.SemaphoreType.DMA] * 4,
         far=(1,),
         limit=PART,
     )

time: 142 us -> 142 us (level)
  no operation moved by 1% of the time
where the time goes in v9:
time: 142 us; the launch traced here: 141 us
  blocking collectives  106 us (75%)
  Pallas kernels  15.5 us (11%)
  starting transfers between devices  12.5 us (9%)
  waiting for transfers between devices  5.97 us (4%)
    all_to_all x7, blocking collectives, over(): return lax.all_to_all(value, axis, 0, 0, tiled=True)  106 us
    pallas_call x12, Pallas kernels, call(): pl.pallas_call(kernel, in_specs=[hbm if place in far else vmem for place...  15.5 us
    ppermute x2, starting transfers between devices, both_ways(): return (lax.ppermute(value, axes, up), lax.ppermute(value, axes, down))  7.65 us
    ppermute x2, starting transfers between devices, on_device(): from_before = lax.ppermute(upper, whole, up)  4.89 us
    ppermute x2, waiting for transfers between devices, on_device(): from_after = lax.ppermute(lower, whole, down)  4.44 us
  transfers between devices with their start and end apart: 6, of which 4 were waited for; matrix products, arithmetic and copies ran while one was open for 0% of the time, Pallas kernels for 2%

profile of v9, /device:TPU:1, one launch (start us, length us, event | category | flops | bytes accessed | tf_op | source)
XLA Modules:
  0.0 141.5 jit_solution(7063920554413155334)
XLA Ops:
  0.7 3.7 %first_terms.1 = (f32[8,64,128]{2,1,0:T(8,128)}, bf16[512,1024]{1,0:T(8,128)(2,1)}, bf16[1024,128]{1,0:T(8,128)(2,1)}) custom-call(f32[1,1024,128]{2,1,0:T(8,128)} %rhs_ref.3, bf16[1,12,1024]{2,1,0:T(8,128)(2,1)} %basis_ref.3, f32[12,3072]{1,0:T(8,128)} %inverse_hbm.1, s32[1,1024]{1,0:T(1,128)} %partner_ref.1), custom_call_target="tpu_custom_call" | custom-call | bytes 16777216 | tf_op jit(solution)/shard_map/first_terms/pallas_call | solution.py:33
  4.4 13.2 %all_to_all.35.received_ref = f32[8,64,128]{2,1,0:T(8,128)S(1)} all-to-all(f32[8,64,128]{2,1,0:T(8,128)} %get-tuple-element.28), channel_id=1, replica_groups=mesh['sub'=32,'load'=8] {'load'}, dimensions={0} | all-to-all | bytes 524288 | tf_op jit(solution)/shard_map/all_to_all | solution.py:406
  17.6 1.6 %first_partial.1 = (f32[32,16,128]{2,1,0:T(8,128)S(1)}, bf16[128,1024]{1,0:T(8,128)(2,1)S(1)}, bf16[1,1024,1024]{2,1,0:T(8,128)(2,1)S(1)}) custom-call(f32[8,64,128]{2,1,0:T(8,128)S(1)} %all_to_all.35.received_ref, bf16[1,1024,1024]{2,1,0:T(8,128)(2,1)} %operator_ref.1), custom_call_target="tpu_custom_call" | custom-call | bytes 16777216 | tf_op jit(solution)/shard_map/first_partial/pallas_call | solution.py:33
  19.1 19.9 %all_to_all.36.received_ref = f32[32,16,128]{2,1,0:T(8,128)S(1)} all-to-all(f32[32,16,128]{2,1,0:T(8,128)S(1)} %get-tuple-element.29), channel_id=1, replica_groups=mesh['sub'=32,'load'=8] {'sub'}, dimensions={0} | all-to-all | bytes 524288 | tf_op jit(solution)/shard_map/all_to_all | solution.py:406
  39.1 1.6 %advance.2 = (f32[1024,128]{1,0:T(8,128)S(1)}, bf16[1024,128]{1,0:T(8,128)(2,1)S(1)}, bf16[256,128]{1,0:T(8,128)(2,1)S(1)}, bf16[256,128]{1,0:T(8,128)(2,1)S(1)}) custom-call(f32[32,16,128]{2,1,0:T(8,128)S(1)} %all_to_all.36.received_ref, f32[1,128]{1,0:T(1,128)S(1)} %bitcast.1, bf16[1024,128]{1,0:T(8,128)(2,1)S(1)} %copy-done.4, ...), custom_call_target="tpu_custom_call" | custom-call | bytes 16777216 | tf_op jit(solution)/shard_map/advance/pallas_call | solution.py:33
  40.7 3.9 %collective-permute-start = (bf16[256,128]{1,0:T(8,128)(2,1)S(1)}, bf16[256,128]{1,0:T(8,128)(2,1)S(1)}, u32[]{:S(2)}, u32[]{:S(2)}) collective-permute-start(bf16[256,128]{1,0:T(8,128)(2,1)S(1)} %get-tuple-element.36), channel_id=1, source_target_pairs={{0,1},{1,2},{2,3},{3,4},{4,5},{5,6},{6,7},{7,8},{8,9},{9,10},{10,1... | collective-permute-start | bytes 196616 | tf_op jit(solution)/shard_map/ppermute | solution.py:448
  44.6 1.6 %first_inner.1 = (f32[1024,128]{1,0:T(8,128)S(1)}, bf16[1024,1536]{1,0:T(8,128)(2,1)S(1)}) custom-call(bf16[1024,128]{1,0:T(8,128)(2,1)S(1)} %get-tuple-element.33.images_ref, s32[1,1024]{1,0:T(1,128)S(1)} %copy-done.10), custom_call_target="tpu_custom_call" | custom-call | flops 2147483648 | bytes 8388608 | tf_op jit(solution)/shard_map/first_inner/pallas_call | solution.py:33
  46.2 2.1 %collective-permute-done.1.after_ref = bf16[256,128]{1,0:T(8,128)(2,1)S(1)} collective-permute-done((bf16[256,128]{1,0:T(8,128)(2,1)S(1)}, bf16[256,128]{1,0:T(8,128)(2,1)S(1)}, u32[]{:S(2)}, u32[]{:S(2)}) %collective-permute-start.1) | collective-permute-done | bytes 65568 | tf_op jit(solution)/shard_map/ppermute | solution.py:449
  48.3 0.6 residual_terms.2
  48.9 13.7 %all_to_all.37.received_ref = f32[32,16,128]{2,1,0:T(8,128)S(1)} all-to-all(f32[32,16,128]{2,1,0:T(8,128)S(1)} %get-tuple-element.38), channel_id=1, replica_groups=mesh['sub'=32,'load'=8] {'sub'}, dimensions={0} | all-to-all | bytes 524288 | tf_op jit(solution)/shard_map/all_to_all | solution.py:406
  62.8 16.1 %all_to_all.38.received_ref = f32[8,16,128]{2,1,0:T(8,128)S(1)} all-to-all(f32[8,16,128]{2,1,0:T(8,128)S(1)} %get-tuple-element.40), channel_id=1, replica_groups=mesh['sub'=32,'load'=8] {'load'}, dimensions={0} | all-to-all | bytes 131072 | tf_op jit(solution)/shard_map/all_to_all | solution.py:406
  78.9 1.6 %advance.3 = (f32[1024,128]{1,0:T(8,128)S(1)}, bf16[1024,128]{1,0:T(8,128)(2,1)S(1)}, bf16[256,128]{1,0:T(8,128)(2,1)S(1)}, bf16[256,128]{1,0:T(8,128)(2,1)S(1)}) custom-call(f32[8,16,128]{2,1,0:T(8,128)S(1)} %all_to_all.38.received_ref, f32[1,128]{1,0:T(1,128)S(1)} %bitcast.2, bf16[1024,128]{1,0:T(8,128)(2,1)S(1)} %copy-done.4, ...), custom_call_target="tpu_custom_call" | custom-call | bytes 16777216 | tf_op jit(solution)/shard_map/advance/pallas_call | solution.py:33
  80.5 1.0 collective-permute-start.2
  81.6 0.7 inner_classes.1
  82.9 2.4 %collective-permute-done.3.after_ref = bf16[256,128]{1,0:T(8,128)(2,1)S(1)} collective-permute-done((bf16[256,128]{1,0:T(8,128)(2,1)S(1)}, bf16[256,128]{1,0:T(8,128)(2,1)S(1)}, u32[]{:S(2)}, u32[]{:S(2)}) %collective-permute-start.3) | collective-permute-done | bytes 65568 | tf_op jit(solution)/shard_map/ppermute | solution.py:449
  85.3 0.6 residual_terms.3
  85.9 13.9 %all_to_all.39.received_ref = f32[32,16,128]{2,1,0:T(8,128)S(1)} all-to-all(f32[32,16,128]{2,1,0:T(8,128)S(1)} %get-tuple-element.48), channel_id=1, replica_groups=mesh['sub'=32,'load'=8] {'sub'}, dimensions={0} | all-to-all | bytes 524288 | tf_op jit(solution)/shard_map/all_to_all | solution.py:406
  100.0 15.9 %all_to_all.40.received_ref = f32[8,16,128]{2,1,0:T(8,128)S(1)} all-to-all(f32[8,16,128]{2,1,0:T(8,128)S(1)} %later_partial.1), channel_id=1, replica_groups=mesh['sub'=32,'load'=8] {'load'}, dimensions={0} | all-to-all | bytes 131072 | tf_op jit(solution)/shard_map/all_to_all | solution.py:406
  115.9 2.2 %gradients.1 = (f32[1,1024,128]{2,1,0:T(8,128)}, f32[32,16,128]{2,1,0:T(8,128)S(1)}) custom-call(f32[8,16,128]{2,1,0:T(8,128)S(1)} %all_to_all.40.received_ref, f32[1,128]{1,0:T(1,128)S(1)} %bitcast.3, bf16[1024,128]{1,0:T(8,128)(2,1)S(1)} %copy-done.4, f32[1024,128]{1,0:T(8,128)S(1)} %get-tuple-element.49.residual_ref, ...), custom_call_target="tpu_custom_call" | custom-call | bytes 16777216 | tf_op jit(solution)/shard_map/gradients/pallas_call | solution.py:33
  118.1 13.8 %all_to_all.41 = f32[32,16,128]{2,1,0:T(8,128)S(1)} all-to-all(f32[32,16,128]{2,1,0:T(8,128)S(1)} %get-tuple-element.52), channel_id=1, replica_groups=mesh['sub'=32,'load'=8] {'sub'}, dimensions={0} | all-to-all | bytes 524288 | tf_op jit(solution)/shard_map/all_to_all | solution.py:406
  132.0 5.6 %collective-permute-start.5 = (f32[16,128]{1,0:T(8,128)S(1)}, f32[16,128]{1,0:T(8,128)S(1)}, u32[]{:S(2)}, u32[]{:S(2)}) collective-permute-start(f32[16,128]{1,0:T(8,128)S(1)} %reduce_sum.9.middle_ref), channel_id=1, source_target_pairs={{1,0},{2,1},{3,2},{4,3},{5,4},{6,5},{7,6},{9,8},{10,9},{11,10},{12... | collective-permute-start | bytes 24584 | tf_op jit(solution)/shard_map/ppermute | solution.py:380
  137.6 2.1 %collective-permute-start.4 = (f32[16,128]{1,0:T(8,128)S(1)}, f32[16,128]{1,0:T(8,128)S(1)}, u32[]{:S(2)}, u32[]{:S(2)}) collective-permute-start(f32[16,128]{1,0:T(8,128)S(1)} %reduce_sum.9.middle_ref), channel_id=1, source_target_pairs={{0,1},{1,2},{2,3},{3,4},{4,5},{5,6},{6,7},{8,9},{9,10},{10,11},{11... | collective-permute-start | bytes 24584 | tf_op jit(solution)/shard_map/ppermute | solution.py:380
  139.7 1.0 collective-permute-done.4.left_ref
  140.7 0.8 smooth.1
  (32 shorter events, 1.2 us)
Async XLA Ops:
  0.6 38.4 %copy-start.1 = (f32[1,1024,128]{2,1,0:T(8,128)S(1)}, f32[1,1024,128]{2,1,0:T(8,128)}, u32[]{:S(2)}) copy-start(f32[1,1024,128]{2,1,0:T(8,128)} %rhs_ref.3) | copy-start | bytes 1572868
  0.6 38.4 %copy-start.9 = (f32[128]{0:T(128)S(1)}, f32[128]{0:T(128)}, u32[]{:S(2)}) copy-start(f32[128]{0:T(128)} %param.16) | copy-start | bytes 1540
  4.3 34.7 %copy-start.2 = (bf16[512,1024]{1,0:T(8,128)(2,1)S(1)}, bf16[512,1024]{1,0:T(8,128)(2,1)}, u32[]{:S(2)}) copy-start(bf16[512,1024]{1,0:T(8,128)(2,1)} %get-tuple-element.32.send_ref) | copy-start | bytes 3145732
  4.4 34.7 %copy-start.4 = (bf16[1024,128]{1,0:T(8,128)(2,1)S(1)}, bf16[1024,128]{1,0:T(8,128)(2,1)}, u32[]{:S(2)}) copy-start(bf16[1024,128]{1,0:T(8,128)(2,1)} %get-tuple-element.30.lifted_ref) | copy-start | bytes 786436
  17.6 27.0 %copy-start.10 = (s32[1,1024]{1,0:T(1,128)S(1)}, s32[1,1024]{1,0:T(1,128)}, u32[]{:S(2)}) copy-start(s32[1,1024]{1,0:T(1,128)} %partner_ref.1) | copy-start | bytes 12292
  40.7 5.5 %collective-permute-start = (bf16[256,128]{1,0:T(8,128)(2,1)S(1)}, bf16[256,128]{1,0:T(8,128)(2,1)S(1)}, u32[]{:S(2)}, u32[]{:S(2)}) collective-permute-start(bf16[256,128]{1,0:T(8,128)(2,1)S(1)} %get-tuple-element.36), channel_id=1, source_target_pairs={{0,1},{1,2},{2,3},{3,4},{4,5},{5,6},{6,7},{7,8},{8,9},{9,10},{10,1... | collective-permute-start | bytes 196616 | tf_op jit(solution)/shard_map/ppermute | solution.py:448
  44.6 3.7 %collective-permute-start.1 = (bf16[256,128]{1,0:T(8,128)(2,1)S(1)}, bf16[256,128]{1,0:T(8,128)(2,1)S(1)}, u32[]{:S(2)}, u32[]{:S(2)}) collective-permute-start(bf16[256,128]{1,0:T(8,128)(2,1)S(1)} %get-tuple-element.37), channel_id=1, source_target_pairs={{1,0},{2,1},{3,2},{4,3},{5,4},{6,5},{7,6},{8,7},{9,8},{10,9},{11,1... | collective-permute-start | bytes 196616 | tf_op jit(solution)/shard_map/ppermute | solution.py:449
  44.6 3.7 %copy-start.7 = (bf16[1,12,1024]{2,1,0:T(8,128)(2,1)S(1)}, bf16[1,12,1024]{2,1,0:T(8,128)(2,1)}, u32[]{:S(2)}) copy-start(bf16[1,12,1024]{2,1,0:T(8,128)(2,1)} %basis_ref.3) | copy-start | bytes 73732
  44.6 3.7 %copy-start.8 = (s32[8,128]{1,0:T(8,128)S(1)}, s32[8,128]{1,0:T(8,128)}, u32[]{:S(2)}) copy-start(s32[8,128]{1,0:T(8,128)} %class_ref.5) | copy-start | bytes 12292
  46.2 32.7 %copy-start = (bf16[1,1024,1024]{2,1,0:T(8,128)(2,1)S(1)}, bf16[1,1024,1024]{2,1,0:T(8,128)(2,1)}, u32[]{:S(2)}) copy-start(bf16[1,1024,1024]{2,1,0:T(8,128)(2,1)} %operator_ref.1) | copy-start | bytes 6291460
  80.5 2.4 %collective-permute-start.2 = (bf16[256,128]{1,0:T(8,128)(2,1)S(1)}, bf16[256,128]{1,0:T(8,128)(2,1)S(1)}, u32[]{:S(2)}, u32[]{:S(2)}) collective-permute-start(bf16[256,128]{1,0:T(8,128)(2,1)S(1)} %get-tuple-element.46), channel_id=1, source_target_pairs={{0,1},{1,2},{2,3},{3,4},{4,5},{5,6},{6,7},{7,8},{8,9},{9,10},{10,1... | collective-permute-start | bytes 196616 | tf_op jit(solution)/shard_map/ppermute | solution.py:448
  81.6 3.7 %collective-permute-start.3 = (bf16[256,128]{1,0:T(8,128)(2,1)S(1)}, bf16[256,128]{1,0:T(8,128)(2,1)S(1)}, u32[]{:S(2)}, u32[]{:S(2)}) collective-permute-start(bf16[256,128]{1,0:T(8,128)(2,1)S(1)} %get-tuple-element.47), channel_id=1, source_target_pairs={{1,0},{2,1},{3,2},{4,3},{5,4},{6,5},{7,6},{8,7},{9,8},{10,9},{11,1... | collective-permute-start | bytes 196616 | tf_op jit(solution)/shard_map/ppermute | solution.py:449
  82.3 33.6 %copy-start.3 = (bf16[1,1536,1024]{2,1,0:T(8,128)(2,1)S(1)}, bf16[1,1536,1024]{2,1,0:T(8,128)(2,1)}, u32[]{:S(2)}) copy-start(bf16[1,1536,1024]{2,1,0:T(8,128)(2,1)} %recovery_ref.1) | copy-start | bytes 9437188
  82.3 33.6 %copy-start.5 = (bf16[1,1536,128]{2,1,0:T(8,128)(2,1)S(1)}, bf16[1,1536,128]{2,1,0:T(8,128)(2,1)}, u32[]{:S(2)}) copy-start(bf16[1,1536,128]{2,1,0:T(8,128)(2,1)} %base_ref.1) | copy-start | bytes 1179652
  82.3 33.6 %copy-start.6 = (bf16[1,1536,128]{2,1,0:T(8,128)(2,1)S(1)}, bf16[1,1536,128]{2,1,0:T(8,128)(2,1)}, u32[]{:S(2)}) copy-start(bf16[1,1536,128]{2,1,0:T(8,128)(2,1)} %adjoint_ref.1) | copy-start | bytes 1179652
  82.3 33.6 %copy-start.11 = (s32[1,128]{1,0:T(1,128)S(1)}, s32[1,128]{1,0:T(1,128)}, u32[]{:S(2)}) copy-start(s32[1,128]{1,0:T(1,128)} %voxel_ref.1) | copy-start | bytes 1540
  132.0 7.7 %collective-permute-start.5 = (f32[16,128]{1,0:T(8,128)S(1)}, f32[16,128]{1,0:T(8,128)S(1)}, u32[]{:S(2)}, u32[]{:S(2)}) collective-permute-start(f32[16,128]{1,0:T(8,128)S(1)} %reduce_sum.9.middle_ref), channel_id=1, source_target_pairs={{1,0},{2,1},{3,2},{4,3},{5,4},{6,5},{7,6},{9,8},{10,9},{11,10},{12... | collective-permute-start | bytes 24584 | tf_op jit(solution)/shard_map/ppermute | solution.py:380
  137.6 3.1 %collective-permute-start.4 = (f32[16,128]{1,0:T(8,128)S(1)}, f32[16,128]{1,0:T(8,128)S(1)}, u32[]{:S(2)}, u32[]{:S(2)}) collective-permute-start(f32[16,128]{1,0:T(8,128)S(1)} %reduce_sum.9.middle_ref), channel_id=1, source_target_pairs={{0,1},{1,2},{2,3},{3,4},{4,5},{5,6},{6,7},{8,9},{9,10},{10,11},{11... | collective-permute-start | bytes 24584 | tf_op jit(solution)/shard_map/ppermute | solution.py:380
